TPU v7x, 32 devices: a whole 2x2x4 slice. The times are simulated.
32 devices in a mesh: dp: 16 (over z, y, core), chan: 2 (over x).
Axes of the slice: x: 2, y: 2, z: 4, core: 2. Of those that a mesh axis runs over, the one named last changes fastest.
Arguments:
- features: bfloat16 [64, 384, 1024], P('dp', 'chan'), may hold values from -6 to 6
- pixel_masks: int32 [64, 1024], P('dp'), may hold values 0 or 1
- timesteps: int32 [64], P('dp'), may hold values from 0 to 999
- first_filter: float32 [9, 384, 384], P(None, 'dp', 'chan'), may hold values from -0.109375 to 0.109375
- second_filter: float32 [9, 384, 384], P(None, 'dp', 'chan'), may hold values from -0.109375 to 0.109375
- project_weight: float32 [384, 3, 384], P('dp', None, 'chan'), may hold values from -0.3125 to 0.3125
- output_weight: float32 [384, 384], P('chan', 'dp'), may hold values from -6 to 6
- embed_weight: float32 [2, 768, 384], P(None, 'dp', 'chan'), may hold values from -0.21875 to 0.21875
- norm_gains: float32 [3, 384], P(None, 'chan'), may hold values from 0.1 to 1.9
- norm_biases: float32 [3, 384], P(None, 'chan'), may hold values from -3 to 3
- cotangent: bfloat16 [64, 384, 1024], P('dp', 'chan'), may hold values from -6 to 6
Outputs:
- block_output: bfloat16 [64, 384, 1024], P('dp', 'chan')
- input_grad: float32 [64, 384, 1024], P('dp', 'chan')
- grad_first: float32 [9, 384, 384], P(None, 'dp', 'chan')
- grad_second: float32 [9, 384, 384], P(None, 'dp', 'chan')
- grad_project: float32 [384, 3, 384], P('dp', None, 'chan')
- grad_output: float32 [384, 384], P('chan', 'dp')
- grad_embed: float32 [2, 768, 384], P(None, 'dp', 'chan')
- grad_gains: float32 [3, 384], P(None, 'chan')
- grad_biases: float32 [3, 384], P(None, 'chan')
All inputs are finite; a program needn't handle non-finite values. No bound on the sum of `pixel_masks` on one device may be relied on, other than what follows from the above.
Results may differ from a plain program's by a relative error of at most 0.017.
Values may be sent and summed in bfloat16 or wider, within the bound.
No kernel may reach another device: no remote copies, remote signals or barrier semaphores. Data moves between devices by JAX's collectives and lax.ppermute only.
A program may use at most 128 MiB of HBM per device.

v0:
```python
import functools
import math

import jax
import jax.numpy as jnp
from jax import lax
from jax.experimental import pallas as pl
from jax.experimental.pallas import tpu as pltpu
from jax.sharding import PartitionSpec as P

C = 384
HALF = 192
HEAD = 64
GROUPS = 32
WIDTH = C // GROUPS
SIDE = 32
PIX = SIDE * SIDE
BLOCKS = 16
ROWS = C // BLOCKS
TAPS = 3 * C
EPSILON = 1e-05
SECOND = 3 * HALF + 256
MIXED = 4 * HALF
PAIR = 2 * ROWS
PIECE = 3 * PAIR
JOINT = PIECE + PAIR + PAIR // 3
PAIRS = BLOCKS // 2
KEYS = 128
CHUNK = 256
LOW = jnp.bfloat16
WIDE = jnp.float32
ORDER = (0, 8, 4, 12, 2, 10, 6, 14, 1, 9, 5, 13, 3, 11, 7, 15)

NN = (((1,), (0,)), ((), ()))
NT = (((1,), (1,)), ((), ()))
TN = (((0,), (0,)), ((), ()))


def dot(left, right, dims):
    return lax.dot_general(left, right, dims, preferred_element_type=WIDE)


def pixel_row(keep):
    pixel = lax.broadcasted_iota(jnp.int32, (1, PIX), 1)
    return jnp.where(keep(pixel), 1.0, 0.0).astype(LOW)


def lane_pair(first, second):
    lane = lax.broadcasted_iota(jnp.int32, (C, 128), 1)
    return jnp.where(lane == 0, first, jnp.where(lane == 1, second, 0.0))


def group_sums(member, values):
    high = values.astype(LOW)
    rest = values - high.astype(WIDE)
    middle = rest.astype(LOW)
    low = (rest - middle.astype(WIDE)).astype(LOW)
    return dot(member, high, NN) + dot(member, middle, NN) + dot(member, low, NN)


def group_sum(member, column):
    return group_sums(member, jnp.broadcast_to(column, (C, 128)))[:, 0:1]


def group_stats(value_ref, member, mask, count):
    mean = group_sum(member, jnp.sum(value_ref[...] * mask, axis=1, keepdims=True)) / count
    centred = value_ref[...] - mean
    variance = (
        group_sum(member, jnp.sum(centred * centred * mask, axis=1, keepdims=True)) / count
    )
    return mean, lax.rsqrt(variance + EPSILON)


def silu(value):
    return value / (1.0 + jnp.exp(-value))


def silu_slope(value):
    squashed = 1.0 / (1.0 + jnp.exp(-value))
    return squashed * (1.0 + value * (1.0 - squashed))


def shift_down(piece):
    pixel = lax.broadcasted_iota(jnp.int32, piece.shape, 1)
    return jnp.where(pixel < SIDE, 0.0, pltpu.roll(piece, SIDE, 1))


def shift_up(piece):
    pixel = lax.broadcasted_iota(jnp.int32, piece.shape, 1)
    return jnp.where(pixel >= PIX - SIDE, 0.0, pltpu.roll(piece, PIX - SIDE, 1))


def conv_out(product_ref, chan):
    base = chan * 3 * HALF
    return (
        product_ref[base + HALF : base + 2 * HALF, :]
        + shift_down(product_ref[base : base + HALF, :])
        + shift_up(product_ref[base + 2 * HALF : base + 3 * HALF, :])
    )


def stack_gradient(grad_ref, out_ref):
    not_top = pixel_row(lambda pixel: pixel >= SIDE)
    not_bottom = pixel_row(lambda pixel: pixel < PIX - SIDE)
    for chan in range(2):
        piece = grad_ref[chan * HALF : (chan + 1) * HALF, :]
        base = chan * 3 * HALF
        out_ref[base : base + HALF, :] = pltpu.roll(piece, PIX - SIDE, 1) * not_bottom
        out_ref[base + HALF : base + 2 * HALF, :] = piece
        out_ref[base + 2 * HALF : base + 3 * HALF, :] = pltpu.roll(piece, SIDE, 1) * not_top


def stack_gradients(grads, out_ref):
    at = 0
    for ref in grads:
        for image in range(ref.shape[0]):
            stack_gradient(ref.at[image], out_ref.at[:, at * PIX : (at + 1) * PIX])
            at += 1


def block_offset(place_ref, position):
    return pl.multiple_of(place_ref[position], 8)


def pair_rows(place, ref, pair):
    return jnp.concatenate(
        [ref[pl.ds(block_offset(place, 2 * pair + part), ROWS), :] for part in range(2)], axis=0
    )


def build_stack(place, value, mask, stacks):
    not_left = pixel_row(lambda pixel: pixel % SIDE != 0)
    not_right = pixel_row(lambda pixel: pixel % SIDE != SIDE - 1)
    for pair in range(PAIRS):
        piece = (silu(pair_rows(place, value, pair)) * mask).astype(LOW)
        stack = stacks[pair // (PAIRS // 2)]
        base = pair % (PAIRS // 2) * PIECE
        stack[base : base + PAIR, :] = pltpu.roll(piece, 1, 1) * not_left
        stack[base + PAIR : base + 2 * PAIR, :] = piece
        stack[base + 2 * PAIR : base + 3 * PAIR, :] = pltpu.roll(piece, PIX - 1, 1) * not_right


def back_to_channels(place_ref, product_ref, out_ref):
    column = lax.broadcasted_iota(jnp.int32, (PAIR, PIX), 1) & (SIDE - 1)
    for pair in range(PAIRS):
        base = pair * PIECE
        first = product_ref[base : base + PAIR, :]
        middle = product_ref[base + PAIR : base + 2 * PAIR, :]
        last = product_ref[base + 2 * PAIR : base + 3 * PAIR, :]
        total = (
            middle
            + jnp.where(column == SIDE - 1, 0.0, pltpu.roll(first, PIX - 1, 1))
            + jnp.where(column == 0, 0.0, pltpu.roll(last, 1, 1))
        )
        for part in range(2):
            out_ref[pl.ds(block_offset(place_ref, 2 * pair + part), ROWS), :] = total[
                part * ROWS : (part + 1) * ROWS
            ]


def count_of(mask):
    return jnp.maximum(jnp.sum(mask, axis=1, keepdims=True), 1.0) * float(WIDTH)


def small_columns(columns):
    lane = lax.broadcasted_iota(jnp.int32, (C, 128), 1)
    result = jnp.zeros((C, 128), WIDE)
    for index, column in enumerate(columns):
        result = jnp.where(lane == index, column, result)
    return result


def small_rows(columns):
    return small_columns(columns).T[:8]


def set_rows(rows, count):
    index = lax.broadcasted_iota(jnp.int32, (count, rows[0].shape[1]), 0)
    result = jnp.zeros((count, rows[0].shape[1]), WIDE)
    for at, row in enumerate(rows):
        result = jnp.where(index == at, row, result)
    return result


def three_parts(value):
    high = value.astype(LOW).astype(WIDE)
    rest = value - high
    middle = rest.astype(LOW).astype(WIDE)
    return [high, middle, rest - middle]


def load_weight(weight, pieces):
    @pl.when(pl.program_id(0) == 0)
    def _():
        for index, source in enumerate(pieces):
            weight[index * PIECE : (index + 1) * PIECE, :] = source[...]


def load_second(weight, weight_e, pieces):
    @pl.when(pl.program_id(0) == 0)
    def _():
        for index, source in enumerate(pieces):
            rows = slice(index * PIECE, (index + 1) * PIECE)
            for chan in range(2):
                base = chan * SECOND
                weight[rows, chan * 3 * HALF : (chan + 1) * 3 * HALF] = source[
                    :, base : base + 3 * HALF
                ]
                for part in range(2):
                    lane = base + 3 * HALF + part * 128
                    weight_e[chan, part, rows, :] = source[:, lane : lane + 128]


def both_rows(stacks):
    return jnp.concatenate([stack[...] for stack in stacks], axis=0)


def half_offsets(place):
    own = pl.multiple_of(place[BLOCKS] * HALF, HALF)
    other = pl.multiple_of((1 - place[BLOCKS]) * HALF, HALF)
    return own, other


def prepare_kernel(
    place,
    mine,
    theirs,
    mask_ref,
    params,
    member,
    whole_out,
    low_out,
    high_out,
    stats_out,
    value,
):
    own, other = half_offsets(place)
    value[pl.ds(own, HALF), :] = mine[0].astype(WIDE)
    value[pl.ds(other, HALF), :] = theirs[0].astype(WIDE)
    mask = mask_ref[0]
    whole_out[0] = value[...].astype(LOW)
    mean, factor = group_stats(value, member[...], mask, count_of(mask))
    stats_out[0] = small_columns((mean, factor))
    scale = factor * params[:, 0:1]
    value[...] = (value[...] - mean) * scale + params[:, 1:2]
    build_stack(place, value, mask, (low_out, high_out))


def first_kernel(
    place,
    mask_ref,
    member,
    pieces,
    stacks,
    normed_out,
    stats_out,
    weight,
    value,
    product,
):
    load_weight(weight, pieces)
    mask = mask_ref[0]
    product[...] = dot(weight[...], both_rows(stacks), TN)
    for chan in range(2):
        value[chan * HALF : (chan + 1) * HALF, :] = conv_out(product, chan)
    mean, factor = group_stats(value, member[...], mask, count_of(mask))
    normed_out[0] = (value[...] - mean) * factor
    stats_out[0] = small_columns((factor,))


def second_kernel(
    place,
    normed,
    whole,
    embed_in,
    mask_ref,
    params,
    member,
    pieces,
    low_out,
    high_out,
    residual_out,
    attend_out,
    stats_out,
    weight,
    weight_e,
    value,
    product,
):
    load_second(weight, weight_e, pieces)
    mask = mask_ref[0]
    count = count_of(mask)
    scales, shifts = [], []
    for chan in range(2):
        low = dot(weight_e[chan, 0], embed_in[0, 0], TN)
        high = dot(weight_e[chan, 1], embed_in[0, 1], TN)
        column = jnp.concatenate(
            [
                low[:, 0:1] + low[:, 1:2] + low[:, 2:3],
                low[:, 3:4] + low[:, 4:5] + low[:, 5:6] + high[:, 0:1] + high[:, 1:2] + high[:, 2:3],
                high[:, 3:4] + high[:, 4:5] + high[:, 5:6],
            ],
            axis=0,
        )
        scales.append(column[:HALF])
        shifts.append(column[HALF:])
    time_scale = jnp.concatenate(scales, axis=0)
    time_shift = jnp.concatenate(shifts, axis=0)
    affine = normed[0] * params[:, 2:3] + params[:, 3:4]
    value[...] = affine * (1.0 + time_scale) + time_shift
    stacks = (low_out, high_out)
    build_stack(place, value, mask, stacks)
    product[...] = dot(weight[...], both_rows(stacks), TN)
    for chan in range(2):
        rows = slice(chan * HALF, (chan + 1) * HALF)
        value[rows, :] = whole[0, rows, :].astype(WIDE) + conv_out(product, chan)
    residual_out[0] = value[...]
    mean, factor = group_stats(value, member[...], mask, count)
    scale = factor * params[:, 4:5]
    attend_out[0] = ((value[...] - mean) * scale + params[:, 5:6]).astype(LOW)
    stats_out[0] = small_columns((mean, factor, time_scale, time_shift))


def attend_kernel(
    place,
    attend_in,
    residual,
    stats,
    mine,
    theirs,
    mask_ref,
    params,
    member,
    bundle,
    block_out,
    send_out,
    residual_grad_out,
    second_grad_out,
    mixed_keep,
    mixed_send,
    small_out,
    weight_f,
    project,
    output,
    gradient,
    projected,
    attend_grad,
    attended,
    projected_grad,
    key_side,
    value_side,
    value_rows,
    query_side,
    grad_side,
    scores,
    probs,
    score_grads,
    accumulated,
    value,
):
    image = pl.program_id(0)

    @pl.when(image == 0)
    def _():
        for chan in range(2):
            for pair in range(PAIRS):
                block = bundle[pair][:, chan * MIXED : (chan + 1) * MIXED].astype(WIDE)
                for part in range(2):
                    weight_f[chan, pl.ds(block_offset(place, 2 * pair + part), ROWS), :] = block[
                        part * ROWS : (part + 1) * ROWS
                    ]
        project[...] = jnp.concatenate(
            [weight_f[0, :, : 3 * HALF], weight_f[1, :, : 3 * HALF]], axis=1
        ).astype(LOW)
        output[...] = jnp.concatenate(
            [weight_f[0, :, 3 * HALF :], weight_f[1, :, 3 * HALF :]], axis=1
        ).astype(LOW)
        accumulated[...] = jnp.zeros_like(accumulated)

    own, other = half_offsets(place)
    mask = mask_ref[0]
    count = count_of(mask)
    gradient[pl.ds(own, HALF), :] = (mine[0].astype(WIDE) * mask).astype(LOW)
    gradient[pl.ds(other, HALF), :] = (theirs[0].astype(WIDE) * mask).astype(LOW)
    projected[...] = dot(project[...], attend_in[0], TN).astype(LOW)
    attend_grad[...] = dot(output[...], gradient[...], TN).astype(LOW)

    penalty = mask - 1.0
    one = jnp.ones((1, PIX), WIDE)
    fill = jnp.zeros((KEYS - HEAD - 16, PIX), LOW)
    key_rows = jnp.concatenate(
        [set_rows([penalty * 9984.0, penalty * 16.0], 16).astype(LOW), fill], axis=0
    )
    one_rows = jnp.concatenate([set_rows([one, one, one], 16).astype(LOW), fill], axis=0)
    query_side[HEAD:, :] = one_rows
    grad_side[HEAD:, :] = jnp.zeros((KEYS - HEAD, PIX), LOW)

    def one_head(head, carry):
        chan = head // 3
        row_q = pl.multiple_of(chan * (3 * HALF) + (head - 3 * chan) * HEAD, HEAD)
        row_k = pl.multiple_of(row_q + HALF, HEAD)
        row_v = pl.multiple_of(row_q + 2 * HALF, HEAD)
        row_o = pl.multiple_of(head * HEAD, HEAD)
        queries = projected[pl.ds(row_q, HEAD), :]
        keys = projected[pl.ds(row_k, HEAD), :]
        values = jnp.concatenate([projected[pl.ds(row_v, HEAD), :], one_rows], axis=0)
        grads = attend_grad[pl.ds(row_o, HEAD), :].astype(WIDE)
        key_side[...] = jnp.concatenate([keys, key_rows], axis=0).T
        value_rows[...] = values[: HEAD + 16]
        value_side[...] = values.T
        query_side[:HEAD, :] = (queries.astype(WIDE) * HEAD**-0.5).astype(LOW)
        peak = None
        for start in range(0, PIX, CHUNK):
            part = dot(key_side[start : start + CHUNK, :], query_side[...], NN)
            scores[start : start + CHUNK, :] = part
            highest = jnp.max(part.reshape(CHUNK // 8, 8, PIX), axis=0)
            peak = highest if peak is None else jnp.maximum(peak, highest)
        peak = jnp.max(peak, axis=0, keepdims=True)
        for start in range(0, PIX, CHUNK):
            span = slice(start, start + CHUNK)
            probs[span, :] = jnp.exp(scores[span, :] - peak).astype(LOW)
        result = dot(value_rows[...], probs[...], NN)
        inverse = 1.0 / result[HEAD : HEAD + 1, :]
        result = result[:HEAD, :] * inverse
        attended[pl.ds(row_o, HEAD), :] = result.astype(LOW)
        scaled = grads * inverse
        delta = jnp.sum(scaled * result, axis=0, keepdims=True)
        grad_side[:HEAD, :] = scaled.astype(LOW)
        grad_side[HEAD : HEAD + 16, :] = set_rows(three_parts(-delta), 16).astype(LOW)
        for start in range(0, PIX, CHUNK):
            span = slice(start, start + CHUNK)
            part = dot(value_side[span, :], grad_side[...], NN)
            score_grads[span, :] = (probs[span, :].astype(WIDE) * part).astype(LOW)
        projected_grad[pl.ds(row_q, HEAD), :] = (
            dot(keys, score_grads[...], NN) * HEAD**-0.5
        ).astype(LOW)
        projected_grad[pl.ds(row_k, HEAD), :] = (
            dot(queries, score_grads[...], NT) * HEAD**-0.5
        ).astype(LOW)
        projected_grad[pl.ds(row_v, HEAD), :] = dot(grad_side[:HEAD, :], probs[...], NT).astype(
            LOW
        )
        return carry

    lax.fori_loop(0, C // HEAD, one_head, 0)

    value[...] = (residual[0] + dot(output[...], attended[...], NN)) * mask
    block_out[0] = value[pl.ds(own, HALF), :].astype(LOW)
    send_out[0] = value[pl.ds(other, HALF), :].astype(LOW)
    accumulated[:, TAPS:] += dot(gradient[...], attended[...], NT)
    accumulated[:, :TAPS] += dot(attend_in[0], projected_grad[...], NT)
    third = dot(project[...], projected_grad[...], NN)
    mean, factor = stats[0, :, 0:1], stats[0, :, 1:2]
    normed = (residual[0] - mean) * factor
    bias_third = jnp.sum(third, axis=1, keepdims=True)
    gain_third = jnp.sum(third * normed, axis=1, keepdims=True)
    gain = params[:, 4:5]
    sums = group_sums(member[...], lane_pair(gain * bias_third, gain * gain_third))
    first_sum, second_sum = sums[:, 0:1] / count, sums[:, 1:2] / count
    total = gradient[...].astype(WIDE) + factor * (
        third * gain - mask * (first_sum + normed * second_sum)
    )
    residual_grad_out[0] = total
    second_grad_out[0] = total.astype(LOW)
    small_out[0] = small_rows((gain_third, bias_third))

    @pl.when(image == pl.num_programs(0) - 1)
    def _():
        for pair in range(PAIRS):
            rows = pair_rows(place, accumulated, pair)
            out = mixed_keep if pair < PAIRS // 2 else mixed_send
            base = pair % (PAIRS // 2) * (JOINT - PIECE)
            third_rows = PAIR // 3
            out[base : base + PAIR, :] = rows[:, :TAPS].astype(out.dtype)
            out[base + PAIR : base + PAIR + third_rows, :] = jnp.concatenate(
                [rows[part * third_rows : (part + 1) * third_rows, TAPS:] for part in range(3)],
                axis=1,
            ).astype(out.dtype)


def filter_kernel(place, grads, stacks, mixed, *refs):
    outs, grad_stack = refs[:-1], refs[-1]
    stack_gradients(grads, grad_stack)
    both = jnp.concatenate([stack[...] for stack in stacks], axis=1)
    total = dot(both, grad_stack[...], NT)
    extra = JOINT - PIECE
    for part, out in enumerate(outs):
        rows = slice(part * extra, (part + 1) * extra)
        out[:PIECE, :] = total[part * PIECE : (part + 1) * PIECE].astype(out.dtype)
        out[PIECE:, :] = (mixed[0][rows, :] + mixed[1][rows, :].astype(WIDE)).astype(out.dtype)


def own_filter_kernel(place, grads, stacks, send_out, keep_out, grad_stack):
    stack_gradients([grads], grad_stack)
    send_out[...] = dot(stacks[1][...], grad_stack[...], NT).astype(LOW)
    keep_out[...] = dot(stacks[0][...], grad_stack[...], NT)


def split_kernel(place, keep, received, *outs):
    for part, out in enumerate(outs):
        rows = slice(part * PIECE, (part + 1) * PIECE)
        out[...] = (keep[rows, :] + received[rows, :].astype(WIDE)).astype(out.dtype)


def conv_back(place, grads, weight, grad_stack, product, value):
    stack_gradient(grads.at[0], grad_stack)
    product[...] = dot(weight[...], grad_stack[...], NN)
    back_to_channels(place, product, value)


def second_back_kernel(
    place,
    grads,
    weight,
    normed_ref,
    stats_first,
    stats,
    mask_ref,
    params,
    member,
    first_grad_out,
    small_out,
    grad_stack,
    product,
    value,
):
    conv_back(place, grads, weight, grad_stack, product, value)
    mask = mask_ref[0]
    count = count_of(mask)
    gain, bias = params[:, 2:3], params[:, 3:4]
    factor = stats_first[0, :, 0:1]
    time_scale, time_shift = 1.0 + stats[0, :, 2:3], stats[0, :, 3:4]
    normed = normed_ref[0]
    hidden = (normed * gain + bias) * time_scale + time_shift
    delta = value[...] * mask * silu_slope(hidden)
    value[...] = delta
    plain = jnp.sum(delta, axis=1, keepdims=True)
    weighted = jnp.sum(delta * normed, axis=1, keepdims=True)
    scaled = gain * time_scale
    sums = group_sums(member[...], lane_pair(scaled * plain, scaled * weighted))
    first_sum, second_sum = sums[:, 0:1] / count, sums[:, 1:2] / count
    first_grad_out[0] = (
        factor * (value[...] * scaled - mask * (first_sum + normed * second_sum))
    ).astype(LOW)
    small_out[0] = small_rows(
        (
            time_scale * weighted,
            time_scale * plain,
            gain * weighted + bias * plain,
            plain,
        )
    )


def first_back_kernel(place, *refs):
    (
        grads,
        weight,
        whole,
        stats_first,
        residual_grad,
        mask_ref,
        params,
        member,
        small_in,
        keep_out,
        send_out,
        small_out,
        grad_stack,
        product,
        value,
    ) = refs[-15:]
    conv_back(place, grads, weight, grad_stack, product, value)
    own, other = half_offsets(place)
    mask = mask_ref[0]
    count = count_of(mask)
    gain, bias = params[:, 0:1], params[:, 1:2]
    mean, factor = stats_first[0, :, 0:1], stats_first[0, :, 1:2]
    normed = (whole[0].astype(WIDE) - mean) * factor
    hidden = normed * gain + bias
    delta = value[...] * mask * silu_slope(hidden)
    value[...] = delta
    plain = jnp.sum(delta, axis=1, keepdims=True)
    weighted = jnp.sum(delta * normed, axis=1, keepdims=True)
    sums = group_sums(member[...], lane_pair(gain * plain, gain * weighted))
    first_sum, second_sum = sums[:, 0:1] / count, sums[:, 1:2] / count
    value[...] = residual_grad[0] + factor * (
        value[...] * gain - mask * (first_sum + normed * second_sum)
    )
    keep_out[0] = value[pl.ds(own, HALF), :]
    send_out[0] = value[pl.ds(other, HALF), :].astype(LOW)
    rows = small_rows((weighted, plain))
    if len(small_in) == 0:
        small_out[...] = rows
    else:
        earlier, second, third, steps = small_in
        for ref in earlier:
            rows = rows + ref[...]
        images = second.shape[0]
        second_sum, third_sum = second[0], third[0]
        for image in range(1, images):
            second_sum, third_sum = second_sum + second[image], third_sum + third[image]
        small_out[:8, :] = set_rows(
            [
                rows[0:1],
                second_sum[0:1],
                third_sum[0:1],
                rows[1:2],
                second_sum[1:2],
                third_sum[1:2],
            ],
            8,
        )
        small_out[8:, :] = set_rows(
            [second[image, 2 + kind : 3 + kind] for kind in range(2) for image in range(images)]
            + [steps[0:1]],
            8,
        )


def cut_kernel(place, own, one, two, three, mine_out, side_out, far_out, corner_out):
    total = own[...] + one[...].astype(WIDE) + two[...].astype(WIDE) + three[...].astype(WIDE)
    left = place[BLOCKS] == 0
    outs = ((mine_out, side_out), (far_out, corner_out))
    for part in range(2):
        rows = jnp.concatenate(
            [total[tap * PAIR + part * ROWS : tap * PAIR + (part + 1) * ROWS] for tap in range(3)],
            axis=0,
        )
        halves = [rows[:, : 3 * HALF], rows[:, 3 * HALF :]]
        here, away = outs[part]
        here[...] = jnp.where(left, halves[0], halves[1]).astype(here.dtype)
        away[...] = jnp.where(left, halves[1], halves[0]).astype(away.dtype)


def unpack(rows, columns):
    return jnp.concatenate(
        [rows[:, third * columns : (third + 1) * columns] for third in range(3)], axis=0
    )


def pack(rows):
    count = rows.shape[0] // 3
    return jnp.concatenate(
        [rows[third * count : (third + 1) * count] for third in range(3)], axis=1
    )


def cut_columns_kernel(place, own, one, two, three, mine_out, side_out):
    total = own[...] + one[...].astype(WIDE) + two[...].astype(WIDE) + three[...].astype(WIDE)
    left = place[BLOCKS] == 0
    wide, output = total[: PIECE + PAIR], unpack(total[PIECE + PAIR :], C)
    halves = [
        jnp.concatenate(
            [
                wide[:, half * 3 * HALF : (half + 1) * 3 * HALF],
                pack(output[:, half * HALF : (half + 1) * HALF]),
            ],
            axis=0,
        )
        for half in range(2)
    ]
    mine_out[...] = jnp.where(left, halves[0], halves[1])
    side_out[...] = jnp.where(left, halves[1], halves[0]).astype(LOW)


def cut_rows_kernel(place, own, received, near_out, far_out):
    total = own[...] + received[...].astype(WIDE)
    output = unpack(total[PIECE + PAIR :], HALF)
    for part, out in enumerate((near_out, far_out)):
        rows = [
            total[tap * PAIR + part * ROWS : tap * PAIR + (part + 1) * ROWS] for tap in range(4)
        ]
        rows.append(pack(output[part * ROWS : (part + 1) * ROWS]))
        out[...] = jnp.concatenate(rows, axis=0).astype(out.dtype)


def finish_kernel(place, own, received, filter_out, *mixed_outs):
    total = own[...]
    for ref in received:
        total = total + ref[...].astype(WIDE)
    for down in range(3):
        for across in range(3):
            filter_out[3 * down + across] = total[
                across * ROWS : (across + 1) * ROWS, down * HALF : (down + 1) * HALF
            ]
    if mixed_outs:
        mixed_outs[0][...] = total[3 * ROWS : 4 * ROWS]
        mixed_outs[1][...] = unpack(total[4 * ROWS :], HALF)


def receive_kernel(place, carried, received, out):
    for image, ref in enumerate(received):

        @pl.when(pl.program_id(0) == image)
        def _(ref=ref):
            out[...] = ref[...].astype(out.dtype)


def shape(*sizes, dtype=WIDE):
    return jax.ShapeDtypeStruct(sizes, dtype)


def per_image(*sizes, first=0):
    return pl.BlockSpec((1,) + sizes, lambda g, place: (first + g,) + (0,) * len(sizes))


def own_image(*sizes, first=0):
    return pl.BlockSpec(
        (1,) + sizes, lambda g, place: (place[BLOCKS + 1] + first + g,) + (0,) * len(sizes)
    )


def other_image(*sizes):
    return pl.BlockSpec(
        (1,) + sizes, lambda g, place: (place[BLOCKS + 2] + g,) + (0,) * len(sizes)
    )


def per_columns(*sizes, first=0):
    return pl.BlockSpec(sizes, lambda g, place: (0, first + g))


def fixed(*sizes):
    return pl.BlockSpec(sizes, lambda g, place: (0,) * len(sizes))


def whole_array(entry):
    return fixed(*entry.shape)


def run(kernel, place, images, ins, outs, scratch, aliases=None, room=24, cost=8):
    arrays, structure = jax.tree.flatten([array for array, _ in ins])
    specs = jax.tree.leaves(
        [spec for _, spec in ins], is_leaf=lambda entry: isinstance(entry, pl.BlockSpec)
    )

    def body(place, *refs):
        given = jax.tree.unflatten(structure, refs[: len(arrays)])
        kernel(place, *given, *refs[len(arrays) :])

    return pl.pallas_call(
        body,
        grid_spec=pltpu.PrefetchScalarGridSpec(
            num_scalar_prefetch=1,
            grid=(images,),
            in_specs=specs,
            out_specs=[spec for _, spec in outs],
            scratch_shapes=scratch,
        ),
        out_shape=[out for out, _ in outs],
        input_output_aliases=aliases or {},
        compiler_params=pltpu.CompilerParams(
            dimension_semantics=("arbitrary",), vmem_limit_bytes=room * 2**20
        ),
        cost_estimate=pl.CostEstimate(flops=cost * 10**9, bytes_accessed=2**20, transcendentals=0),
    )(place, *arrays)


def filter_gradient(place, stacks, grads, mixed):
    images = sum(grad.shape[0] for grad in grads)
    ins = (grads, stacks, mixed)
    outs = [shape(JOINT, TAPS)] + [shape(JOINT, TAPS, dtype=LOW)] * 3
    return run(
        filter_kernel,
        place,
        1,
        [(entry, jax.tree.map(whole_array, entry)) for entry in ins],
        [(out, whole_array(out)) for out in outs],
        [pltpu.VMEM((TAPS, images * PIX), LOW)],
        room=40,
    )


def own_filter_gradient(place, stacks, grads):
    ins = (grads, stacks)
    outs = [shape(TAPS // 2, TAPS, dtype=LOW), shape(TAPS // 2, TAPS)]
    return run(
        own_filter_kernel,
        place,
        1,
        [(entry, jax.tree.map(whole_array, entry)) for entry in ins],
        [(out, whole_array(out)) for out in outs],
        [pltpu.VMEM((TAPS, grads.shape[0] * PIX), LOW)],
        room=32,
        cost=1,
    )


def simple(kernel, place, ins, outs, cost):
    return run(
        kernel,
        place,
        1,
        [(entry, jax.tree.map(whole_array, entry)) for entry in ins],
        [(out, whole_array(out)) for out in outs],
        [],
        cost=cost,
    )


def on_device(
    dp,
    features,
    pixel_masks,
    timesteps,
    first_filter,
    second_filter,
    project_weight,
    output_weight,
    embed_weight,
    norm_gains,
    norm_biases,
    cotangent,
):
    chan = lax.axis_index("chan")
    left = chan == 0
    span = dp // BLOCKS
    groups = [list(range(k * span, (k + 1) * span)) for k in range(BLOCKS)]
    block = lax.axis_index("dp") // span
    images = features.shape[0] // 2

    def swap(value, mask, flip):
        pairs = [
            (2 * d + x, 2 * (d ^ (mask * span)) + (x ^ flip)) for d in range(dp) for x in range(2)
        ]
        return lax.ppermute(value, ("dp", "chan"), pairs)

    def near(value, axis):
        if span == 1:
            return value
        return lax.all_gather(value, "dp", axis=axis, tiled=True, axis_index_groups=groups)

    def halves(mine, theirs, axis):
        return jnp.concatenate(
            [jnp.where(left, mine, theirs), jnp.where(left, theirs, mine)], axis=axis
        )

    def after(value, *others):
        return lax.optimization_barrier((value, others))[0]

    def pair_up(one, two):
        taps = one.shape[0] // ROWS
        columns = one.shape[1]
        both = [v.reshape(taps, ROWS, columns) for v in (one, two)]
        return jnp.stack(both, axis=1).reshape(2 * taps * ROWS, columns)

    def gather_one(shard, extra=None):
        side = swap(shard if extra is None else jnp.concatenate([shard, extra], axis=0), 0, 1)
        far = swap(shard, 8, 0)
        both = swap(shard, 8, 1)
        count = shard.shape[0]
        rows = pair_up(halves(shard, side[:count], 1), halves(far, both, 1))
        return rows if extra is None else (rows, side[count:])

    def gather_slow(shard, late):
        rows = after(pair_up(shard, swap(shard, 8, 0)), late)
        return halves(rows, swap(rows, 0, 1), 1)

    def gather_two(rows):
        return [rows, swap(rows, 4, 0), swap(rows, 2, 0), swap(rows, 6, 0)]

    def gather_three(pieces):
        return [swap(rows, 1, 0) for rows in pieces]

    def scatter_one(send, keep):
        outs = [shape(PIECE, TAPS)] + [shape(PIECE, TAPS, dtype=LOW)] * 3
        return simple(split_kernel, place, [keep, swap(send, 1, 0)], outs, 1)

    def scatter_two(keep, *sends):
        arrived = [swap(send, mask, 0) for send, mask in zip(sends, (4, 2, 6))]
        outs = [shape(3 * ROWS, 3 * HALF)] + [shape(3 * ROWS, 3 * HALF, dtype=LOW)] * 3
        return simple(cut_kernel, place, [keep] + arrived, outs, 30)

    def scatter_three(keep, *sends):
        arrived = [
            swap(send, mask, flip) for send, (mask, flip) in zip(sends, ((0, 1), (8, 0), (8, 1)))
        ]
        return simple(finish_kernel, place, [keep, arrived], [shape(9, ROWS, HALF)], 1)[0]

    def joint_two(keep, *sends, late):
        arrived = [swap(send, mask, 0) for send, mask in zip(sends, (4, 2, 6))]
        outs = [shape(JOINT, 3 * HALF), shape(JOINT, 3 * HALF, dtype=LOW)]
        return simple(cut_columns_kernel, place, [after(keep, late)] + arrived, outs, 30)

    def joint_three(keep, send, late):
        outs = [shape(JOINT // 2, 3 * HALF), shape(JOINT // 2, 3 * HALF, dtype=LOW)]
        ins = [after(keep, late), swap(send, 0, 1)]
        return simple(cut_rows_kernel, place, ins, outs, 1)

    def joint_four(keep, send, late):
        outs = [shape(9, ROWS, HALF), shape(ROWS, 3 * HALF), shape(ROWS, HALF)]
        ins = [after(keep, late), [swap(send, 8, 0)]]
        return simple(finish_kernel, place, ins, outs, 1)

    def share(value, dimension):
        if span == 1:
            return value
        return lax.psum_scatter(
            value, "dp", scatter_dimension=dimension, tiled=True, axis_index_groups=groups
        )

    def parts_of(value):
        high = value.astype(LOW)
        rest = value - high.astype(WIDE)
        middle = rest.astype(LOW)
        return [high, middle, (rest - middle.astype(WIDE)).astype(LOW)]

    own_start, other_start = chan * images, (1 - chan) * images

    def others(value):
        return lax.dynamic_slice_in_dim(value, other_start, images, 0)

    theirs = swap(others(features), 0, 1)

    def filter_rows(weight):
        rows = near(weight.astype(LOW), 1).reshape(3, 3, ROWS, HALF)
        return jnp.transpose(rows, (1, 2, 0, 3)).reshape(3 * ROWS, 3 * HALF)

    norms = jnp.concatenate([norm_gains, norm_biases], axis=0)
    norm_rows = jnp.pad(jnp.concatenate(parts_of(norms), axis=1), ((0, 2), (0, 0)))
    first_one, norm_rows = gather_one(filter_rows(first_filter), norm_rows)
    their_norms = norm_rows[:6].astype(WIDE).reshape(6, 3, HALF)
    their_norms = their_norms[:, 0] + their_norms[:, 1] + their_norms[:, 2]
    norms = halves(norms, their_norms, 1)
    params = jnp.stack([norms[0], norms[3], norms[1], norms[4], norms[2], norms[5]], axis=1)
    params = jnp.pad(params, ((0, 0), (0, 2)))
    first_pieces = gather_two(first_one)

    embed_rows = jnp.transpose(near(embed_weight.astype(LOW), 1), (1, 0, 2))
    embed_rows = jnp.transpose(embed_rows.reshape(PAIR, 3, 128), (1, 0, 2))
    embed_rows = embed_rows.reshape(2, 3 * ROWS, 128)
    second_rows = jnp.concatenate(
        [filter_rows(second_filter), embed_rows[0], embed_rows[1]], axis=1
    )
    bundle_rows = jnp.concatenate(
        [
            near(project_weight.astype(LOW), 0).reshape(ROWS, 3 * HALF),
            near(output_weight.astype(LOW), 1).T,
        ],
        axis=1,
    )
    second_one = gather_slow(second_rows, first_one)
    bundle_one = gather_slow(after(bundle_rows, theirs), second_one)
    first_pieces = first_pieces + gather_three(
        [after(first_pieces[0], theirs)] + first_pieces[1:]
    )

    validity = lax.dynamic_slice_in_dim(pixel_masks, own_start, images, 0).astype(WIDE)
    validity = validity.reshape(images, 1, PIX)
    member = (jnp.arange(C)[:, None] // WIDTH == jnp.arange(C)[None, :] // WIDTH).astype(LOW)
    order = jnp.array(ORDER, jnp.int32)
    place = jnp.concatenate(
        [
            jnp.bitwise_xor(block, order) * ROWS,
            jnp.stack([chan, own_start, other_start]).astype(jnp.int32),
        ]
    )

    def time_features(steps, index, embed_width):
        half_width = embed_width // 2
        power = jnp.where(index < half_width, index, index - half_width).astype(WIDE)
        frequency = jnp.exp(-math.log(10000.0) * power / half_width)
        angles = steps[:, None] * frequency[None, :]
        return jax.nn.silu(
            jnp.where(index[None, :] < half_width, jnp.cos(angles), jnp.sin(angles))
        )

    embed_width = embed_weight.shape[1] * dp
    own_steps = lax.dynamic_slice_in_dim(timesteps, own_start, images, 0).astype(WIDE)
    flat = jnp.arange(2 * 3 * ROWS)
    third, entry_row = flat // PAIR, flat % PAIR
    embed_index = (jnp.bitwise_xor(block, order)[:, None] * PAIR + entry_row).reshape(-1)
    embed_values = time_features(own_steps, embed_index, embed_width)
    embed_split = jnp.stack(parts_of(embed_values), axis=2)
    embed_split = embed_split.reshape(images, PAIRS, 2, 2, 3, ROWS, 3)
    embed_split = jnp.transpose(embed_split, (0, 3, 1, 4, 2, 5, 6))
    late = (third.reshape(2, 3, ROWS) == jnp.array([1, 2])[:, None, None])
    late = late[None, :, None, :, None, :, None]
    embed_parts = jnp.concatenate(
        [jnp.where(late, 0, embed_split), jnp.where(late, embed_split, 0)], axis=6
    ).reshape(images, 2, TAPS, 6)
    embed_parts = jnp.pad(embed_parts, ((0, 0), (0, 0), (0, 0), (0, 122)))
    steps_row = jnp.pad(own_steps, (0, HALF - images))
    steps_row = jnp.pad(jnp.concatenate([steps_row, steps_row])[None, :], ((0, 7), (0, 0)))

    value_scratch = pltpu.VMEM((C, PIX), WIDE)
    product_scratch = pltpu.VMEM((TAPS, PIX), WIDE)
    back_scratch = [pltpu.VMEM((TAPS, PIX), LOW), product_scratch, value_scratch]
    mask_in = (validity, per_image(1, PIX))
    params_in = (params, fixed(C, 8))
    member_in = (member, fixed(C, C))
    image_low = (shape(images, C, PIX, dtype=LOW), per_image(C, PIX))
    image_wide = (shape(images, C, PIX), per_image(C, PIX))
    image_small = (shape(images, C, 128), per_image(C, 128))
    image_rows = (shape(images, 8, C), per_image(8, C))
    weight_out = (shape(TAPS, TAPS, dtype=LOW), fixed(TAPS, TAPS))
    stack_out = (shape(TAPS // 2, images * PIX, dtype=LOW), per_columns(TAPS // 2, PIX))
    anywhere = pl.BlockSpec(memory_space=pl.ANY)

    prepared = run(
        prepare_kernel,
        place,
        images,
        [
            (features, own_image(HALF, PIX)),
            (theirs, per_image(HALF, PIX)),
            mask_in,
            params_in,
            member_in,
        ],
        [image_low, stack_out, stack_out, image_small],
        [value_scratch],
    )
    whole, first_low, first_high, stats_whole = prepared
    cots = others(cotangent)
    second_normed, stats_first, first_weight = run(
        first_kernel,
        place,
        images,
        [
            mask_in,
            member_in,
            (first_pieces, [fixed(PIECE, TAPS)] * 8),
            (after([first_low, first_high], second_one, cots), [per_columns(TAPS // 2, PIX)] * 2),
        ],
        [image_wide, image_small, weight_out],
        [value_scratch, product_scratch],
    )
    second_pieces = gather_two(second_one)
    second_pieces = second_pieces + gather_three(after(second_pieces, second_normed))
    bundle_pieces = gather_two(bundle_one)
    their_cots = swap(after(cots, second_normed), 0, 1)
    second_low, second_high, residual, attend_input, stats_second, second_weight = run(
        second_kernel,
        place,
        images,
        [
            (after(second_normed, bundle_one), per_image(C, PIX)),
            (whole, per_image(C, PIX)),
            (embed_parts, per_image(2, TAPS, 128)),
            mask_in,
            params_in,
            member_in,
            (second_pieces, [fixed(PIECE, 2 * SECOND)] * 8),
        ],
        [stack_out, stack_out, image_wide, image_low, image_small, weight_out],
        [pltpu.VMEM((2, 2, TAPS, 128), LOW), value_scratch, product_scratch],
        room=60,
    )
    bundle_pieces = bundle_pieces + gather_three(after(bundle_pieces, attend_input))
    second_theirs = swap(second_high, 1, 0)
    mixed_rows = PAIRS // 2 * (JOINT - PIECE)
    block_keep, block_send, residual_grad, second_grad, *mixed, small_third = run(
        attend_kernel,
        place,
        images,
        [
            (attend_input, per_image(C, PIX)),
            (residual, per_image(C, PIX)),
            (stats_second, per_image(C, 128)),
            (cotangent, own_image(HALF, PIX)),
            (their_cots, per_image(HALF, PIX)),
            mask_in,
            params_in,
            member_in,
            (bundle_pieces, [fixed(PAIR, 2 * MIXED)] * 8),
        ],
        [
            (shape(2 * images, HALF, PIX, dtype=LOW), own_image(HALF, PIX)),
            (shape(images, HALF, PIX, dtype=LOW), per_image(HALF, PIX)),
            image_wide,
            image_low,
            (shape(mixed_rows, TAPS), fixed(mixed_rows, TAPS)),
            (shape(mixed_rows, TAPS, dtype=LOW), fixed(mixed_rows, TAPS)),
            image_rows,
        ],
        [
            pltpu.VMEM((2, C, 2 * C), WIDE),
            pltpu.VMEM((C, TAPS), LOW),
            pltpu.VMEM((C, C), LOW),
            pltpu.VMEM((C, PIX), LOW),
            pltpu.VMEM((TAPS, PIX), LOW),
            pltpu.VMEM((C, PIX), LOW),
            pltpu.VMEM((C, PIX), LOW),
            pltpu.VMEM((TAPS, PIX), LOW),
            pltpu.VMEM((PIX, KEYS), LOW),
            pltpu.VMEM((PIX, KEYS), LOW),
            pltpu.VMEM((HEAD + 16, PIX), LOW),
            pltpu.VMEM((KEYS, PIX), LOW),
            pltpu.VMEM((KEYS, PIX), LOW),
            pltpu.VMEM((PIX, PIX), WIDE),
            pltpu.VMEM((PIX, PIX), LOW),
            pltpu.VMEM((PIX, PIX), LOW),
            pltpu.VMEM((C, TAPS + C), WIDE),
            value_scratch,
        ],
        room=62,
        cost=60,
    )
    block_theirs = swap(block_send, 0, 1)
    mixed = [mixed[0], swap(mixed[1], 1, 0)]
    grads_theirs = swap(second_grad, 1, 0)
    joint = filter_gradient(
        place, [second_low, second_theirs], [second_grad, grads_theirs], mixed
    )
    first_grad, small_second = run(
        second_back_kernel,
        place,
        images,
        [
            (after(second_grad, joint), per_image(C, PIX)),
            (second_weight, fixed(TAPS, TAPS)),
            (second_normed, per_image(C, PIX)),
            (stats_first, per_image(C, 128)),
            (stats_second, per_image(C, 128)),
            mask_in,
            params_in,
            member_in,
        ],
        [image_low, image_rows],
        back_scratch,
    )
    masked_out = lax.dynamic_update_slice_in_dim(
        after(block_keep, joint), block_theirs, other_start, 0
    )
    send, keep = own_filter_gradient(
        place, [first_low, first_high], after(first_grad, masked_out)
    )
    first_part = scatter_one(send, keep)
    joint = joint_two(*joint, late=send)
    input_grad, input_theirs, smalls = None, [], []
    back_grad = after(first_grad, first_part, joint)
    for image in range(images):
        last = image == images - 1
        small_in = (smalls, small_second, small_third, steps_row) if last else ()
        carried = [] if input_grad is None else [(input_grad, anywhere)]
        small_shape = shape(16 if last else 8, C)
        input_grad, input_send, small = run(
            first_back_kernel,
            place,
            1,
            carried
            + [
                (back_grad, per_image(C, PIX, first=image)),
                (first_weight, fixed(TAPS, TAPS)),
                (whole, per_image(C, PIX, first=image)),
                (stats_whole, per_image(C, 128, first=image)),
                (residual_grad, per_image(C, PIX, first=image)),
                (validity, per_image(1, PIX, first=image)),
                params_in,
                member_in,
                (small_in, jax.tree.map(whole_array, small_in)),
            ],
            [
                (shape(2 * images, HALF, PIX), own_image(HALF, PIX, first=image)),
                (shape(1, HALF, PIX, dtype=LOW), per_image(HALF, PIX)),
                (small_shape, whole_array(small_shape)),
            ],
            back_scratch,
            {1: 0} if carried else None,
        )
        smalls.append(small)
        input_theirs.append(swap(input_send, 0, 1))
        if image == 0:
            joint = joint_three(*joint, late=small)
            back_grad = after(back_grad, joint)
    first_part = scatter_two(*first_part)
    message = after(smalls[-1], input_theirs[:-1])

    def merge(arrived):
        total = sum(message[:8] for message in arrived)
        return jnp.concatenate([total] + [message[8:] for message in arrived], axis=0)

    message = after(merge([message, swap(message, 1, 0)]), first_part)
    joint = joint_four(*joint, late=first_part)
    grad_first = share(scatter_three(*first_part), 1)
    grad_second = share(joint[0], 1)
    grad_project = share(joint[1].reshape(ROWS, 3, HALF), 0)
    grad_output = share(joint[2].T, 1)
    (input_grad,) = run(
        receive_kernel,
        place,
        images,
        [(input_grad, anywhere), (input_theirs, [fixed(1, HALF, PIX)] * images)],
        [(shape(2 * images, HALF, PIX), other_image(HALF, PIX))],
        [],
        {1: 0},
        cost=1,
    )

    message = merge([message] + [swap(message, m, 0) for m in (4, 2, 6)])
    one, two = after(message[:, :HALF], input_theirs[-1]), message[:, HALF:]
    own, away = jnp.where(left, one, two), jnp.where(left, two, one)
    message = merge([own, swap(away, 0, 1), swap(own, 8, 0), swap(away, 8, 1)])
    total, entries = message[:6], message[8:]
    if span > 1:
        total = lax.psum(total, "dp", axis_index_groups=groups)
        entries = lax.all_gather(entries, "dp", axis=0, tiled=True, axis_index_groups=groups)
    entries = entries.reshape(-1, 8, HALF)
    all_steps = entries[:, 2 * images, :images].reshape(-1)
    scale_grads = entries[:, :images].reshape(-1, HALF)
    shift_grads = entries[:, images : 2 * images].reshape(-1, HALF)
    rows = embed_weight.shape[1]
    row_index = lax.axis_index("dp") * rows + jnp.arange(rows)
    all_embed = time_features(all_steps, row_index, embed_width)
    grad_embed = jnp.einsum(
        "be,kbd->ked",
        all_embed,
        jnp.stack([scale_grads, shift_grads]),
        precision=lax.Precision.HIGHEST,
    )
    return (
        masked_out,
        input_grad,
        grad_first,
        grad_second,
        grad_project,
        grad_output,
        grad_embed,
        total[:3],
        total[3:],
    )


def solution(mesh):
    in_specs = (
        P("dp", "chan", None),
        P("dp", None),
        P("dp"),
        P(None, "dp", "chan"),
        P(None, "dp", "chan"),
        P("dp", None, "chan"),
        P("chan", "dp"),
        P(None, "dp", "chan"),
        P(None, "chan"),
        P(None, "chan"),
        P("dp", "chan", None),
    )
    out_specs = (
        P("dp", "chan", None),
        P("dp", "chan", None),
        P(None, "dp", "chan"),
        P(None, "dp", "chan"),
        P("dp", None, "chan"),
        P("chan", "dp"),
        P(None, "dp", "chan"),
        P(None, "chan"),
        P(None, "chan"),
    )
    return jax.shard_map(
        functools.partial(on_device, mesh.shape["dp"]),
        mesh=mesh,
        in_specs=in_specs,
        out_specs=out_specs,
        check_vma=False,
    )
```

profile of v0, /device:TPU:0, one launch (start us, length us, event | category | flops | bytes accessed | tf_op | source)
XLA Modules:
  0.0 268.8 jit_solution(105425497801184132)
XLA Ops:
  1.9 4.1 %collective-permute-start.1 = (bf16[72,576]{1,0:T(8,128)(2,1)S(1)}, bf16[72,576]{1,0:T(8,128)(2,1)S(1)}, u32[]{:S(2)}, u32[]{:S(2)}) collective-permute-start(bf16[72,576]{1,0:T(8,128)(2,1)S(1)} %reshape.345), channel_id=1, source_target_pairs={{0,16},{1,17},{2,18},{3,19},{4,20},{5,21},{6,22},{7,23},{8,24},{9,... | collective-permute-start | bytes 248840 | tf_op jit(solution)/shard_map/ppermute | solution.py:827
  6.0 1.3 collective-permute-start.2
  9.1 2.2 constant_dynamic-slice_fusion.1
  11.3 1.7 collective-permute-start.6
  14.9 2.6 collective-permute-start.11
  23.9 2.5 collective-permute-start.5
  32.4 5.2 %collective-permute-done.12 = bf16[144,832]{1,0:T(8,128)(2,1)} collective-permute-done((bf16[144,832]{1,0:T(8,128)(2,1)}, bf16[144,832]{1,0:T(8,128)(2,1)}, u32[]{:S(2)}, u32[]{:S(2)}) %collective-permute-start.12) | collective-permute-done | bytes 239648 | tf_op jit(solution)/shard_map/ppermute | solution.py:827
  40.8 1.2 collective-permute-start.13
  42.1 5.8 %shard_map.196 = (bf16[2,384,1024]{2,1,0:T(8,128)(2,1)S(1)}, bf16[576,2048]{1,0:T(8,128)(2,1)S(1)}, bf16[576,2048]{1,0:T(8,128)(2,1)S(1)}, f32[2,384,128]{2,1,0:T(8,128)S(1)}) custom-call(s32[19]{0:T(128)S(1)} %pad_add_fusion.place, bf16[4,192,1024]{2,1,0:T(8,128)(2,1)S(1)} %copy-done.4, bf16[2,192,1024]{2,1,0:T(8,128)(2,1)S(1)} %collective-permute-done.6.refs_1_, ...), custom_call_target="tpu_custom_call" | custom-call | flops 8000000000 | bytes 1048576 | tf_op jit(solution)/shard_map/pallas_call | solution.py:742
  49.9 3.2 %collective-permute-start.15 = (bf16[144,1664]{1,0:T(8,128)(2,1)}, bf16[144,1664]{1,0:T(8,128)(2,1)S(1)}, u32[]{:S(2)}, u32[]{:S(2)}) collective-permute-start(bf16[144,1664]{1,0:T(8,128)(2,1)} %pad_maximum_fusion.refs_6_), channel_id=1, source_target_pairs={{0,8},{1,9},{2,10},{3,11},{4,12},{5,13},{6,14},{7,15},{8,0},{9,1},... | collective-permute-start | bytes 1437704 | tf_op jit(solution)/shard_map/ppermute | solution.py:827
  53.1 1.6 collective-permute-start.16
  55.3 11.8 %shard_map.197 = (f32[2,384,1024]{2,1,0:T(8,128)S(1)}, f32[2,384,128]{2,1,0:T(8,128)S(1)}, bf16[1152,1152]{1,0:T(8,128)(2,1)S(1)}) custom-call(s32[19]{0:T(128)S(1)} %pad_add_fusion.place, f32[2,1,1024]{2,1,0:T(1,128)S(1)} %reshape.343.refs_2_.refs_0_.refs_3_.refs_5_.refs_6_, ...), custom_call_target="tpu_custom_call" | custom-call | flops 8000000000 | bytes 1048576 | tf_op jit(solution)/shard_map/pallas_call | solution.py:742
  67.1 1.6 copy-done.16
  68.7 1.7 copy-done.18
  71.1 5.0 %collective-permute-done.16.refs_8_ = bf16[144,1664]{1,0:T(8,128)(2,1)} collective-permute-done((bf16[144,1664]{1,0:T(8,128)(2,1)}, bf16[144,1664]{1,0:T(8,128)(2,1)}, u32[]{:S(2)}, u32[]{:S(2)}) %collective-permute-start.16) | collective-permute-done | bytes 479264 | tf_op jit(solution)/shard_map/ppermute | solution.py:827
  77.2 1.2 copy.95
  78.4 1.2 pad.22.refs_2_
  81.6 1.7 collective-permute-start.25
  83.8 20.0 %shard_map.198 = (bf16[576,2048]{1,0:T(8,128)(2,1)}, bf16[576,2048]{1,0:T(8,128)(2,1)}, f32[2,384,1024]{2,1,0:T(8,128)}, bf16[2,384,1024]{2,1,0:T(8,128)(2,1)}, ...) custom-call(s32[19]{0:T(128)} %copy-done.9, f32[2,384,1024]{2,1,0:T(8,128)} %copy-done.18, ...), custom_call_target="tpu_custom_call" | custom-call | flops 8000000000 | bytes 1048576 | tf_op jit(solution)/shard_map/pallas_call | solution.py:742
  107.1 67.5 %shard_map.199 = (bf16[4,192,1024]{2,1,0:T(8,128)(2,1)}, bf16[2,192,1024]{2,1,0:T(8,128)(2,1)}, f32[2,384,1024]{2,1,0:T(8,128)}, bf16[2,384,1024]{2,1,0:T(8,128)...) custom-call(s32[19]{0:T(128)} %copy-done.9, ...), custom_call_target="tpu_custom_call" | custom-call | flops 60000002048 | bytes 1048576 | tf_op jit(solution)/shard_map/pallas_call | solution.py:742
  175.3 1.6 collective-permute-start.33
  176.9 2.2 collective-permute-done.32.refs_5_
  179.1 1.4 copy-done.13
  180.5 1.7 copy-done.21
  182.2 1.3 copy-done.24
  183.5 9.1 %shard_map.200 = (f32[208,1152]{1,0:T(8,128)S(1)}, bf16[208,1152]{1,0:T(8,128)(2,1)S(1)}, bf16[208,1152]{1,0:T(8,128)(2,1)S(1)}, bf16[208,1152]{1,0:T(8,128)(2,1)S(1)}) custom-call(s32[19]{0:T(128)S(1)} %copy-done.10, bf16[2,384,1024]{2,1,0:T(8,128)(2,1)S(1)} %copy-done.13, bf16[2,384,1024]{2,1,0:T(8,128)(2,1)S(1)} %collective-permute-done.30.refs_1_, ...), custom_call_target="tpu_custom_call" | custom-call | flops 8000000000 | bytes 1048576 | tf_op jit(solution)/shard_map/pallas_call | solution.py:742
  192.6 1.2 collective-permute-start.35
  194.5 1.7 collective-permute-start.37
  196.3 11.3 %shard_map.201 = (bf16[2,384,1024]{2,1,0:T(8,128)(2,1)S(1)}, f32[2,8,384]{2,1,0:T(8,128)S(1)}) custom-call(s32[19]{0:T(128)S(1)} %copy-done.10, bf16[2,384,1024]{2,1,0:T(8,128)(2,1)S(1)} %copy-done.14, bf16[1152,1152]{1,0:T(8,128)(2,1)S(1)} %copy-done.20, f32[2,384,1024]{2,1,0:T(8,128)S(1)} %copy-done.19, f32[2,384,128]{2,1,0:T(8,128)S(1)} %copy-done.29, ...), custom_call_target="tpu_custom_call" | custom-call | flops 8000000000 | bytes 1048576 | tf_op jit(solution)/shard_map/pallas_call | solution.py:742
  208.8 6.9 %shard_map.202 = (bf16[576,1152]{1,0:T(8,128)(2,1)S(1)}, f32[576,1152]{1,0:T(8,128)S(1)}) custom-call(s32[19]{0:T(128)S(1)} %copy-done.10, bf16[2,384,1024]{2,1,0:T(8,128)(2,1)S(1)} %get-tuple-element.143.refs_0_.refs_1_, bf16[576,2048]{1,0:T(8,128)(2,1)S(1)} %copy-done.1, bf16[576,2048]{1,0:T(8,128)(2,1)S(1)} %copy-done.3), custom_call_target="tpu_custom_call" | custom-call | flops 1000000000 | bytes 1048576 | tf_op jit(solution)/shard_map/pallas_call | solution.py:742
  215.8 1.3 collective-permute-done.37.refs_3_
  218.1 1.6 collective-permute-start.38
  221.3 1.5 collective-permute-start.42
  224.0 6.6 %shard_map.205 = (f32[4,192,1024]{2,1,0:T(8,128)}, bf16[1,192,1024]{2,1,0:T(8,128)(2,1)S(1)}, f32[8,384]{1,0:T(8,128)S(1)}) custom-call(s32[19]{0:T(128)S(1)} %copy-done.10, bf16[2,384,1024]{2,1,0:T(8,128)(2,1)S(1)} %get-tuple-element.143.refs_0_.refs_1_, bf16[1152,1152]{1,0:T(8,128)(2,1)S(1)} %copy-done.17, bf16[2,384,1024]{2,1,0:T(8,128)(2,1)S(1)} %copy-done.23, ...), custom_call_target="tpu_custom_call" | custom-call | flops 8000000000 | bytes 1048576 | tf_op jit(solution)/shard_map/pallas_call | solution.py:742
  232.4 6.8 %shard_map.207 = (f32[4,192,1024]{2,1,0:T(8,128)}, bf16[1,192,1024]{2,1,0:T(8,128)(2,1)S(1)}, f32[16,384]{1,0:T(8,128)S(1)}) custom-call(s32[19]{0:T(128)S(1)} %copy-done.10, f32[4,192,1024]{2,1,0:T(8,128)} %get-tuple-element.138.refs_0_, bf16[2,384,1024]{2,1,0:T(8,128)(2,1)S(1)} %get-tuple-element.143.refs_0_.refs_1_, ...), custom_call_target="tpu_custom_call", output_to_operand_aliasing={{0}: (1, {})} | custom-call | flops 8000000000 | bytes 1048576 | tf_op jit(solution)/shard_map/pallas_call | solution.py:742
  241.4 1.6 collective-permute-start.44
  243.0 1.8 collective-permute-start.45
  244.7 1.3 shard_map.211
  246.8 1.2 collective-permute-start.49
  249.0 1.4 collective-permute-done.40.refs_2_
  250.4 1.4 collective-permute-start.51
  251.8 1.8 shard_map.208
  253.5 3.4 %collective-permute-start.46 = (bf16[72,576]{1,0:T(8,128)(2,1)S(1)}, bf16[72,576]{1,0:T(8,128)(2,1)S(1)}, u32[]{:S(2)}, u32[]{:S(2)}) collective-permute-start(bf16[72,576]{1,0:T(8,128)(2,1)S(1)} %get-tuple-element.152), channel_id=1, source_target_pairs={{0,17},{1,16},{2,19},{3,18},{4,21},{5,20},{6,23},{7,22},{8,25},{9,... | collective-permute-start | bytes 248840 | tf_op jit(solution)/shard_map/ppermute | solution.py:827
  257.6 1.8 collective-permute-start.54
  259.4 2.1 collective-permute-start.53
  261.5 1.7 collective-permute-done.46.refs_3_
  263.2 1.3 shard_map.210
  264.5 2.0 collective-permute-done.53
  (295 shorter events, 45.1 us)
Async XLA Ops:
  1.9 20.3 %collective-permute-start.1 = (bf16[72,576]{1,0:T(8,128)(2,1)S(1)}, bf16[72,576]{1,0:T(8,128)(2,1)S(1)}, u32[]{:S(2)}, u32[]{:S(2)}) collective-permute-start(bf16[72,576]{1,0:T(8,128)(2,1)S(1)} %reshape.345), channel_id=1, source_target_pairs={{0,16},{1,17},{2,18},{3,19},{4,20},{5,21},{6,22},{7,23},{8,24},{9,... | collective-permute-start | bytes 248840 | tf_op jit(solution)/shard_map/ppermute | solution.py:827
  6.0 16.2 %collective-permute-start.2 = (bf16[72,576]{1,0:T(8,128)(2,1)S(1)}, bf16[72,576]{1,0:T(8,128)(2,1)}, u32[]{:S(2)}, u32[]{:S(2)}) collective-permute-start(bf16[72,576]{1,0:T(8,128)(2,1)S(1)} %reshape.345), channel_id=1, source_target_pairs={{0,17},{1,16},{2,19},{3,18},{4,21},{5,20},{6,23},{7,22},{8,25},{9,... | collective-permute-start | bytes 248840 | tf_op jit(solution)/shard_map/ppermute | solution.py:827
  8.8 14.5 %collective-permute-start = (bf16[80,576]{1,0:T(8,128)(2,1)S(1)}, bf16[80,576]{1,0:T(8,128)(2,1)S(1)}, u32[]{:S(2)}, u32[]{:S(2)}) collective-permute-start(bf16[80,576]{1,0:T(8,128)(2,1)S(1)} %pad_maximum_fusion.9), channel_id=1, source_target_pairs={{0,1},{1,0},{2,3},{3,2},{4,5},{5,4},{6,7},{7,6},{8,9},{9,8},{10,11... | collective-permute-start | bytes 276488 | tf_op jit(solution)/shard_map/ppermute | solution.py:827
  11.3 29.5 %collective-permute-start.6 = (bf16[2,192,1024]{2,1,0:T(8,128)(2,1)}, bf16[2,192,1024]{2,1,0:T(8,128)(2,1)S(1)}, u32[]{:S(2)}, u32[]{:S(2)}) collective-permute-start(bf16[2,192,1024]{2,1,0:T(8,128)(2,1)} %constant_dynamic-slice_fusion.1), channel_id=1, source_target_pairs={{0,1},{1,0},{2,3},{3,2},{4,5},{5,4},{6,7},{7,6},{8,9},{9,8},{10,11... | collective-permute-start | bytes 2359304 | tf_op jit(solution)/shard_map/ppermute | solution.py:827
  14.9 13.3 %collective-permute-start.11 = (bf16[72,832]{1,0:T(8,128)(2,1)}, bf16[72,832]{1,0:T(8,128)(2,1)}, u32[]{:S(2)}, u32[]{:S(2)}) collective-permute-start(bf16[72,832]{1,0:T(8,128)(2,1)} %pad_maximum_fusion.8), channel_id=1, source_target_pairs={{0,16},{1,17},{2,18},{3,19},{4,20},{5,21},{6,22},{7,23},{8,24},{9,... | collective-permute-start | bytes 359432 | tf_op jit(solution)/shard_map/ppermute | solution.py:827
  23.9 15.8 %collective-permute-start.5 = (bf16[144,1152]{1,0:T(8,128)(2,1)S(1)}, bf16[144,1152]{1,0:T(8,128)(2,1)S(1)}, u32[]{:S(2)}, u32[]{:S(2)}) collective-permute-start(bf16[144,1152]{1,0:T(8,128)(2,1)S(1)} %bitcast.69), channel_id=1, source_target_pairs={{0,12},{1,13},{2,14},{3,15},{4,8},{5,9},{6,10},{7,11},{8,4},{9,5},... | collective-permute-start | bytes 995336 | tf_op jit(solution)/shard_map/ppermute | solution.py:827
  26.4 13.8 %collective-permute-start.3 = (bf16[144,1152]{1,0:T(8,128)(2,1)S(1)}, bf16[144,1152]{1,0:T(8,128)(2,1)}, u32[]{:S(2)}, u32[]{:S(2)}) collective-permute-start(bf16[144,1152]{1,0:T(8,128)(2,1)S(1)} %bitcast.70), channel_id=1, source_target_pairs={{0,8},{1,9},{2,10},{3,11},{4,12},{5,13},{6,14},{7,15},{8,0},{9,1},... | collective-permute-start | bytes 995336 | tf_op jit(solution)/shard_map/ppermute | solution.py:827
  26.9 13.4 %collective-permute-start.4 = (bf16[144,1152]{1,0:T(8,128)(2,1)S(1)}, bf16[144,1152]{1,0:T(8,128)(2,1)}, u32[]{:S(2)}, u32[]{:S(2)}) collective-permute-start(bf16[144,1152]{1,0:T(8,128)(2,1)S(1)} %bitcast.71), channel_id=1, source_target_pairs={{0,4},{1,5},{2,6},{3,7},{4,0},{5,1},{6,2},{7,3},{8,12},{9,13},{10,... | collective-permute-start | bytes 995336 | tf_op jit(solution)/shard_map/ppermute | solution.py:827
  30.0 7.7 %collective-permute-start.12 = (bf16[144,832]{1,0:T(8,128)(2,1)}, bf16[144,832]{1,0:T(8,128)(2,1)}, u32[]{:S(2)}, u32[]{:S(2)}) collective-permute-start(bf16[144,832]{1,0:T(8,128)(2,1)} %bitcast.27), channel_id=1, source_target_pairs={{0,1},{1,0},{2,3},{3,2},{4,5},{5,4},{6,7},{7,6},{8,9},{9,8},{10,11... | collective-permute-start | bytes 718856 | tf_op jit(solution)/shard_map/ppermute | solution.py:827
  39.7 13.3 %collective-permute-start.10 = (bf16[144,1152]{1,0:T(8,128)(2,1)S(1)}, bf16[144,1152]{1,0:T(8,128)(2,1)S(1)}, u32[]{:S(2)}, u32[]{:S(2)}) collective-permute-start(bf16[144,1152]{1,0:T(8,128)(2,1)S(1)} %collective-permute-done.5.refs_5_), channel_id=1, source_target_pairs={{0,2},{1,3},{2,0},{3,1},{4,6},{5,7},{6,4},{7,5},{8,10},{9,11},{10,... | collective-permute-start | bytes 995336 | tf_op jit(solution)/shard_map/ppermute | solution.py:827
  40.2 14.4 %collective-permute-start.8 = (bf16[144,1152]{1,0:T(8,128)(2,1)}, bf16[144,1152]{1,0:T(8,128)(2,1)S(1)}, u32[]{:S(2)}, u32[]{:S(2)}) collective-permute-start(bf16[144,1152]{1,0:T(8,128)(2,1)} %collective-permute-done.3.refs_3_), channel_id=1, source_target_pairs={{0,2},{1,3},{2,0},{3,1},{4,6},{5,7},{6,4},{7,5},{8,10},{9,11},{10,... | collective-permute-start | bytes 995336 | tf_op jit(solution)/shard_map/ppermute | solution.py:827
  40.3 14.4 %collective-permute-start.9 = (bf16[144,1152]{1,0:T(8,128)(2,1)}, bf16[144,1152]{1,0:T(8,128)(2,1)S(1)}, u32[]{:S(2)}, u32[]{:S(2)}) collective-permute-start(bf16[144,1152]{1,0:T(8,128)(2,1)} %collective-permute-done.4.refs_4_), channel_id=1, source_target_pairs={{0,2},{1,3},{2,0},{3,1},{4,6},{5,7},{6,4},{7,5},{8,10},{9,11},{10,... | collective-permute-start | bytes 995336 | tf_op jit(solution)/shard_map/ppermute | solution.py:827
  40.8 14.5 %collective-permute-start.7 = (bf16[144,1152]{1,0:T(8,128)(2,1)S(1)}, bf16[144,1152]{1,0:T(8,128)(2,1)S(1)}, u32[]{:S(2)}, u32[]{:S(2)}) collective-permute-start(bf16[144,1152]{1,0:T(8,128)(2,1)S(1)} %bitcast.72), channel_id=1, source_target_pairs={{0,2},{1,3},{2,0},{3,1},{4,6},{5,7},{6,4},{7,5},{8,10},{9,11},{10,... | collective-permute-start | bytes 995336 | tf_op jit(solution)/shard_map/ppermute | solution.py:827
  40.8 9.0 %collective-permute-start.13 = (bf16[24,768]{1,0:T(8,128)(2,1)}, bf16[24,768]{1,0:T(8,128)(2,1)S(1)}, u32[]{:S(2)}, u32[]{:S(2)}) collective-permute-start(bf16[24,768]{1,0:T(8,128)(2,1)} %pad_maximum_fusion.11), channel_id=1, source_target_pairs={{0,16},{1,17},{2,18},{3,19},{4,20},{5,21},{6,22},{7,23},{8,24},{9,... | collective-permute-start | bytes 110600 | tf_op jit(solution)/shard_map/ppermute | solution.py:827
  49.9 21.3 %collective-permute-start.15 = (bf16[144,1664]{1,0:T(8,128)(2,1)}, bf16[144,1664]{1,0:T(8,128)(2,1)S(1)}, u32[]{:S(2)}, u32[]{:S(2)}) collective-permute-start(bf16[144,1664]{1,0:T(8,128)(2,1)} %pad_maximum_fusion.refs_6_), channel_id=1, source_target_pairs={{0,8},{1,9},{2,10},{3,11},{4,12},{5,13},{6,14},{7,15},{8,0},{9,1},... | collective-permute-start | bytes 1437704 | tf_op jit(solution)/shard_map/ppermute | solution.py:827
  53.1 23.0 %collective-permute-start.16 = (bf16[144,1664]{1,0:T(8,128)(2,1)}, bf16[144,1664]{1,0:T(8,128)(2,1)}, u32[]{:S(2)}, u32[]{:S(2)}) collective-permute-start(bf16[144,1664]{1,0:T(8,128)(2,1)} %pad_maximum_fusion.refs_6_), channel_id=1, source_target_pairs={{0,4},{1,5},{2,6},{3,7},{4,0},{5,1},{6,2},{7,3},{8,12},{9,13},{10,... | collective-permute-start | bytes 1437704 | tf_op jit(solution)/shard_map/ppermute | solution.py:827
  54.7 21.4 %collective-permute-start.17 = (bf16[144,1664]{1,0:T(8,128)(2,1)}, bf16[144,1664]{1,0:T(8,128)(2,1)}, u32[]{:S(2)}, u32[]{:S(2)}) collective-permute-start(bf16[144,1664]{1,0:T(8,128)(2,1)} %pad_maximum_fusion.refs_6_), channel_id=1, source_target_pairs={{0,12},{1,13},{2,14},{3,15},{4,8},{5,9},{6,10},{7,11},{8,4},{9,5},... | collective-permute-start | bytes 1437704 | tf_op jit(solution)/shard_map/ppermute | solution.py:827
  54.7 25.0 %collective-permute-start.14 = (bf16[48,768]{1,0:T(8,128)(2,1)S(1)}, bf16[48,768]{1,0:T(8,128)(2,1)S(1)}, u32[]{:S(2)}, u32[]{:S(2)}) collective-permute-start(bf16[48,768]{1,0:T(8,128)(2,1)S(1)} %bitcast.82), channel_id=1, source_target_pairs={{0,1},{1,0},{2,3},{3,2},{4,5},{5,4},{6,7},{7,6},{8,9},{9,8},{10,11... | collective-permute-start | bytes 221192 | tf_op jit(solution)/shard_map/ppermute | solution.py:827
  76.1 4.8 %collective-permute-start.18 = (bf16[144,1664]{1,0:T(8,128)(2,1)}, bf16[144,1664]{1,0:T(8,128)(2,1)S(1)}, u32[]{:S(2)}, u32[]{:S(2)}) collective-permute-start(bf16[144,1664]{1,0:T(8,128)(2,1)} %pad_maximum_fusion.refs_6_), channel_id=1, source_target_pairs={{0,2},{1,3},{2,0},{3,1},{4,6},{5,7},{6,4},{7,5},{8,10},{9,11},{10,... | collective-permute-start | bytes 1437704 | tf_op jit(solution)/shard_map/ppermute | solution.py:827
  76.1 5.5 %collective-permute-start.19 = (bf16[144,1664]{1,0:T(8,128)(2,1)S(1)}, bf16[144,1664]{1,0:T(8,128)(2,1)}, u32[]{:S(2)}, u32[]{:S(2)}) collective-permute-start(bf16[144,1664]{1,0:T(8,128)(2,1)S(1)} %collective-permute-done.15.refs_7_), channel_id=1, source_target_pairs={{0,2},{1,3},{2,0},{3,1},{4,6},{5,7},{6,4},{7,5},{8,10},{9,11},{10,... | collective-permute-start | bytes 1437704 | tf_op jit(solution)/shard_map/ppermute | solution.py:827
  76.6 6.7 %collective-permute-start.20 = (bf16[144,1664]{1,0:T(8,128)(2,1)}, bf16[144,1664]{1,0:T(8,128)(2,1)}, u32[]{:S(2)}, u32[]{:S(2)}) collective-permute-start(bf16[144,1664]{1,0:T(8,128)(2,1)} %collective-permute-done.16.refs_8_), channel_id=1, source_target_pairs={{0,2},{1,3},{2,0},{3,1},{4,6},{5,7},{6,4},{7,5},{8,10},{9,11},{10,... | collective-permute-start | bytes 1437704 | tf_op jit(solution)/shard_map/ppermute | solution.py:827
  76.6 7.2 %collective-permute-start.21 = (bf16[144,1664]{1,0:T(8,128)(2,1)}, bf16[144,1664]{1,0:T(8,128)(2,1)}, u32[]{:S(2)}, u32[]{:S(2)}) collective-permute-start(bf16[144,1664]{1,0:T(8,128)(2,1)} %collective-permute-done.17.refs_9_), channel_id=1, source_target_pairs={{0,2},{1,3},{2,0},{3,1},{4,6},{5,7},{6,4},{7,5},{8,10},{9,11},{10,... | collective-permute-start | bytes 1437704 | tf_op jit(solution)/shard_map/ppermute | solution.py:827
  79.7 24.1 %collective-permute-start.23 = (bf16[48,1536]{1,0:T(8,128)(2,1)S(1)}, bf16[48,1536]{1,0:T(8,128)(2,1)S(1)}, u32[]{:S(2)}, u32[]{:S(2)}) collective-permute-start(bf16[48,1536]{1,0:T(8,128)(2,1)S(1)} %pad_maximum_fusion.6.refs_8_), channel_id=1, source_target_pairs={{0,8},{1,9},{2,10},{3,11},{4,12},{5,13},{6,14},{7,15},{8,0},{9,1},... | collective-permute-start | bytes 442376 | tf_op jit(solution)/shard_map/ppermute | solution.py:827
  80.9 22.9 %collective-permute-start.24 = (bf16[48,1536]{1,0:T(8,128)(2,1)S(1)}, bf16[48,1536]{1,0:T(8,128)(2,1)S(1)}, u32[]{:S(2)}, u32[]{:S(2)}) collective-permute-start(bf16[48,1536]{1,0:T(8,128)(2,1)S(1)} %pad_maximum_fusion.6.refs_8_), channel_id=1, source_target_pairs={{0,4},{1,5},{2,6},{3,7},{4,0},{5,1},{6,2},{7,3},{8,12},{9,13},{10,... | collective-permute-start | bytes 442376 | tf_op jit(solution)/shard_map/ppermute | solution.py:827
  81.6 22.2 %collective-permute-start.25 = (bf16[48,1536]{1,0:T(8,128)(2,1)S(1)}, bf16[48,1536]{1,0:T(8,128)(2,1)S(1)}, u32[]{:S(2)}, u32[]{:S(2)}) collective-permute-start(bf16[48,1536]{1,0:T(8,128)(2,1)S(1)} %pad_maximum_fusion.6.refs_8_), channel_id=1, source_target_pairs={{0,12},{1,13},{2,14},{3,15},{4,8},{5,9},{6,10},{7,11},{8,4},{9,5},... | collective-permute-start | bytes 442376 | tf_op jit(solution)/shard_map/ppermute | solution.py:827
  83.3 22.8 %collective-permute-start.22 = (bf16[2,192,1024]{2,1,0:T(8,128)(2,1)S(1)}, bf16[2,192,1024]{2,1,0:T(8,128)(2,1)S(1)}, u32[]{:S(2)}, u32[]{:S(2)}) collective-permute-start(bf16[2,192,1024]{2,1,0:T(8,128)(2,1)S(1)} %copy-done.31), channel_id=1, source_target_pairs={{0,1},{1,0},{2,3},{3,2},{4,5},{5,4},{6,7},{7,6},{8,9},{9,8},{10,11... | collective-permute-start | bytes 2359304 | tf_op jit(solution)/shard_map/ppermute | solution.py:827
  105.3 73.8 %collective-permute-start.31 = (bf16[576,2048]{1,0:T(8,128)(2,1)}, bf16[576,2048]{1,0:T(8,128)(2,1)}, u32[]{:S(2)}, u32[]{:S(2)}) collective-permute-start(bf16[576,2048]{1,0:T(8,128)(2,1)} %get-tuple-element.111), channel_id=1, source_target_pairs={{0,2},{1,3},{2,0},{3,1},{4,6},{5,7},{6,4},{7,5},{8,10},{9,11},{10,... | collective-permute-start | bytes 7077896 | tf_op jit(solution)/shard_map/ppermute | solution.py:827
  174.6 4.5 %collective-permute-start.30 = (bf16[2,384,1024]{2,1,0:T(8,128)(2,1)}, bf16[2,384,1024]{2,1,0:T(8,128)(2,1)S(1)}, u32[]{:S(2)}, u32[]{:S(2)}) collective-permute-start(bf16[2,384,1024]{2,1,0:T(8,128)(2,1)} %get-tuple-element.120.refs_0_), channel_id=1, source_target_pairs={{0,2},{1,3},{2,0},{3,1},{4,6},{5,7},{6,4},{7,5},{8,10},{9,11},{10,... | collective-permute-start | bytes 4718600 | tf_op jit(solution)/shard_map/ppermute | solution.py:827
  175.3 32.3 %collective-permute-start.33 = (bf16[2,192,1024]{2,1,0:T(8,128)(2,1)}, bf16[2,192,1024]{2,1,0:T(8,128)(2,1)S(1)}, u32[]{:S(2)}, u32[]{:S(2)}) collective-permute-start(bf16[2,192,1024]{2,1,0:T(8,128)(2,1)} %get-tuple-element.119), channel_id=1, source_target_pairs={{0,1},{1,0},{2,3},{3,2},{4,5},{5,4},{6,7},{7,6},{8,9},{9,8},{10,11... | collective-permute-start | bytes 2359304 | tf_op jit(solution)/shard_map/ppermute | solution.py:827
  192.6 23.2 %collective-permute-start.35 = (bf16[208,1152]{1,0:T(8,128)(2,1)S(1)}, bf16[208,1152]{1,0:T(8,128)(2,1)S(1)}, u32[]{:S(2)}, u32[]{:S(2)}) collective-permute-start(bf16[208,1152]{1,0:T(8,128)(2,1)S(1)} %get-tuple-element.115), channel_id=1, source_target_pairs={{0,8},{1,9},{2,10},{3,11},{4,12},{5,13},{6,14},{7,15},{8,0},{9,1},... | collective-permute-start | bytes 1437704 | tf_op jit(solution)/shard_map/ppermute | solution.py:827
  193.8 22.0 %collective-permute-start.36 = (bf16[208,1152]{1,0:T(8,128)(2,1)S(1)}, bf16[208,1152]{1,0:T(8,128)(2,1)S(1)}, u32[]{:S(2)}, u32[]{:S(2)}) collective-permute-start(bf16[208,1152]{1,0:T(8,128)(2,1)S(1)} %get-tuple-element.116), channel_id=1, source_target_pairs={{0,4},{1,5},{2,6},{3,7},{4,0},{5,1},{6,2},{7,3},{8,12},{9,13},{10,... | collective-permute-start | bytes 1437704 | tf_op jit(solution)/shard_map/ppermute | solution.py:827
  194.5 22.6 %collective-permute-start.37 = (bf16[208,1152]{1,0:T(8,128)(2,1)S(1)}, bf16[208,1152]{1,0:T(8,128)(2,1)S(1)}, u32[]{:S(2)}, u32[]{:S(2)}) collective-permute-start(bf16[208,1152]{1,0:T(8,128)(2,1)S(1)} %get-tuple-element.117), channel_id=1, source_target_pairs={{0,12},{1,13},{2,14},{3,15},{4,8},{5,9},{6,10},{7,11},{8,4},{9,5},... | collective-permute-start | bytes 1437704 | tf_op jit(solution)/shard_map/ppermute | solution.py:827
  218.1 12.5 %collective-permute-start.38 = (bf16[208,576]{1,0:T(8,128)(2,1)S(1)}, bf16[208,576]{1,0:T(8,128)(2,1)S(1)}, u32[]{:S(2)}, u32[]{:S(2)}) collective-permute-start(bf16[208,576]{1,0:T(8,128)(2,1)S(1)} %get-tuple-element.133), channel_id=1, source_target_pairs={{0,1},{1,0},{2,3},{3,2},{4,5},{5,4},{6,7},{7,6},{8,9},{9,8},{10,11... | collective-permute-start | bytes 718856 | tf_op jit(solution)/shard_map/ppermute | solution.py:827
  220.4 18.8 %collective-permute-start.41 = (bf16[144,1152]{1,0:T(8,128)(2,1)S(1)}, bf16[144,1152]{1,0:T(8,128)(2,1)S(1)}, u32[]{:S(2)}, u32[]{:S(2)}) collective-permute-start(bf16[144,1152]{1,0:T(8,128)(2,1)S(1)} %get-tuple-element.128), channel_id=1, source_target_pairs={{0,8},{1,9},{2,10},{3,11},{4,12},{5,13},{6,14},{7,15},{8,0},{9,1},... | collective-permute-start | bytes 995336 | tf_op jit(solution)/shard_map/ppermute | solution.py:827
  221.3 19.1 %collective-permute-start.42 = (bf16[144,1152]{1,0:T(8,128)(2,1)S(1)}, bf16[144,1152]{1,0:T(8,128)(2,1)S(1)}, u32[]{:S(2)}, u32[]{:S(2)}) collective-permute-start(bf16[144,1152]{1,0:T(8,128)(2,1)S(1)} %get-tuple-element.129), channel_id=1, source_target_pairs={{0,4},{1,5},{2,6},{3,7},{4,0},{5,1},{6,2},{7,3},{8,12},{9,13},{10,... | collective-permute-start | bytes 995336 | tf_op jit(solution)/shard_map/ppermute | solution.py:827
  222.8 17.7 %collective-permute-start.43 = (bf16[144,1152]{1,0:T(8,128)(2,1)S(1)}, bf16[144,1152]{1,0:T(8,128)(2,1)S(1)}, u32[]{:S(2)}, u32[]{:S(2)}) collective-permute-start(bf16[144,1152]{1,0:T(8,128)(2,1)S(1)} %get-tuple-element.130), channel_id=1, source_target_pairs={{0,12},{1,13},{2,14},{3,15},{4,8},{5,9},{6,10},{7,11},{8,4},{9,5},... | collective-permute-start | bytes 995336 | tf_op jit(solution)/shard_map/ppermute | solution.py:827
  231.2 13.5 %collective-permute-start.47 = (bf16[104,576]{1,0:T(8,128)(2,1)S(1)}, bf16[104,576]{1,0:T(8,128)(2,1)S(1)}, u32[]{:S(2)}, u32[]{:S(2)}) collective-permute-start(bf16[104,576]{1,0:T(8,128)(2,1)S(1)} %get-tuple-element.142), channel_id=1, source_target_pairs={{0,16},{1,17},{2,18},{3,19},{4,20},{5,21},{6,22},{7,23},{8,24},{9,... | collective-permute-start | bytes 359432 | tf_op jit(solution)/shard_map/ppermute | solution.py:827
  231.6 13.2 %collective-permute-start.39 = (bf16[1,192,1024]{2,1,0:T(8,128)(2,1)S(1)}, bf16[1,192,1024]{2,1,0:T(8,128)(2,1)S(1)}, u32[]{:S(2)}, u32[]{:S(2)}) collective-permute-start(bf16[1,192,1024]{2,1,0:T(8,128)(2,1)S(1)} %get-tuple-element.147), channel_id=1, source_target_pairs={{0,1},{1,0},{2,3},{3,2},{4,5},{5,4},{6,7},{7,6},{8,9},{9,8},{10,11... | collective-permute-start | bytes 1179656 | tf_op jit(solution)/shard_map/ppermute | solution.py:827
  239.3 11.1 %collective-permute-start.40 = (bf16[1,192,1024]{2,1,0:T(8,128)(2,1)S(1)}, bf16[1,192,1024]{2,1,0:T(8,128)(2,1)S(1)}, u32[]{:S(2)}, u32[]{:S(2)}) collective-permute-start(bf16[1,192,1024]{2,1,0:T(8,128)(2,1)S(1)} %get-tuple-element.148), channel_id=1, source_target_pairs={{0,1},{1,0},{2,3},{3,2},{4,5},{5,4},{6,7},{7,6},{8,9},{9,8},{10,11... | collective-permute-start | bytes 1179656 | tf_op jit(solution)/shard_map/ppermute | solution.py:827
  241.4 18.0 %collective-permute-start.44 = (bf16[72,576]{1,0:T(8,128)(2,1)S(1)}, bf16[72,576]{1,0:T(8,128)(2,1)S(1)}, u32[]{:S(2)}, u32[]{:S(2)}) collective-permute-start(bf16[72,576]{1,0:T(8,128)(2,1)S(1)} %get-tuple-element.150), channel_id=1, source_target_pairs={{0,1},{1,0},{2,3},{3,2},{4,5},{5,4},{6,7},{7,6},{8,9},{9,8},{10,11... | collective-permute-start | bytes 248840 | tf_op jit(solution)/shard_map/ppermute | solution.py:827
  243.0 18.6 %collective-permute-start.45 = (bf16[72,576]{1,0:T(8,128)(2,1)S(1)}, bf16[72,576]{1,0:T(8,128)(2,1)S(1)}, u32[]{:S(2)}, u32[]{:S(2)}) collective-permute-start(bf16[72,576]{1,0:T(8,128)(2,1)S(1)} %get-tuple-element.151), channel_id=1, source_target_pairs={{0,16},{1,17},{2,18},{3,19},{4,20},{5,21},{6,22},{7,23},{8,24},{9,... | collective-permute-start | bytes 248840 | tf_op jit(solution)/shard_map/ppermute | solution.py:827
  246.8 6.7 %collective-permute-start.49 = (f32[24,384]{1,0:T(8,128)S(1)}, f32[24,384]{1,0:T(8,128)S(1)}, u32[]{:S(2)}, u32[]{:S(2)}) collective-permute-start(f32[24,384]{1,0:T(8,128)S(1)} %pad_maximum_fusion.12), channel_id=1, source_target_pairs={{0,8},{1,9},{2,10},{3,11},{4,12},{5,13},{6,14},{7,15},{8,0},{9,1},... | collective-permute-start | bytes 110600 | tf_op jit(solution)/shard_map/ppermute | solution.py:827
  248.0 8.9 %collective-permute-start.50 = (f32[24,384]{1,0:T(8,128)S(1)}, f32[24,384]{1,0:T(8,128)S(1)}, u32[]{:S(2)}, u32[]{:S(2)}) collective-permute-start(f32[24,384]{1,0:T(8,128)S(1)} %pad_maximum_fusion.12), channel_id=1, source_target_pairs={{0,4},{1,5},{2,6},{3,7},{4,0},{5,1},{6,2},{7,3},{8,12},{9,13},{10,... | collective-permute-start | bytes 110600 | tf_op jit(solution)/shard_map/ppermute | solution.py:827
  250.4 6.5 %collective-permute-start.51 = (f32[24,384]{1,0:T(8,128)S(1)}, f32[24,384]{1,0:T(8,128)S(1)}, u32[]{:S(2)}, u32[]{:S(2)}) collective-permute-start(f32[24,384]{1,0:T(8,128)S(1)} %pad_maximum_fusion.12), channel_id=1, source_target_pairs={{0,12},{1,13},{2,14},{3,15},{4,8},{5,9},{6,10},{7,11},{8,4},{9,5},... | collective-permute-start | bytes 110600 | tf_op jit(solution)/shard_map/ppermute | solution.py:827
  253.5 9.7 %collective-permute-start.46 = (bf16[72,576]{1,0:T(8,128)(2,1)S(1)}, bf16[72,576]{1,0:T(8,128)(2,1)S(1)}, u32[]{:S(2)}, u32[]{:S(2)}) collective-permute-start(bf16[72,576]{1,0:T(8,128)(2,1)S(1)} %get-tuple-element.152), channel_id=1, source_target_pairs={{0,17},{1,16},{2,19},{3,18},{4,21},{5,20},{6,23},{7,22},{8,25},{9,... | collective-permute-start | bytes 248840 | tf_op jit(solution)/shard_map/ppermute | solution.py:827
  257.1 7.5 %collective-permute-start.52 = (f32[72,192]{1,0:T(8,128)S(1)}, f32[72,192]{1,0:T(8,128)S(1)}, u32[]{:S(2)}, u32[]{:S(2)}) collective-permute-start(f32[72,192]{1,0:T(8,128)S(1)} %get-tuple-element.213), channel_id=1, source_target_pairs={{0,1},{1,0},{2,3},{3,2},{4,5},{5,4},{6,7},{7,6},{8,9},{9,8},{10,11... | collective-permute-start | bytes 165896 | tf_op jit(solution)/shard_map/ppermute | solution.py:827
  257.6 8.9 %collective-permute-start.54 = (f32[72,192]{1,0:T(8,128)S(1)}, f32[72,192]{1,0:T(8,128)S(1)}, u32[]{:S(2)}, u32[]{:S(2)}) collective-permute-start(f32[72,192]{1,0:T(8,128)S(1)} %get-tuple-element.213), channel_id=1, source_target_pairs={{0,17},{1,16},{2,19},{3,18},{4,21},{5,20},{6,23},{7,22},{8,25},{9,... | collective-permute-start | bytes 165896 | tf_op jit(solution)/shard_map/ppermute | solution.py:827
  259.4 7.1 %collective-permute-start.53 = (f32[72,192]{1,0:T(8,128)S(1)}, f32[72,192]{1,0:T(8,128)S(1)}, u32[]{:S(2)}, u32[]{:S(2)}) collective-permute-start(f32[72,192]{1,0:T(8,128)S(1)} %get-tuple-element.212), channel_id=1, source_target_pairs={{0,16},{1,17},{2,18},{3,19},{4,20},{5,21},{6,22},{7,23},{8,24},{9,... | collective-permute-start | bytes 165896 | tf_op jit(solution)/shard_map/ppermute | solution.py:827
  (69 other events, 657.5 us)
where the time goes:
time: 272 us; the launch traced here: 269 us
  Pallas kernels  153 us (56%)
  starting transfers between devices  55.6 us (20%)
  local copies, waits for them, and re-layouts  25.3 us (9%)
  waiting for transfers between devices  20.3 us (7%)
  other arithmetic  11.2 us (4%)
    pallas_call x16, Pallas kernels, run(): pl.pallas_call(body, grid_spec=pltpu.PrefetchScalarGridSpec(num_scalar_pr...  153 us
    ppermute x55, starting transfers between devices, swap(): return lax.ppermute(value, ('dp', 'chan'), pairs)  55.6 us
    ppermute x55, waiting for transfers between devices, swap(): return lax.ppermute(value, ('dp', 'chan'), pairs)  20.3 us
    unnamed x128, local copies, waits for them, and re-layouts  13.7 us
  transfers between devices with their start and end apart: 55, of which 13 were waited for; matrix products, arithmetic and copies ran while one was open for 8% of the time, Pallas kernels for 57%

commit v1 on v0

--- a/solution.py
+++ b/solution.py
@@ -21,6 +21,7 @@
 EPSILON = 1e-05
 SECOND = 3 * HALF + 256
 MIXED = 4 * HALF
+PACKED = MIXED // 3
 PAIR = 2 * ROWS
 PIECE = 3 * PAIR
 JOINT = PIECE + PAIR + PAIR // 3
@@ -128,16 +129,22 @@
     )
 
 
-def build_stack(place, value, mask, stacks):
+def side_shifts(piece, out, base):
     not_left = pixel_row(lambda pixel: pixel % SIDE != 0)
     not_right = pixel_row(lambda pixel: pixel % SIDE != SIDE - 1)
+    rows = piece.shape[0]
+    out[base : base + rows, :] = pltpu.roll(piece, 1, 1) * not_left
+    out[base + rows : base + 2 * rows, :] = piece
+    out[base + 2 * rows : base + 3 * rows, :] = pltpu.roll(piece, PIX - 1, 1) * not_right
+
+
+def build_stack(place, value, mask, stacks, inputs=None):
     for pair in range(PAIRS):
         piece = (silu(pair_rows(place, value, pair)) * mask).astype(LOW)
-        stack = stacks[pair // (PAIRS // 2)]
-        base = pair % (PAIRS // 2) * PIECE
-        stack[base : base + PAIR, :] = pltpu.roll(piece, 1, 1) * not_left
-        stack[base + PAIR : base + 2 * PAIR, :] = piece
-        stack[base + 2 * PAIR : base + 3 * PAIR, :] = pltpu.roll(piece, PIX - 1, 1) * not_right
+        half, at = pair // (PAIRS // 2), pair % (PAIRS // 2)
+        side_shifts(piece, stacks[half], at * PIECE)
+        if inputs is not None:
+            inputs[half][at * PAIR : (at + 1) * PAIR, :] = piece
 
 
 def back_to_channels(place_ref, product_ref, out_ref):
@@ -206,7 +213,7 @@
                 weight[rows, chan * 3 * HALF : (chan + 1) * 3 * HALF] = source[
                     :, base : base + 3 * HALF
                 ]
-                for part in range(2):
+                for part in range(0 if weight_e is None else 2):
                     lane = base + 3 * HALF + part * 128
                     weight_e[chan, part, rows, :] = source[:, lane : lane + 128]
 
@@ -280,20 +287,25 @@
     low_out,
     high_out,
     residual_out,
-    attend_out,
     stats_out,
     weight,
     weight_e,
     value,
+    stack,
     product,
 ):
     load_second(weight, weight_e, pieces)
     mask = mask_ref[0]
     count = count_of(mask)
+    image = pl.program_id(0)
+
+    def own_columns(sums):
+        return jnp.where(image == 0, sums[:, :6], sums[:, 6:12])
+
     scales, shifts = [], []
     for chan in range(2):
-        low = dot(weight_e[chan, 0], embed_in[0, 0], TN)
-        high = dot(weight_e[chan, 1], embed_in[0, 1], TN)
+        low = own_columns(dot(weight_e[chan, 0], embed_in[0], TN))
+        high = own_columns(dot(weight_e[chan, 1], embed_in[1], TN))
         column = jnp.concatenate(
             [
                 low[:, 0:1] + low[:, 1:2] + low[:, 2:3],
@@ -308,22 +320,20 @@
     time_shift = jnp.concatenate(shifts, axis=0)
     affine = normed[0] * params[:, 2:3] + params[:, 3:4]
     value[...] = affine * (1.0 + time_scale) + time_shift
-    stacks = (low_out, high_out)
-    build_stack(place, value, mask, stacks)
-    product[...] = dot(weight[...], both_rows(stacks), TN)
+    middle = TAPS // 2
+    stacks = (stack.at[:middle, :], stack.at[middle:, :])
+    build_stack(place, value, mask, stacks, (low_out, high_out))
+    product[...] = dot(weight[...], stack[...], TN)
     for chan in range(2):
         rows = slice(chan * HALF, (chan + 1) * HALF)
         value[rows, :] = whole[0, rows, :].astype(WIDE) + conv_out(product, chan)
     residual_out[0] = value[...]
     mean, factor = group_stats(value, member[...], mask, count)
-    scale = factor * params[:, 4:5]
-    attend_out[0] = ((value[...] - mean) * scale + params[:, 5:6]).astype(LOW)
     stats_out[0] = small_columns((mean, factor, time_scale, time_shift))
 
 
 def attend_kernel(
     place,
-    attend_in,
     residual,
     stats,
     mine,
@@ -334,12 +344,12 @@
     bundle,
     block_out,
     send_out,
-    residual_grad_out,
     second_grad_out,
     mixed_keep,
     mixed_send,
     small_out,
     weight_f,
+    attend_in,
     project,
     output,
     gradient,
@@ -364,11 +374,15 @@
     def _():
         for chan in range(2):
             for pair in range(PAIRS):
-                block = bundle[pair][:, chan * MIXED : (chan + 1) * MIXED].astype(WIDE)
+                block = bundle[pair][:, chan * PACKED : (chan + 1) * PACKED].astype(WIDE)
                 for part in range(2):
-                    weight_f[chan, pl.ds(block_offset(place, 2 * pair + part), ROWS), :] = block[
-                        part * ROWS : (part + 1) * ROWS
-                    ]
+                    for third in range(3):
+                        first = third * PAIR + part * ROWS
+                        weight_f[
+                            chan,
+                            pl.ds(block_offset(place, 2 * pair + part), ROWS),
+                            third * PACKED : (third + 1) * PACKED,
+                        ] = block[first : first + ROWS]
         project[...] = jnp.concatenate(
             [weight_f[0, :, : 3 * HALF], weight_f[1, :, : 3 * HALF]], axis=1
         ).astype(LOW)
@@ -382,7 +396,10 @@
     count = count_of(mask)
     gradient[pl.ds(own, HALF), :] = (mine[0].astype(WIDE) * mask).astype(LOW)
     gradient[pl.ds(other, HALF), :] = (theirs[0].astype(WIDE) * mask).astype(LOW)
-    projected[...] = dot(project[...], attend_in[0], TN).astype(LOW)
+    mean, factor = stats[0, :, 0:1], stats[0, :, 1:2]
+    scale = factor * params[:, 4:5]
+    attend_in[...] = ((residual[0] - mean) * scale + params[:, 5:6]).astype(LOW)
+    projected[...] = dot(project[...], attend_in[...], TN).astype(LOW)
     attend_grad[...] = dot(output[...], gradient[...], TN).astype(LOW)
 
     penalty = mask - 1.0
@@ -442,15 +459,14 @@
         )
         return carry
 
-    lax.fori_loop(0, C // HEAD, one_head, 0)
+    lax.fori_loop(0, C // HEAD, one_head, 0, unroll=3)
 
     value[...] = (residual[0] + dot(output[...], attended[...], NN)) * mask
     block_out[0] = value[pl.ds(own, HALF), :].astype(LOW)
     send_out[0] = value[pl.ds(other, HALF), :].astype(LOW)
     accumulated[:, TAPS:] += dot(gradient[...], attended[...], NT)
-    accumulated[:, :TAPS] += dot(attend_in[0], projected_grad[...], NT)
+    accumulated[:, :TAPS] += dot(attend_in[...], projected_grad[...], NT)
     third = dot(project[...], projected_grad[...], NN)
-    mean, factor = stats[0, :, 0:1], stats[0, :, 1:2]
     normed = (residual[0] - mean) * factor
     bias_third = jnp.sum(third, axis=1, keepdims=True)
     gain_third = jnp.sum(third * normed, axis=1, keepdims=True)
@@ -460,7 +476,6 @@
     total = gradient[...].astype(WIDE) + factor * (
         third * gain - mask * (first_sum + normed * second_sum)
     )
-    residual_grad_out[0] = total
     second_grad_out[0] = total.astype(LOW)
     small_out[0] = small_rows((gain_third, bias_third))
 
@@ -478,11 +493,25 @@
             ).astype(out.dtype)
 
 
-def filter_kernel(place, grads, stacks, mixed, *refs):
-    outs, grad_stack = refs[:-1], refs[-1]
-    stack_gradients(grads, grad_stack)
-    both = jnp.concatenate([stack[...] for stack in stacks], axis=1)
-    total = dot(both, grad_stack[...], NT)
+def side_stack(inputs, stack):
+    for image in range(inputs.shape[1] // PIX):
+        columns = slice(image * PIX, (image + 1) * PIX)
+        for pair in range(PAIRS // 2):
+            piece = inputs[pair * PAIR : (pair + 1) * PAIR, columns]
+            side_shifts(piece, stack.at[:, columns], pair * PIECE)
+
+
+def one_core_kernel(place, grads, inputs, total_out, grad_stack, stack):
+    stack_gradients([grads], grad_stack)
+    side_stack(inputs, stack)
+    total_out[...] = dot(stack[...], grad_stack[...], NT)
+
+
+def both_cores_kernel(place, grads, inputs, partial, mixed, *refs):
+    outs, grad_stack, stack = refs[:-2], refs[-2], refs[-1]
+    stack_gradients([grads], grad_stack)
+    side_stack(inputs, stack)
+    total = partial[...] + dot(stack[...], grad_stack[...], NT)
     extra = JOINT - PIECE
     for part, out in enumerate(outs):
         rows = slice(part * extra, (part + 1) * extra)
@@ -511,7 +540,7 @@
 def second_back_kernel(
     place,
     grads,
-    weight,
+    pieces,
     normed_ref,
     stats_first,
     stats,
@@ -520,10 +549,12 @@
     member,
     first_grad_out,
     small_out,
+    weight,
     grad_stack,
     product,
     value,
 ):
+    load_second(weight, None, pieces)
     conv_back(place, grads, weight, grad_stack, product, value)
     mask = mask_ref[0]
     count = count_of(mask)
@@ -584,7 +615,7 @@
     weighted = jnp.sum(delta * normed, axis=1, keepdims=True)
     sums = group_sums(member[...], lane_pair(gain * plain, gain * weighted))
     first_sum, second_sum = sums[:, 0:1] / count, sums[:, 1:2] / count
-    value[...] = residual_grad[0] + factor * (
+    value[...] = residual_grad[0].astype(WIDE) + factor * (
         value[...] * gain - mask * (first_sum + normed * second_sum)
     )
     keep_out[0] = value[pl.ds(own, HALF), :]
@@ -757,18 +788,32 @@
     )(place, *arrays)
 
 
-def filter_gradient(place, stacks, grads, mixed):
-    images = sum(grad.shape[0] for grad in grads)
-    ins = (grads, stacks, mixed)
+def filter_gradient(place, inputs, grads, mixed):
+    scratch = [
+        pltpu.VMEM((TAPS, grads[0].shape[0] * PIX), LOW),
+        pltpu.VMEM((TAPS // 2, grads[0].shape[0] * PIX), LOW),
+    ]
+    partial = shape(TAPS // 2, TAPS)
+    ins = (grads[0], inputs[0])
+    (partial,) = run(
+        one_core_kernel,
+        place,
+        1,
+        [(entry, jax.tree.map(whole_array, entry)) for entry in ins],
+        [(partial, whole_array(partial))],
+        scratch,
+        room=24,
+    )
+    ins = (grads[1], inputs[1], partial, mixed)
     outs = [shape(JOINT, TAPS)] + [shape(JOINT, TAPS, dtype=LOW)] * 3
     return run(
-        filter_kernel,
+        both_cores_kernel,
         place,
         1,
         [(entry, jax.tree.map(whole_array, entry)) for entry in ins],
         [(out, whole_array(out)) for out in outs],
-        [pltpu.VMEM((TAPS, images * PIX), LOW)],
-        room=40,
+        scratch,
+        room=32,
     )
 
 
@@ -855,7 +900,7 @@
 
     def gather_slow(shard, late):
         rows = after(pair_up(shard, swap(shard, 8, 0)), late)
-        return halves(rows, swap(rows, 0, 1), 1)
+        return rows, swap(rows, 0, 1)
 
     def gather_two(rows):
         return [rows, swap(rows, 4, 0), swap(rows, 2, 0), swap(rows, 6, 0)]
@@ -930,9 +975,6 @@
     embed_rows = jnp.transpose(near(embed_weight.astype(LOW), 1), (1, 0, 2))
     embed_rows = jnp.transpose(embed_rows.reshape(PAIR, 3, 128), (1, 0, 2))
     embed_rows = embed_rows.reshape(2, 3 * ROWS, 128)
-    second_rows = jnp.concatenate(
-        [filter_rows(second_filter), embed_rows[0], embed_rows[1]], axis=1
-    )
     bundle_rows = jnp.concatenate(
         [
             near(project_weight.astype(LOW), 0).reshape(ROWS, 3 * HALF),
@@ -940,12 +982,17 @@
         ],
         axis=1,
     )
+    bundle_rows = jnp.transpose(bundle_rows.reshape(ROWS, 3, PACKED), (1, 0, 2))
+    second_rows = jnp.concatenate(
+        [
+            filter_rows(second_filter),
+            embed_rows[0],
+            embed_rows[1],
+            bundle_rows.reshape(3 * ROWS, PACKED),
+        ],
+        axis=1,
+    )
     second_one = gather_slow(second_rows, first_one)
-    bundle_one = gather_slow(after(bundle_rows, theirs), second_one)
-    first_pieces = first_pieces + gather_three(
-        [after(first_pieces[0], theirs)] + first_pieces[1:]
-    )
-
     validity = lax.dynamic_slice_in_dim(pixel_masks, own_start, images, 0).astype(WIDE)
     validity = validity.reshape(images, 1, PIX)
     member = (jnp.arange(C)[:, None] // WIDTH == jnp.arange(C)[None, :] // WIDTH).astype(LOW)
@@ -971,7 +1018,7 @@
     flat = jnp.arange(2 * 3 * ROWS)
     third, entry_row = flat // PAIR, flat % PAIR
     embed_index = (jnp.bitwise_xor(block, order)[:, None] * PAIR + entry_row).reshape(-1)
-    embed_values = time_features(own_steps, embed_index, embed_width)
+    embed_values = time_features(after(own_steps, first_one), embed_index, embed_width)
     embed_split = jnp.stack(parts_of(embed_values), axis=2)
     embed_split = embed_split.reshape(images, PAIRS, 2, 2, 3, ROWS, 3)
     embed_split = jnp.transpose(embed_split, (0, 3, 1, 4, 2, 5, 6))
@@ -980,7 +1027,8 @@
     embed_parts = jnp.concatenate(
         [jnp.where(late, 0, embed_split), jnp.where(late, embed_split, 0)], axis=6
     ).reshape(images, 2, TAPS, 6)
-    embed_parts = jnp.pad(embed_parts, ((0, 0), (0, 0), (0, 0), (0, 122)))
+    embed_parts = jnp.concatenate([embed_parts[image] for image in range(images)], axis=2)
+    embed_parts = jnp.pad(embed_parts, ((0, 0), (0, 0), (0, 128 - 6 * images)))
     steps_row = jnp.pad(own_steps, (0, HALF - images))
     steps_row = jnp.pad(jnp.concatenate([steps_row, steps_row])[None, :], ((0, 7), (0, 0)))
 
@@ -996,6 +1044,7 @@
     image_rows = (shape(images, 8, C), per_image(8, C))
     weight_out = (shape(TAPS, TAPS, dtype=LOW), fixed(TAPS, TAPS))
     stack_out = (shape(TAPS // 2, images * PIX, dtype=LOW), per_columns(TAPS // 2, PIX))
+    input_out = (shape(C // 2, images * PIX, dtype=LOW), per_columns(C // 2, PIX))
     anywhere = pl.BlockSpec(memory_space=pl.ANY)
 
     prepared = run(
@@ -1013,7 +1062,11 @@
         [value_scratch],
     )
     whole, first_low, first_high, stats_whole = prepared
-    cots = others(cotangent)
+    cots = others(after(cotangent, first_one))
+    first_pieces = first_pieces + gather_three(after(first_pieces, first_low))
+    mine, side = after(second_one, first_low)
+    second_one = halves(mine[:, :SECOND], side[:, :SECOND], 1)
+    bundle_one = halves(mine[:, SECOND:], side[:, SECOND:], 1)
     second_normed, stats_first, first_weight = run(
         first_kernel,
         place,
@@ -1022,7 +1075,7 @@
             mask_in,
             member_in,
             (first_pieces, [fixed(PIECE, TAPS)] * 8),
-            (after([first_low, first_high], second_one, cots), [per_columns(TAPS // 2, PIX)] * 2),
+            (after([first_low, first_high], second_one, cots, embed_parts), [per_columns(TAPS // 2, PIX)] * 2),
         ],
         [image_wide, image_small, weight_out],
         [value_scratch, product_scratch],
@@ -1030,33 +1083,38 @@
     second_pieces = gather_two(second_one)
     second_pieces = second_pieces + gather_three(after(second_pieces, second_normed))
     bundle_pieces = gather_two(bundle_one)
-    their_cots = swap(after(cots, second_normed), 0, 1)
-    second_low, second_high, residual, attend_input, stats_second, second_weight = run(
+    their_cots = swap(after(cots, first_low), 0, 1)
+    second_low, second_high, residual, stats_second = run(
         second_kernel,
         place,
         images,
         [
             (after(second_normed, bundle_one), per_image(C, PIX)),
             (whole, per_image(C, PIX)),
-            (embed_parts, per_image(2, TAPS, 128)),
+            (embed_parts, fixed(2, TAPS, 128)),
             mask_in,
             params_in,
             member_in,
             (second_pieces, [fixed(PIECE, 2 * SECOND)] * 8),
         ],
-        [stack_out, stack_out, image_wide, image_low, image_small, weight_out],
-        [pltpu.VMEM((2, 2, TAPS, 128), LOW), value_scratch, product_scratch],
+        [input_out, input_out, image_wide, image_small],
+        [
+            pltpu.VMEM((TAPS, TAPS), LOW),
+            pltpu.VMEM((2, 2, TAPS, 128), LOW),
+            value_scratch,
+            pltpu.VMEM((TAPS, PIX), LOW),
+            product_scratch,
+        ],
         room=60,
     )
-    bundle_pieces = bundle_pieces + gather_three(after(bundle_pieces, attend_input))
+    bundle_pieces = bundle_pieces + gather_three(after(bundle_pieces, residual))
     second_theirs = swap(second_high, 1, 0)
     mixed_rows = PAIRS // 2 * (JOINT - PIECE)
-    block_keep, block_send, residual_grad, second_grad, *mixed, small_third = run(
+    block_keep, block_send, second_grad, *mixed, small_third = run(
         attend_kernel,
         place,
         images,
         [
-            (attend_input, per_image(C, PIX)),
             (residual, per_image(C, PIX)),
             (stats_second, per_image(C, 128)),
             (cotangent, own_image(HALF, PIX)),
@@ -1064,12 +1122,11 @@
             mask_in,
             params_in,
             member_in,
-            (bundle_pieces, [fixed(PAIR, 2 * MIXED)] * 8),
+            (bundle_pieces, [fixed(PIECE, 2 * PACKED)] * 8),
         ],
         [
             (shape(2 * images, HALF, PIX, dtype=LOW), own_image(HALF, PIX)),
             (shape(images, HALF, PIX, dtype=LOW), per_image(HALF, PIX)),
-            image_wide,
             image_low,
             (shape(mixed_rows, TAPS), fixed(mixed_rows, TAPS)),
             (shape(mixed_rows, TAPS, dtype=LOW), fixed(mixed_rows, TAPS)),
@@ -1077,6 +1134,7 @@
         ],
         [
             pltpu.VMEM((2, C, 2 * C), WIDE),
+            pltpu.VMEM((C, PIX), LOW),
             pltpu.VMEM((C, TAPS), LOW),
             pltpu.VMEM((C, C), LOW),
             pltpu.VMEM((C, PIX), LOW),
@@ -1110,7 +1168,7 @@
         images,
         [
             (after(second_grad, joint), per_image(C, PIX)),
-            (second_weight, fixed(TAPS, TAPS)),
+            (second_pieces, [fixed(PIECE, 2 * SECOND)] * 8),
             (second_normed, per_image(C, PIX)),
             (stats_first, per_image(C, 128)),
             (stats_second, per_image(C, 128)),
@@ -1119,7 +1177,8 @@
             member_in,
         ],
         [image_low, image_rows],
-        back_scratch,
+        [pltpu.VMEM((TAPS, TAPS), LOW)] + back_scratch,
+        room=32,
     )
     masked_out = lax.dynamic_update_slice_in_dim(
         after(block_keep, joint), block_theirs, other_start, 0
@@ -1146,7 +1205,7 @@
                 (first_weight, fixed(TAPS, TAPS)),
                 (whole, per_image(C, PIX, first=image)),
                 (stats_whole, per_image(C, 128, first=image)),
-                (residual_grad, per_image(C, PIX, first=image)),
+                (second_grad, per_image(C, PIX, first=image)),
                 (validity, per_image(1, PIX, first=image)),
                 params_in,
                 member_in,

time: 272 us -> 253 us (0.930)
  Pallas kernels: 153 us -> 147 us
  other arithmetic: 11.2 us -> 5.75 us
  starting transfers between devices: 55.6 us -> 51.9 us
  local copies, waits for them, and re-layouts: 25.3 us -> 22.1 us
    pallas_call x16 -> x17, Pallas kernels: 153 us -> 147 us  [run(): pl.pallas_call(body, grid_spec=pltpu.PrefetchScalarGridSpec(num_scalar_pr...]
    ppermute x55 -> x53, starting transfers between devices: 55.6 us -> 51.9 us  [swap(): return lax.ppermute(value, ('dp', 'chan'), pairs)]
    unnamed x128 -> x136, local copies, waits for them, and re-layouts: 13.7 us -> 11.9 us
    ppermute x55 -> x53, waiting for transfers between devices: 20.3 us -> 19.1 us  [swap(): return lax.ppermute(value, ('dp', 'chan'), pairs)]
  transfers between devices with their start and end apart: 55 -> 53, of which waited for: 13 -> 12; matrix products, arithmetic and copies ran while one was open for 8% -> 6% of each run, Pallas kernels for 57% -> 33%
where the time goes in v1:
time: 253 us; the launch traced here: 249 us
  Pallas kernels  147 us (58%)
  starting transfers between devices  51.9 us (21%)
  local copies, waits for them, and re-layouts  22.1 us (9%)
  waiting for transfers between devices  19.1 us (8%)
  other arithmetic  5.75 us (2%)
    pallas_call x17, Pallas kernels, run(): pl.pallas_call(body, grid_spec=pltpu.PrefetchScalarGridSpec(num_scalar_pr...  147 us
    ppermute x53, starting transfers between devices, swap(): return lax.ppermute(value, ('dp', 'chan'), pairs)  51.9 us
    ppermute x53, waiting for transfers between devices, swap(): return lax.ppermute(value, ('dp', 'chan'), pairs)  19.1 us
    unnamed x136, local copies, waits for them, and re-layouts  11.9 us
  transfers between devices with their start and end apart: 53, of which 12 were waited for; matrix products, arithmetic and copies ran while one was open for 6% of the time, Pallas kernels for 33%

profile of v1, /device:TPU:0, one launch (start us, length us, event | category | flops | bytes accessed | tf_op | source)
XLA Modules:
  0.0 249.4 jit_solution(6521051137153865020)
XLA Ops:
  1.9 4.1 %collective-permute-start.1 = (bf16[72,576]{1,0:T(8,128)(2,1)S(1)}, bf16[72,576]{1,0:T(8,128)(2,1)S(1)}, u32[]{:S(2)}, u32[]{:S(2)}) collective-permute-start(bf16[72,576]{1,0:T(8,128)(2,1)S(1)} %reshape.352), channel_id=1, source_target_pairs={{0,16},{1,17},{2,18},{3,19},{4,20},{5,21},{6,22},{7,23},{8,24},{9,... | collective-permute-start | bytes 248840 | tf_op jit(solution)/shard_map/ppermute | solution.py:872
  6.0 1.3 collective-permute-start.2
  9.1 2.1 constant_dynamic-slice_fusion.1
  11.2 1.7 collective-permute-start.6
  14.4 2.6 %collective-permute-start.11 = (bf16[72,1088]{1,0:T(8,128)(2,1)}, bf16[72,1088]{1,0:T(8,128)(2,1)}, u32[]{:S(2)}, u32[]{:S(2)}) collective-permute-start(bf16[72,1088]{1,0:T(8,128)(2,1)} %concatenate.76), channel_id=1, source_target_pairs={{0,16},{1,17},{2,18},{3,19},{4,20},{5,21},{6,22},{7,23},{8,24},{9,... | collective-permute-start | bytes 470024 | tf_op jit(solution)/shard_map/ppermute | solution.py:872
  19.1 1.6 collective-permute-start.3
  20.7 1.5 collective-permute-start.4
  25.8 2.2 constant_dynamic-slice_fusion
  29.7 2.9 %collective-permute-done.6.refs_1_ = bf16[2,192,1024]{2,1,0:T(8,128)(2,1)S(1)} collective-permute-done((bf16[2,192,1024]{2,1,0:T(8,128)(2,1)}, bf16[2,192,1024]{2,1,0:T(8,128)(2,1)S(1)}, u32[]{:S(2)}, u32[]{:S(2)}) %collective-permute-start.6) | collective-permute-done | bytes 786464 | tf_op jit(solution)/shard_map/ppermute | solution.py:872
  32.6 5.5 %shard_map.196 = (bf16[2,384,1024]{2,1,0:T(8,128)(2,1)S(1)}, bf16[576,2048]{1,0:T(8,128)(2,1)S(1)}, bf16[576,2048]{1,0:T(8,128)(2,1)S(1)}, f32[2,384,128]{2,1,0:T(8,128)S(1)}) custom-call(s32[19]{0:T(128)S(1)} %pad_add_fusion.place, bf16[4,192,1024]{2,1,0:T(8,128)(2,1)S(1)} %copy-done.6, bf16[2,192,1024]{2,1,0:T(8,128)(2,1)S(1)} %collective-permute-done.6.refs_1_, ...), custom_call_target="tpu_custom_call" | custom-call | flops 8000000000 | bytes 1048576 | tf_op jit(solution)/shard_map/pallas_call | solution.py:773
  38.1 1.2 copy-done.35
  41.4 1.2 collective-permute-start.13
  42.6 1.5 collective-permute-start.14
  45.0 10.9 %shard_map.197 = (f32[2,384,1024]{2,1,0:T(8,128)S(1)}, f32[2,384,128]{2,1,0:T(8,128)S(1)}, bf16[1152,1152]{1,0:T(8,128)(2,1)S(1)}) custom-call(s32[19]{0:T(128)S(1)} %pad_add_fusion.place, f32[2,1,1024]{2,1,0:T(1,128)S(1)} %reshape.350.refs_2_.refs_0_.refs_3_.refs_4_.refs_12_.refs_5_.refs_6_, ...), custom_call_target="tpu_custom_call" | custom-call | flops 8000000000 | bytes 1048576 | tf_op jit(solution)/shard_map/pallas_call | solution.py:773
  55.9 1.5 copy-done.31
  57.4 1.7 copy-done.33
  59.8 4.7 %collective-permute-done.14.refs_8_.refs_3_ = bf16[144,1664]{1,0:T(8,128)(2,1)S(1)} collective-permute-done((bf16[144,1664]{1,0:T(8,128)(2,1)S(1)}, bf16[144,1664]{1,0:T(8,128)(2,1)S(1)}, u32[]{:S(2)}, u32[]{:S(2)}) %collective-permute-start.14) | collective-permute-done | bytes 479264 | tf_op jit(solution)/shard_map/ppermute | solution.py:872
  66.8 1.2 collective-permute-start.21
  68.0 1.2 collective-permute-start.22
  69.3 1.1 collective-permute-start.23
  70.4 1.5 collective-permute-start.20
  72.6 18.2 %shard_map.198 = (bf16[192,2048]{1,0:T(8,128)(2,1)}, bf16[192,2048]{1,0:T(8,128)(2,1)}, f32[2,384,1024]{2,1,0:T(8,128)}, f32[2,384,128]{2,1,0:T(8,128)}) custom-call(s32[19]{0:T(128)} %copy-done.11, f32[2,384,1024]{2,1,0:T(8,128)} %copy-done.33, bf16[2,384,1024]{2,1,0:T(8,128)(2,1)} %copy-done.35, bf16[2,1152,128]{2,1,0:T(8,128)(2,1)} %pad.22.refs_2_, ...), custom_call_target="tpu_custom_call" | custom-call | flops 8000000000 | bytes 1048576 | tf_op jit(solution)/shard_map/pallas_call | solution.py:773
  93.7 65.6 %shard_map.199 = (bf16[4,192,1024]{2,1,0:T(8,128)(2,1)}, bf16[2,192,1024]{2,1,0:T(8,128)(2,1)}, bf16[2,384,1024]{2,1,0:T(8,128)(2,1)}, f32[256,1152]{1,0:T(8,128...) custom-call(s32[19]{0:T(128)} %copy-done.11, f32[2,384,1024]{2,1,0:T(8,128)} %get-tuple-element.107.refs_0_, ...), custom_call_target="tpu_custom_call" | custom-call | flops 60000002048 | bytes 1048576 | tf_op jit(solution)/shard_map/pallas_call | solution.py:773
  161.0 1.4 copy-done.15
  162.4 1.1 copy-done.38
  163.5 3.9 %shard_map.200.refs_2_ = f32[576,1152]{1,0:T(8,128)S(1)} custom-call(s32[19]{0:T(128)S(1)} %copy-done.12, bf16[2,384,1024]{2,1,0:T(8,128)(2,1)S(1)} %copy-done.15, bf16[192,2048]{1,0:T(8,128)(2,1)S(1)} %copy-done.38), custom_call_target="tpu_custom_call" | custom-call | flops 8000000000 | bytes 1048576 | tf_op jit(solution)/shard_map/pallas_call | solution.py:773
  167.7 4.0 %shard_map.201 = (f32[208,1152]{1,0:T(8,128)S(1)}, bf16[208,1152]{1,0:T(8,128)(2,1)S(1)}, bf16[208,1152]{1,0:T(8,128)(2,1)S(1)}, bf16[208,1152]{1,0:T(8,128)(2,1)S(1)}) custom-call(s32[19]{0:T(128)S(1)} %copy-done.12, bf16[2,384,1024]{2,1,0:T(8,128)(2,1)S(1)} %collective-permute-done.28.refs_0_, bf16[192,2048]{1,0:T(8,128)(2,1)S(1)} %collective-permute-done.29.refs_1_, ...), custom_call_target="tpu_custom_call" | custom-call | flops 8000000000 | bytes 1048576 | tf_op jit(solution)/shard_map/pallas_call | solution.py:773
  171.7 1.2 collective-permute-start.33
  172.9 1.2 collective-permute-start.34
  174.2 1.1 collective-permute-start.35
  175.4 11.3 %shard_map.202 = (bf16[2,384,1024]{2,1,0:T(8,128)(2,1)S(1)}, f32[2,8,384]{2,1,0:T(8,128)S(1)}) custom-call(s32[19]{0:T(128)S(1)} %copy-done.12, bf16[2,384,1024]{2,1,0:T(8,128)(2,1)S(1)} %copy-done.16, bf16[144,1664]{1,0:T(8,128)(2,1)S(1)} %copy-done.5, bf16[144,1664]{1,0:T(8,128)(2,1)S(1)} %copy-done.18, bf16[144,1664]{1,0:T(8,128)(2,1)S(1)} %copy-done.20, ...), custom_call_target="tpu_custom_call" | custom-call | flops 8000000000 | bytes 1048576 | tf_op jit(solution)/shard_map/pallas_call | solution.py:773
  186.8 1.1 copy-done.56
  188.0 6.9 %shard_map.203 = (bf16[576,1152]{1,0:T(8,128)(2,1)S(1)}, f32[576,1152]{1,0:T(8,128)S(1)}) custom-call(s32[19]{0:T(128)S(1)} %copy-done.12, bf16[2,384,1024]{2,1,0:T(8,128)(2,1)S(1)} %get-tuple-element.147.refs_0_.refs_1_, bf16[576,2048]{1,0:T(8,128)(2,1)S(1)} %copy-done.1, bf16[576,2048]{1,0:T(8,128)(2,1)S(1)} %copy-done.3), custom_call_target="tpu_custom_call" | custom-call | flops 1000000000 | bytes 1048576 | tf_op jit(solution)/shard_map/pallas_call | solution.py:773
  196.8 1.6 collective-permute-start.36
  200.0 1.5 collective-permute-start.40
  201.5 1.2 collective-permute-start.41
  202.7 6.6 %shard_map.206 = (f32[4,192,1024]{2,1,0:T(8,128)}, bf16[1,192,1024]{2,1,0:T(8,128)(2,1)S(1)}, f32[8,384]{1,0:T(8,128)S(1)}) custom-call(s32[19]{0:T(128)S(1)} %copy-done.12, bf16[2,384,1024]{2,1,0:T(8,128)(2,1)S(1)} %get-tuple-element.147.refs_0_.refs_1_, bf16[1152,1152]{1,0:T(8,128)(2,1)S(1)} %copy-done.32, bf16[2,384,1024]{2,1,0:T(8,128)(2,1)S(1)} %copy-done.36, ...), custom_call_target="tpu_custom_call" | custom-call | flops 8000000000 | bytes 1048576 | tf_op jit(solution)/shard_map/pallas_call | solution.py:773
  209.8 2.8 %collective-permute-start.45 = (bf16[104,576]{1,0:T(8,128)(2,1)S(1)}, bf16[104,576]{1,0:T(8,128)(2,1)S(1)}, u32[]{:S(2)}, u32[]{:S(2)}) collective-permute-start(bf16[104,576]{1,0:T(8,128)(2,1)S(1)} %get-tuple-element.146), channel_id=1, source_target_pairs={{0,16},{1,17},{2,18},{3,19},{4,20},{5,21},{6,22},{7,23},{8,24},{9,... | collective-permute-start | bytes 359432 | tf_op jit(solution)/shard_map/ppermute | solution.py:872
  213.6 6.8 %shard_map.208 = (f32[4,192,1024]{2,1,0:T(8,128)}, bf16[1,192,1024]{2,1,0:T(8,128)(2,1)S(1)}, f32[16,384]{1,0:T(8,128)S(1)}) custom-call(s32[19]{0:T(128)S(1)} %copy-done.12, f32[4,192,1024]{2,1,0:T(8,128)} %get-tuple-element.142.refs_0_, bf16[2,384,1024]{2,1,0:T(8,128)(2,1)S(1)} %get-tuple-element.147.refs_0_.refs_1_, ...), custom_call_target="tpu_custom_call", output_to_operand_aliasing={{0}: (1, {})} | custom-call | flops 8000000000 | bytes 1048576 | tf_op jit(solution)/shard_map/pallas_call | solution.py:773
  223.8 1.3 shard_map.212
  225.9 1.6 collective-permute-start.47
  228.5 3.5 %collective-permute-done.38.refs_2_ = bf16[1,192,1024]{2,1,0:T(8,128)(2,1)S(1)} collective-permute-done((bf16[1,192,1024]{2,1,0:T(8,128)(2,1)S(1)}, bf16[1,192,1024]{2,1,0:T(8,128)(2,1)S(1)}, u32[]{:S(2)}, u32[]{:S(2)}) %collective-permute-start.38) | collective-permute-done | bytes 393248 | tf_op jit(solution)/shard_map/ppermute | solution.py:872
  232.1 1.6 collective-permute-start.49
  233.7 1.8 shard_map.209
  238.2 2.4 collective-permute-start.52
  241.5 2.8 %collective-permute-done.44.refs_3_ = bf16[72,576]{1,0:T(8,128)(2,1)S(1)} collective-permute-done((bf16[72,576]{1,0:T(8,128)(2,1)S(1)}, bf16[72,576]{1,0:T(8,128)(2,1)S(1)}, u32[]{:S(2)}, u32[]{:S(2)}) %collective-permute-start.44) | collective-permute-done | bytes 82976 | tf_op jit(solution)/shard_map/ppermute | solution.py:872
  244.3 1.3 shard_map.211
  245.7 1.4 collective-permute-done.51
  (306 shorter events, 38.7 us)
Async XLA Ops:
  1.9 16.9 %collective-permute-start.1 = (bf16[72,576]{1,0:T(8,128)(2,1)S(1)}, bf16[72,576]{1,0:T(8,128)(2,1)S(1)}, u32[]{:S(2)}, u32[]{:S(2)}) collective-permute-start(bf16[72,576]{1,0:T(8,128)(2,1)S(1)} %reshape.352), channel_id=1, source_target_pairs={{0,16},{1,17},{2,18},{3,19},{4,20},{5,21},{6,22},{7,23},{8,24},{9,... | collective-permute-start | bytes 248840 | tf_op jit(solution)/shard_map/ppermute | solution.py:872
  6.0 12.8 %collective-permute-start.2 = (bf16[72,576]{1,0:T(8,128)(2,1)S(1)}, bf16[72,576]{1,0:T(8,128)(2,1)S(1)}, u32[]{:S(2)}, u32[]{:S(2)}) collective-permute-start(bf16[72,576]{1,0:T(8,128)(2,1)S(1)} %reshape.352), channel_id=1, source_target_pairs={{0,17},{1,16},{2,19},{3,18},{4,21},{5,20},{6,23},{7,22},{8,25},{9,... | collective-permute-start | bytes 248840 | tf_op jit(solution)/shard_map/ppermute | solution.py:872
  8.8 10.2 %collective-permute-start = (bf16[80,576]{1,0:T(8,128)(2,1)S(1)}, bf16[80,576]{1,0:T(8,128)(2,1)S(1)}, u32[]{:S(2)}, u32[]{:S(2)}) collective-permute-start(bf16[80,576]{1,0:T(8,128)(2,1)S(1)} %pad_maximum_fusion.8), channel_id=1, source_target_pairs={{0,1},{1,0},{2,3},{3,2},{4,5},{5,4},{6,7},{7,6},{8,9},{9,8},{10,11... | collective-permute-start | bytes 276488 | tf_op jit(solution)/shard_map/ppermute | solution.py:872
  11.2 21.4 %collective-permute-start.6 = (bf16[2,192,1024]{2,1,0:T(8,128)(2,1)}, bf16[2,192,1024]{2,1,0:T(8,128)(2,1)S(1)}, u32[]{:S(2)}, u32[]{:S(2)}) collective-permute-start(bf16[2,192,1024]{2,1,0:T(8,128)(2,1)} %constant_dynamic-slice_fusion.1), channel_id=1, source_target_pairs={{0,1},{1,0},{2,3},{3,2},{4,5},{5,4},{6,7},{7,6},{8,9},{9,8},{10,11... | collective-permute-start | bytes 2359304 | tf_op jit(solution)/shard_map/ppermute | solution.py:872
  14.4 13.6 %collective-permute-start.11 = (bf16[72,1088]{1,0:T(8,128)(2,1)}, bf16[72,1088]{1,0:T(8,128)(2,1)}, u32[]{:S(2)}, u32[]{:S(2)}) collective-permute-start(bf16[72,1088]{1,0:T(8,128)(2,1)} %concatenate.76), channel_id=1, source_target_pairs={{0,16},{1,17},{2,18},{3,19},{4,20},{5,21},{6,22},{7,23},{8,24},{9,... | collective-permute-start | bytes 470024 | tf_op jit(solution)/shard_map/ppermute | solution.py:872
  19.1 20.9 %collective-permute-start.3 = (bf16[144,1152]{1,0:T(8,128)(2,1)S(1)}, bf16[144,1152]{1,0:T(8,128)(2,1)S(1)}, u32[]{:S(2)}, u32[]{:S(2)}) collective-permute-start(bf16[144,1152]{1,0:T(8,128)(2,1)S(1)} %bitcast.82), channel_id=1, source_target_pairs={{0,8},{1,9},{2,10},{3,11},{4,12},{5,13},{6,14},{7,15},{8,0},{9,1},... | collective-permute-start | bytes 995336 | tf_op jit(solution)/shard_map/ppermute | solution.py:872
  20.7 19.3 %collective-permute-start.4 = (bf16[144,1152]{1,0:T(8,128)(2,1)S(1)}, bf16[144,1152]{1,0:T(8,128)(2,1)S(1)}, u32[]{:S(2)}, u32[]{:S(2)}) collective-permute-start(bf16[144,1152]{1,0:T(8,128)(2,1)S(1)} %bitcast.83), channel_id=1, source_target_pairs={{0,4},{1,5},{2,6},{3,7},{4,0},{5,1},{6,2},{7,3},{8,12},{9,13},{10,... | collective-permute-start | bytes 995336 | tf_op jit(solution)/shard_map/ppermute | solution.py:872
  22.3 17.8 %collective-permute-start.5 = (bf16[144,1152]{1,0:T(8,128)(2,1)S(1)}, bf16[144,1152]{1,0:T(8,128)(2,1)S(1)}, u32[]{:S(2)}, u32[]{:S(2)}) collective-permute-start(bf16[144,1152]{1,0:T(8,128)(2,1)S(1)} %bitcast.84), channel_id=1, source_target_pairs={{0,12},{1,13},{2,14},{3,15},{4,8},{5,9},{6,10},{7,11},{8,4},{9,5},... | collective-permute-start | bytes 995336 | tf_op jit(solution)/shard_map/ppermute | solution.py:872
  29.1 11.0 %collective-permute-start.12 = (bf16[144,1088]{1,0:T(8,128)(2,1)S(1)}, bf16[144,1088]{1,0:T(8,128)(2,1)S(1)}, u32[]{:S(2)}, u32[]{:S(2)}) collective-permute-start(bf16[144,1088]{1,0:T(8,128)(2,1)S(1)} %bitcast.87), channel_id=1, source_target_pairs={{0,1},{1,0},{2,3},{3,2},{4,5},{5,4},{6,7},{7,6},{8,9},{9,8},{10,11... | collective-permute-start | bytes 940040 | tf_op jit(solution)/shard_map/ppermute | solution.py:872
  40.1 2.5 %collective-permute-start.10 = (bf16[144,1152]{1,0:T(8,128)(2,1)S(1)}, bf16[144,1152]{1,0:T(8,128)(2,1)S(1)}, u32[]{:S(2)}, u32[]{:S(2)}) collective-permute-start(bf16[144,1152]{1,0:T(8,128)(2,1)S(1)} %collective-permute-done.5.refs_5_), channel_id=1, source_target_pairs={{0,2},{1,3},{2,0},{3,1},{4,6},{5,7},{6,4},{7,5},{8,10},{9,11},{10,... | collective-permute-start | bytes 995336 | tf_op jit(solution)/shard_map/ppermute | solution.py:872
  40.2 4.0 %collective-permute-start.7 = (bf16[144,1152]{1,0:T(8,128)(2,1)S(1)}, bf16[144,1152]{1,0:T(8,128)(2,1)S(1)}, u32[]{:S(2)}, u32[]{:S(2)}) collective-permute-start(bf16[144,1152]{1,0:T(8,128)(2,1)S(1)} %bitcast.85), channel_id=1, source_target_pairs={{0,2},{1,3},{2,0},{3,1},{4,6},{5,7},{6,4},{7,5},{8,10},{9,11},{10,... | collective-permute-start | bytes 995336 | tf_op jit(solution)/shard_map/ppermute | solution.py:872
  40.6 4.3 %collective-permute-start.8 = (bf16[144,1152]{1,0:T(8,128)(2,1)S(1)}, bf16[144,1152]{1,0:T(8,128)(2,1)S(1)}, u32[]{:S(2)}, u32[]{:S(2)}) collective-permute-start(bf16[144,1152]{1,0:T(8,128)(2,1)S(1)} %collective-permute-done.3.refs_3_), channel_id=1, source_target_pairs={{0,2},{1,3},{2,0},{3,1},{4,6},{5,7},{6,4},{7,5},{8,10},{9,11},{10,... | collective-permute-start | bytes 995336 | tf_op jit(solution)/shard_map/ppermute | solution.py:872
  40.7 4.2 %collective-permute-start.9 = (bf16[144,1152]{1,0:T(8,128)(2,1)S(1)}, bf16[144,1152]{1,0:T(8,128)(2,1)S(1)}, u32[]{:S(2)}, u32[]{:S(2)}) collective-permute-start(bf16[144,1152]{1,0:T(8,128)(2,1)S(1)} %collective-permute-done.4.refs_4_), channel_id=1, source_target_pairs={{0,2},{1,3},{2,0},{3,1},{4,6},{5,7},{6,4},{7,5},{8,10},{9,11},{10,... | collective-permute-start | bytes 995336 | tf_op jit(solution)/shard_map/ppermute | solution.py:872
  41.4 18.4 %collective-permute-start.13 = (bf16[144,1664]{1,0:T(8,128)(2,1)S(1)}, bf16[144,1664]{1,0:T(8,128)(2,1)S(1)}, u32[]{:S(2)}, u32[]{:S(2)}) collective-permute-start(bf16[144,1664]{1,0:T(8,128)(2,1)S(1)} %pad_maximum_fusion.refs_6_.refs_1_), channel_id=1, source_target_pairs={{0,8},{1,9},{2,10},{3,11},{4,12},{5,13},{6,14},{7,15},{8,0},{9,1},... | collective-permute-start | bytes 1437704 | tf_op jit(solution)/shard_map/ppermute | solution.py:872
  42.6 22.0 %collective-permute-start.14 = (bf16[144,1664]{1,0:T(8,128)(2,1)S(1)}, bf16[144,1664]{1,0:T(8,128)(2,1)S(1)}, u32[]{:S(2)}, u32[]{:S(2)}) collective-permute-start(bf16[144,1664]{1,0:T(8,128)(2,1)S(1)} %pad_maximum_fusion.refs_6_.refs_1_), channel_id=1, source_target_pairs={{0,4},{1,5},{2,6},{3,7},{4,0},{5,1},{6,2},{7,3},{8,12},{9,13},{10,... | collective-permute-start | bytes 1437704 | tf_op jit(solution)/shard_map/ppermute | solution.py:872
  44.1 21.5 %collective-permute-start.15 = (bf16[144,1664]{1,0:T(8,128)(2,1)S(1)}, bf16[144,1664]{1,0:T(8,128)(2,1)S(1)}, u32[]{:S(2)}, u32[]{:S(2)}) collective-permute-start(bf16[144,1664]{1,0:T(8,128)(2,1)S(1)} %pad_maximum_fusion.refs_6_.refs_1_), channel_id=1, source_target_pairs={{0,12},{1,13},{2,14},{3,15},{4,8},{5,9},{6,10},{7,11},{8,4},{9,5},... | collective-permute-start | bytes 1437704 | tf_op jit(solution)/shard_map/ppermute | solution.py:872
  65.6 2.4 collective-permute-start.16
  65.6 3.6 %collective-permute-start.17 = (bf16[144,1664]{1,0:T(8,128)(2,1)S(1)}, bf16[144,1664]{1,0:T(8,128)(2,1)S(1)}, u32[]{:S(2)}, u32[]{:S(2)}) collective-permute-start(bf16[144,1664]{1,0:T(8,128)(2,1)S(1)} %collective-permute-done.13.refs_7_.refs_2_), channel_id=1, source_target_pairs={{0,2},{1,3},{2,0},{3,1},{4,6},{5,7},{6,4},{7,5},{8,10},{9,11},{10,... | collective-permute-start | bytes 1437704 | tf_op jit(solution)/shard_map/ppermute | solution.py:872
  66.1 4.2 %collective-permute-start.18 = (bf16[144,1664]{1,0:T(8,128)(2,1)S(1)}, bf16[144,1664]{1,0:T(8,128)(2,1)S(1)}, u32[]{:S(2)}, u32[]{:S(2)}) collective-permute-start(bf16[144,1664]{1,0:T(8,128)(2,1)S(1)} %collective-permute-done.14.refs_8_.refs_3_), channel_id=1, source_target_pairs={{0,2},{1,3},{2,0},{3,1},{4,6},{5,7},{6,4},{7,5},{8,10},{9,11},{10,... | collective-permute-start | bytes 1437704 | tf_op jit(solution)/shard_map/ppermute | solution.py:872
  66.2 5.6 %collective-permute-start.19 = (bf16[144,1664]{1,0:T(8,128)(2,1)S(1)}, bf16[144,1664]{1,0:T(8,128)(2,1)S(1)}, u32[]{:S(2)}, u32[]{:S(2)}) collective-permute-start(bf16[144,1664]{1,0:T(8,128)(2,1)S(1)} %collective-permute-done.15.refs_9_.refs_4_), channel_id=1, source_target_pairs={{0,2},{1,3},{2,0},{3,1},{4,6},{5,7},{6,4},{7,5},{8,10},{9,11},{10,... | collective-permute-start | bytes 1437704 | tf_op jit(solution)/shard_map/ppermute | solution.py:872
  66.8 24.1 %collective-permute-start.21 = (bf16[144,512]{1,0:T(8,128)(2,1)S(1)}, bf16[144,512]{1,0:T(8,128)(2,1)S(1)}, u32[]{:S(2)}, u32[]{:S(2)}) collective-permute-start(bf16[144,512]{1,0:T(8,128)(2,1)S(1)} %pad_maximum_fusion.7.refs_7_), channel_id=1, source_target_pairs={{0,8},{1,9},{2,10},{3,11},{4,12},{5,13},{6,14},{7,15},{8,0},{9,1},... | collective-permute-start | bytes 442376 | tf_op jit(solution)/shard_map/ppermute | solution.py:872
  68.0 22.9 %collective-permute-start.22 = (bf16[144,512]{1,0:T(8,128)(2,1)S(1)}, bf16[144,512]{1,0:T(8,128)(2,1)S(1)}, u32[]{:S(2)}, u32[]{:S(2)}) collective-permute-start(bf16[144,512]{1,0:T(8,128)(2,1)S(1)} %pad_maximum_fusion.7.refs_7_), channel_id=1, source_target_pairs={{0,4},{1,5},{2,6},{3,7},{4,0},{5,1},{6,2},{7,3},{8,12},{9,13},{10,... | collective-permute-start | bytes 442376 | tf_op jit(solution)/shard_map/ppermute | solution.py:872
  69.3 21.6 %collective-permute-start.23 = (bf16[144,512]{1,0:T(8,128)(2,1)S(1)}, bf16[144,512]{1,0:T(8,128)(2,1)S(1)}, u32[]{:S(2)}, u32[]{:S(2)}) collective-permute-start(bf16[144,512]{1,0:T(8,128)(2,1)S(1)} %pad_maximum_fusion.7.refs_7_), channel_id=1, source_target_pairs={{0,12},{1,13},{2,14},{3,15},{4,8},{5,9},{6,10},{7,11},{8,4},{9,5},... | collective-permute-start | bytes 442376 | tf_op jit(solution)/shard_map/ppermute | solution.py:872
  70.4 21.6 %collective-permute-start.20 = (bf16[2,192,1024]{2,1,0:T(8,128)(2,1)}, bf16[2,192,1024]{2,1,0:T(8,128)(2,1)}, u32[]{:S(2)}, u32[]{:S(2)}) collective-permute-start(bf16[2,192,1024]{2,1,0:T(8,128)(2,1)} %constant_dynamic-slice_fusion), channel_id=1, source_target_pairs={{0,1},{1,0},{2,3},{3,2},{4,5},{5,4},{6,7},{7,6},{8,9},{9,8},{10,11... | collective-permute-start | bytes 2359304 | tf_op jit(solution)/shard_map/ppermute | solution.py:872
  159.4 8.2 %collective-permute-start.28 = (bf16[2,384,1024]{2,1,0:T(8,128)(2,1)}, bf16[2,384,1024]{2,1,0:T(8,128)(2,1)S(1)}, u32[]{:S(2)}, u32[]{:S(2)}) collective-permute-start(bf16[2,384,1024]{2,1,0:T(8,128)(2,1)} %get-tuple-element.126.refs_0_.refs_4_.refs_5_), channel_id=1, source_target_pairs={{0,2},{1,3},{2,0},{3,1},{4,6},{5,7},{6,4},{7,5},{8,10},{9,11},{10,... | collective-permute-start | bytes 4718600 | tf_op jit(solution)/shard_map/ppermute | solution.py:872
  159.8 7.7 %collective-permute-start.29 = (bf16[192,2048]{1,0:T(8,128)(2,1)}, bf16[192,2048]{1,0:T(8,128)(2,1)S(1)}, u32[]{:S(2)}, u32[]{:S(2)}) collective-permute-start(bf16[192,2048]{1,0:T(8,128)(2,1)} %get-tuple-element.116), channel_id=1, source_target_pairs={{0,2},{1,3},{2,0},{3,1},{4,6},{5,7},{6,4},{7,5},{8,10},{9,11},{10,... | collective-permute-start | bytes 2359304 | tf_op jit(solution)/shard_map/ppermute | solution.py:872
  160.1 7.4 %collective-permute-start.30 = (bf16[256,1152]{1,0:T(8,128)(2,1)}, bf16[256,1152]{1,0:T(8,128)(2,1)S(1)}, u32[]{:S(2)}, u32[]{:S(2)}) collective-permute-start(bf16[256,1152]{1,0:T(8,128)(2,1)} %get-tuple-element.119), channel_id=1, source_target_pairs={{0,2},{1,3},{2,0},{3,1},{4,6},{5,7},{6,4},{7,5},{8,10},{9,11},{10,... | collective-permute-start | bytes 1769480 | tf_op jit(solution)/shard_map/ppermute | solution.py:872
  160.4 26.3 %collective-permute-start.31 = (bf16[2,192,1024]{2,1,0:T(8,128)(2,1)}, bf16[2,192,1024]{2,1,0:T(8,128)(2,1)S(1)}, u32[]{:S(2)}, u32[]{:S(2)}) collective-permute-start(bf16[2,192,1024]{2,1,0:T(8,128)(2,1)} %get-tuple-element.125), channel_id=1, source_target_pairs={{0,1},{1,0},{2,3},{3,2},{4,5},{5,4},{6,7},{7,6},{8,9},{9,8},{10,11... | collective-permute-start | bytes 2359304 | tf_op jit(solution)/shard_map/ppermute | solution.py:872
  171.7 23.2 %collective-permute-start.33 = (bf16[208,1152]{1,0:T(8,128)(2,1)S(1)}, bf16[208,1152]{1,0:T(8,128)(2,1)S(1)}, u32[]{:S(2)}, u32[]{:S(2)}) collective-permute-start(bf16[208,1152]{1,0:T(8,128)(2,1)S(1)} %get-tuple-element.121), channel_id=1, source_target_pairs={{0,8},{1,9},{2,10},{3,11},{4,12},{5,13},{6,14},{7,15},{8,0},{9,1},... | collective-permute-start | bytes 1437704 | tf_op jit(solution)/shard_map/ppermute | solution.py:872
  172.9 22.1 %collective-permute-start.34 = (bf16[208,1152]{1,0:T(8,128)(2,1)S(1)}, bf16[208,1152]{1,0:T(8,128)(2,1)S(1)}, u32[]{:S(2)}, u32[]{:S(2)}) collective-permute-start(bf16[208,1152]{1,0:T(8,128)(2,1)S(1)} %get-tuple-element.122), channel_id=1, source_target_pairs={{0,4},{1,5},{2,6},{3,7},{4,0},{5,1},{6,2},{7,3},{8,12},{9,13},{10,... | collective-permute-start | bytes 1437704 | tf_op jit(solution)/shard_map/ppermute | solution.py:872
  174.2 21.6 %collective-permute-start.35 = (bf16[208,1152]{1,0:T(8,128)(2,1)S(1)}, bf16[208,1152]{1,0:T(8,128)(2,1)S(1)}, u32[]{:S(2)}, u32[]{:S(2)}) collective-permute-start(bf16[208,1152]{1,0:T(8,128)(2,1)S(1)} %get-tuple-element.123), channel_id=1, source_target_pairs={{0,12},{1,13},{2,14},{3,15},{4,8},{5,9},{6,10},{7,11},{8,4},{9,5},... | collective-permute-start | bytes 1437704 | tf_op jit(solution)/shard_map/ppermute | solution.py:872
  194.9 3.4 %collective-permute-start.32 = (bf16[576,1152]{1,0:T(8,128)(2,1)S(1)}, bf16[576,1152]{1,0:T(8,128)(2,1)S(1)}, u32[]{:S(2)}, u32[]{:S(2)}) collective-permute-start(bf16[576,1152]{1,0:T(8,128)(2,1)S(1)} %get-tuple-element.131), channel_id=1, source_target_pairs={{0,2},{1,3},{2,0},{3,1},{4,6},{5,7},{6,4},{7,5},{8,10},{9,11},{10,... | collective-permute-start | bytes 3981320 | tf_op jit(solution)/shard_map/ppermute | solution.py:872
  196.8 12.5 %collective-permute-start.36 = (bf16[208,576]{1,0:T(8,128)(2,1)S(1)}, bf16[208,576]{1,0:T(8,128)(2,1)S(1)}, u32[]{:S(2)}, u32[]{:S(2)}) collective-permute-start(bf16[208,576]{1,0:T(8,128)(2,1)S(1)} %get-tuple-element.138), channel_id=1, source_target_pairs={{0,1},{1,0},{2,3},{3,2},{4,5},{5,4},{6,7},{7,6},{8,9},{9,8},{10,11... | collective-permute-start | bytes 718856 | tf_op jit(solution)/shard_map/ppermute | solution.py:872
  199.1 21.4 %collective-permute-start.39 = (bf16[144,1152]{1,0:T(8,128)(2,1)S(1)}, bf16[144,1152]{1,0:T(8,128)(2,1)S(1)}, u32[]{:S(2)}, u32[]{:S(2)}) collective-permute-start(bf16[144,1152]{1,0:T(8,128)(2,1)S(1)} %get-tuple-element.133), channel_id=1, source_target_pairs={{0,8},{1,9},{2,10},{3,11},{4,12},{5,13},{6,14},{7,15},{8,0},{9,1},... | collective-permute-start | bytes 995336 | tf_op jit(solution)/shard_map/ppermute | solution.py:872
  200.0 21.5 %collective-permute-start.40 = (bf16[144,1152]{1,0:T(8,128)(2,1)S(1)}, bf16[144,1152]{1,0:T(8,128)(2,1)S(1)}, u32[]{:S(2)}, u32[]{:S(2)}) collective-permute-start(bf16[144,1152]{1,0:T(8,128)(2,1)S(1)} %get-tuple-element.134), channel_id=1, source_target_pairs={{0,4},{1,5},{2,6},{3,7},{4,0},{5,1},{6,2},{7,3},{8,12},{9,13},{10,... | collective-permute-start | bytes 995336 | tf_op jit(solution)/shard_map/ppermute | solution.py:872
  201.5 20.0 %collective-permute-start.41 = (bf16[144,1152]{1,0:T(8,128)(2,1)S(1)}, bf16[144,1152]{1,0:T(8,128)(2,1)S(1)}, u32[]{:S(2)}, u32[]{:S(2)}) collective-permute-start(bf16[144,1152]{1,0:T(8,128)(2,1)S(1)} %get-tuple-element.135), channel_id=1, source_target_pairs={{0,12},{1,13},{2,14},{3,15},{4,8},{5,9},{6,10},{7,11},{8,4},{9,5},... | collective-permute-start | bytes 995336 | tf_op jit(solution)/shard_map/ppermute | solution.py:872
  209.8 14.0 %collective-permute-start.45 = (bf16[104,576]{1,0:T(8,128)(2,1)S(1)}, bf16[104,576]{1,0:T(8,128)(2,1)S(1)}, u32[]{:S(2)}, u32[]{:S(2)}) collective-permute-start(bf16[104,576]{1,0:T(8,128)(2,1)S(1)} %get-tuple-element.146), channel_id=1, source_target_pairs={{0,16},{1,17},{2,18},{3,19},{4,20},{5,21},{6,22},{7,23},{8,24},{9,... | collective-permute-start | bytes 359432 | tf_op jit(solution)/shard_map/ppermute | solution.py:872
  212.6 11.2 %collective-permute-start.37 = (bf16[1,192,1024]{2,1,0:T(8,128)(2,1)S(1)}, bf16[1,192,1024]{2,1,0:T(8,128)(2,1)S(1)}, u32[]{:S(2)}, u32[]{:S(2)}) collective-permute-start(bf16[1,192,1024]{2,1,0:T(8,128)(2,1)S(1)} %get-tuple-element.151), channel_id=1, source_target_pairs={{0,1},{1,0},{2,3},{3,2},{4,5},{5,4},{6,7},{7,6},{8,9},{9,8},{10,11... | collective-permute-start | bytes 1179656 | tf_op jit(solution)/shard_map/ppermute | solution.py:872
  220.5 11.6 %collective-permute-start.38 = (bf16[1,192,1024]{2,1,0:T(8,128)(2,1)S(1)}, bf16[1,192,1024]{2,1,0:T(8,128)(2,1)S(1)}, u32[]{:S(2)}, u32[]{:S(2)}) collective-permute-start(bf16[1,192,1024]{2,1,0:T(8,128)(2,1)S(1)} %get-tuple-element.152), channel_id=1, source_target_pairs={{0,1},{1,0},{2,3},{3,2},{4,5},{5,4},{6,7},{7,6},{8,9},{9,8},{10,11... | collective-permute-start | bytes 1179656 | tf_op jit(solution)/shard_map/ppermute | solution.py:872
  222.4 18.2 %collective-permute-start.42 = (bf16[72,576]{1,0:T(8,128)(2,1)S(1)}, bf16[72,576]{1,0:T(8,128)(2,1)S(1)}, u32[]{:S(2)}, u32[]{:S(2)}) collective-permute-start(bf16[72,576]{1,0:T(8,128)(2,1)S(1)} %get-tuple-element.154), channel_id=1, source_target_pairs={{0,1},{1,0},{2,3},{3,2},{4,5},{5,4},{6,7},{7,6},{8,9},{9,8},{10,11... | collective-permute-start | bytes 248840 | tf_op jit(solution)/shard_map/ppermute | solution.py:872
  223.5 18.1 %collective-permute-start.43 = (bf16[72,576]{1,0:T(8,128)(2,1)S(1)}, bf16[72,576]{1,0:T(8,128)(2,1)S(1)}, u32[]{:S(2)}, u32[]{:S(2)}) collective-permute-start(bf16[72,576]{1,0:T(8,128)(2,1)S(1)} %get-tuple-element.155), channel_id=1, source_target_pairs={{0,16},{1,17},{2,18},{3,19},{4,20},{5,21},{6,22},{7,23},{8,24},{9,... | collective-permute-start | bytes 248840 | tf_op jit(solution)/shard_map/ppermute | solution.py:872
  225.9 9.5 %collective-permute-start.47 = (f32[24,384]{1,0:T(8,128)S(1)}, f32[24,384]{1,0:T(8,128)S(1)}, u32[]{:S(2)}, u32[]{:S(2)}) collective-permute-start(f32[24,384]{1,0:T(8,128)S(1)} %pad_maximum_fusion.11), channel_id=1, source_target_pairs={{0,8},{1,9},{2,10},{3,11},{4,12},{5,13},{6,14},{7,15},{8,0},{9,1},... | collective-permute-start | bytes 110600 | tf_op jit(solution)/shard_map/ppermute | solution.py:872
  227.5 8.8 %collective-permute-start.48 = (f32[24,384]{1,0:T(8,128)S(1)}, f32[24,384]{1,0:T(8,128)S(1)}, u32[]{:S(2)}, u32[]{:S(2)}) collective-permute-start(f32[24,384]{1,0:T(8,128)S(1)} %pad_maximum_fusion.11), channel_id=1, source_target_pairs={{0,4},{1,5},{2,6},{3,7},{4,0},{5,1},{6,2},{7,3},{8,12},{9,13},{10,... | collective-permute-start | bytes 110600 | tf_op jit(solution)/shard_map/ppermute | solution.py:872
  232.1 4.9 %collective-permute-start.49 = (f32[24,384]{1,0:T(8,128)S(1)}, f32[24,384]{1,0:T(8,128)S(1)}, u32[]{:S(2)}, u32[]{:S(2)}) collective-permute-start(f32[24,384]{1,0:T(8,128)S(1)} %pad_maximum_fusion.11), channel_id=1, source_target_pairs={{0,12},{1,13},{2,14},{3,15},{4,8},{5,9},{6,10},{7,11},{8,4},{9,5},... | collective-permute-start | bytes 110600 | tf_op jit(solution)/shard_map/ppermute | solution.py:872
  235.4 8.9 %collective-permute-start.44 = (bf16[72,576]{1,0:T(8,128)(2,1)S(1)}, bf16[72,576]{1,0:T(8,128)(2,1)S(1)}, u32[]{:S(2)}, u32[]{:S(2)}) collective-permute-start(bf16[72,576]{1,0:T(8,128)(2,1)S(1)} %get-tuple-element.156), channel_id=1, source_target_pairs={{0,17},{1,16},{2,19},{3,18},{4,21},{5,20},{6,23},{7,22},{8,25},{9,... | collective-permute-start | bytes 248840 | tf_op jit(solution)/shard_map/ppermute | solution.py:872
  237.1 8.6 %collective-permute-start.50 = (f32[72,192]{1,0:T(8,128)S(1)}, f32[72,192]{1,0:T(8,128)S(1)}, u32[]{:S(2)}, u32[]{:S(2)}) collective-permute-start(f32[72,192]{1,0:T(8,128)S(1)} %get-tuple-element.221), channel_id=1, source_target_pairs={{0,1},{1,0},{2,3},{3,2},{4,5},{5,4},{6,7},{7,6},{8,9},{9,8},{10,11... | collective-permute-start | bytes 165896 | tf_op jit(solution)/shard_map/ppermute | solution.py:872
  238.2 8.9 %collective-permute-start.52 = (f32[72,192]{1,0:T(8,128)S(1)}, f32[72,192]{1,0:T(8,128)S(1)}, u32[]{:S(2)}, u32[]{:S(2)}) collective-permute-start(f32[72,192]{1,0:T(8,128)S(1)} %get-tuple-element.221), channel_id=1, source_target_pairs={{0,17},{1,16},{2,19},{3,18},{4,21},{5,20},{6,23},{7,22},{8,25},{9,... | collective-permute-start | bytes 165896 | tf_op jit(solution)/shard_map/ppermute | solution.py:872
  240.5 6.6 %collective-permute-start.51 = (f32[72,192]{1,0:T(8,128)S(1)}, f32[72,192]{1,0:T(8,128)S(1)}, u32[]{:S(2)}, u32[]{:S(2)}) collective-permute-start(f32[72,192]{1,0:T(8,128)S(1)} %get-tuple-element.220), channel_id=1, source_target_pairs={{0,16},{1,17},{2,18},{3,19},{4,20},{5,21},{6,22},{7,23},{8,24},{9,... | collective-permute-start | bytes 165896 | tf_op jit(solution)/shard_map/ppermute | solution.py:872
  (71 other events, 564.7 us)

commit v2 on v1

--- a/solution.py
+++ b/solution.py
@@ -28,6 +28,7 @@
 PAIRS = BLOCKS // 2
 KEYS = 128
 CHUNK = 256
+PART = 512
 LOW = jnp.bfloat16
 WIDE = jnp.float32
 ORDER = (0, 8, 4, 12, 2, 10, 6, 14, 1, 9, 5, 13, 3, 11, 7, 15)
@@ -148,7 +149,8 @@
 
 
 def back_to_channels(place_ref, product_ref, out_ref):
-    column = lax.broadcasted_iota(jnp.int32, (PAIR, PIX), 1) & (SIDE - 1)
+    pixels = product_ref.shape[1]
+    column = lax.broadcasted_iota(jnp.int32, (PAIR, pixels), 1) & (SIDE - 1)
     for pair in range(PAIRS):
         base = pair * PIECE
         first = product_ref[base : base + PAIR, :]
@@ -156,7 +158,7 @@
         last = product_ref[base + 2 * PAIR : base + 3 * PAIR, :]
         total = (
             middle
-            + jnp.where(column == SIDE - 1, 0.0, pltpu.roll(first, PIX - 1, 1))
+            + jnp.where(column == SIDE - 1, 0.0, pltpu.roll(first, pixels - 1, 1))
             + jnp.where(column == 0, 0.0, pltpu.roll(last, 1, 1))
         )
         for part in range(2):
@@ -179,6 +181,16 @@
 
 def small_rows(columns):
     return small_columns(columns).T[:8]
+
+
+def columns_of(rows):
+    return jnp.concatenate([rows, jnp.zeros((120, C), WIDE)], axis=0).T
+
+
+def join_halves(place, mine, theirs, out):
+    own, other = half_offsets(place)
+    out[pl.ds(own, HALF), :] = mine[0].astype(out.dtype)
+    out[pl.ds(other, HALF), :] = theirs[0].astype(out.dtype)
 
 
 def set_rows(rows, count):
@@ -235,19 +247,15 @@
     mask_ref,
     params,
     member,
-    whole_out,
     low_out,
     high_out,
     stats_out,
     value,
 ):
-    own, other = half_offsets(place)
-    value[pl.ds(own, HALF), :] = mine[0].astype(WIDE)
-    value[pl.ds(other, HALF), :] = theirs[0].astype(WIDE)
+    join_halves(place, mine, theirs, value)
     mask = mask_ref[0]
-    whole_out[0] = value[...].astype(LOW)
     mean, factor = group_stats(value, member[...], mask, count_of(mask))
-    stats_out[0] = small_columns((mean, factor))
+    stats_out[0] = small_rows((mean, factor))
     scale = factor * params[:, 0:1]
     value[...] = (value[...] - mean) * scale + params[:, 1:2]
     build_stack(place, value, mask, (low_out, high_out))
@@ -272,13 +280,15 @@
         value[chan * HALF : (chan + 1) * HALF, :] = conv_out(product, chan)
     mean, factor = group_stats(value, member[...], mask, count_of(mask))
     normed_out[0] = (value[...] - mean) * factor
-    stats_out[0] = small_columns((factor,))
+    stats_out[0] = small_rows((factor,))
 
 
 def second_kernel(
     place,
     normed,
-    whole,
+    stats_first,
+    mine,
+    theirs,
     embed_in,
     mask_ref,
     params,
@@ -326,10 +336,14 @@
     product[...] = dot(weight[...], stack[...], TN)
     for chan in range(2):
         rows = slice(chan * HALF, (chan + 1) * HALF)
-        value[rows, :] = whole[0, rows, :].astype(WIDE) + conv_out(product, chan)
+        value[rows, :] = conv_out(product, chan)
+    own, other = half_offsets(place)
+    value[pl.ds(own, HALF), :] += mine[0].astype(WIDE)
+    value[pl.ds(other, HALF), :] += theirs[0].astype(WIDE)
     residual_out[0] = value[...]
     mean, factor = group_stats(value, member[...], mask, count)
-    stats_out[0] = small_columns((mean, factor, time_scale, time_shift))
+    first_factor = columns_of(stats_first[0])[:, 0:1]
+    stats_out[0] = small_rows((mean, factor, time_scale, time_shift, first_factor))
 
 
 def attend_kernel(
@@ -396,7 +410,8 @@
     count = count_of(mask)
     gradient[pl.ds(own, HALF), :] = (mine[0].astype(WIDE) * mask).astype(LOW)
     gradient[pl.ds(other, HALF), :] = (theirs[0].astype(WIDE) * mask).astype(LOW)
-    mean, factor = stats[0, :, 0:1], stats[0, :, 1:2]
+    columns = columns_of(stats[0])
+    mean, factor = columns[:, 0:1], columns[:, 1:2]
     scale = factor * params[:, 4:5]
     attend_in[...] = ((residual[0] - mean) * scale + params[:, 5:6]).astype(LOW)
     projected[...] = dot(project[...], attend_in[...], TN).astype(LOW)
@@ -521,8 +536,9 @@
 
 def own_filter_kernel(place, grads, stacks, send_out, keep_out, grad_stack):
     stack_gradients([grads], grad_stack)
-    send_out[...] = dot(stacks[1][...], grad_stack[...], NT).astype(LOW)
-    keep_out[...] = dot(stacks[0][...], grad_stack[...], NT)
+    total = dot(both_rows(stacks), grad_stack[...], NT)
+    keep_out[...] = total[: TAPS // 2]
+    send_out[...] = total[TAPS // 2 :].astype(LOW)
 
 
 def split_kernel(place, keep, received, *outs):
@@ -531,10 +547,28 @@
         out[...] = (keep[rows, :] + received[rows, :].astype(WIDE)).astype(out.dtype)
 
 
-def conv_back(place, grads, weight, grad_stack, product, value):
+def lane_sums(value):
+    return sum(value[:, lane : lane + 128] for lane in range(0, value.shape[1], 128))
+
+
+def conv_back(place, grads, weight, grad_stack, product, value, slope_of, mask, normed_of):
     stack_gradient(grads.at[0], grad_stack)
-    product[...] = dot(weight[...], grad_stack[...], NN)
-    back_to_channels(place, product, value)
+    spans = [slice(start, start + PART) for start in range(0, PIX, PART)]
+    plain = weighted = None
+    for index in range(len(spans) + 1):
+        if index < len(spans):
+            span = spans[index]
+            product[:, span] = dot(weight[...], grad_stack[:, span], NN)
+        if index > 0:
+            span = spans[index - 1]
+            back_to_channels(place, product.at[:, span], value.at[:, span])
+            normed = normed_of(span)
+            delta = value[:, span] * mask[:, span] * slope_of(normed)
+            value[:, span] = delta
+            sums = lane_sums(delta), lane_sums(delta * normed)
+            plain = sums[0] if plain is None else plain + sums[0]
+            weighted = sums[1] if weighted is None else weighted + sums[1]
+    return [jnp.sum(sums, axis=1, keepdims=True) for sums in (plain, weighted)]
 
 
 def second_back_kernel(
@@ -542,7 +576,6 @@
     grads,
     pieces,
     normed_ref,
-    stats_first,
     stats,
     mask_ref,
     params,
@@ -555,18 +588,28 @@
     value,
 ):
     load_second(weight, None, pieces)
-    conv_back(place, grads, weight, grad_stack, product, value)
     mask = mask_ref[0]
     count = count_of(mask)
     gain, bias = params[:, 2:3], params[:, 3:4]
-    factor = stats_first[0, :, 0:1]
-    time_scale, time_shift = 1.0 + stats[0, :, 2:3], stats[0, :, 3:4]
+    columns = columns_of(stats[0])
+    factor = columns[:, 4:5]
+    time_scale, time_shift = 1.0 + columns[:, 2:3], columns[:, 3:4]
+
+    def slope_of(normed):
+        return silu_slope((normed * gain + bias) * time_scale + time_shift)
+
+    plain, weighted = conv_back(
+        place,
+        grads,
+        weight,
+        grad_stack,
+        product,
+        value,
+        slope_of,
+        mask,
+        lambda span: normed_ref[0, :, span],
+    )
     normed = normed_ref[0]
-    hidden = (normed * gain + bias) * time_scale + time_shift
-    delta = value[...] * mask * silu_slope(hidden)
-    value[...] = delta
-    plain = jnp.sum(delta, axis=1, keepdims=True)
-    weighted = jnp.sum(delta * normed, axis=1, keepdims=True)
     scaled = gain * time_scale
     sums = group_sums(member[...], lane_pair(scaled * plain, scaled * weighted))
     first_sum, second_sum = sums[:, 0:1] / count, sums[:, 1:2] / count
@@ -587,7 +630,8 @@
     (
         grads,
         weight,
-        whole,
+        mine,
+        theirs,
         stats_first,
         residual_grad,
         mask_ref,
@@ -600,19 +644,31 @@
         grad_stack,
         product,
         value,
-    ) = refs[-15:]
-    conv_back(place, grads, weight, grad_stack, product, value)
+        whole,
+    ) = refs[-17:]
+    join_halves(place, mine, theirs, whole)
     own, other = half_offsets(place)
     mask = mask_ref[0]
     count = count_of(mask)
     gain, bias = params[:, 0:1], params[:, 1:2]
-    mean, factor = stats_first[0, :, 0:1], stats_first[0, :, 1:2]
-    normed = (whole[0].astype(WIDE) - mean) * factor
-    hidden = normed * gain + bias
-    delta = value[...] * mask * silu_slope(hidden)
-    value[...] = delta
-    plain = jnp.sum(delta, axis=1, keepdims=True)
-    weighted = jnp.sum(delta * normed, axis=1, keepdims=True)
+    columns = columns_of(stats_first[0])
+    mean, factor = columns[:, 0:1], columns[:, 1:2]
+
+    def normed_of(span):
+        return (whole[:, span].astype(WIDE) - mean) * factor
+
+    plain, weighted = conv_back(
+        place,
+        grads,
+        weight,
+        grad_stack,
+        product,
+        value,
+        lambda normed: silu_slope(normed * gain + bias),
+        mask,
+        normed_of,
+    )
+    normed = normed_of(slice(None))
     sums = group_sums(member[...], lane_pair(gain * plain, gain * weighted))
     first_sum, second_sum = sums[:, 0:1] / count, sums[:, 1:2] / count
     value[...] = residual_grad[0].astype(WIDE) + factor * (
@@ -1040,7 +1096,6 @@
     member_in = (member, fixed(C, C))
     image_low = (shape(images, C, PIX, dtype=LOW), per_image(C, PIX))
     image_wide = (shape(images, C, PIX), per_image(C, PIX))
-    image_small = (shape(images, C, 128), per_image(C, 128))
     image_rows = (shape(images, 8, C), per_image(8, C))
     weight_out = (shape(TAPS, TAPS, dtype=LOW), fixed(TAPS, TAPS))
     stack_out = (shape(TAPS // 2, images * PIX, dtype=LOW), per_columns(TAPS // 2, PIX))
@@ -1058,10 +1113,10 @@
             params_in,
             member_in,
         ],
-        [image_low, stack_out, stack_out, image_small],
+        [stack_out, stack_out, image_rows],
         [value_scratch],
     )
-    whole, first_low, first_high, stats_whole = prepared
+    first_low, first_high, stats_whole = prepared
     cots = others(after(cotangent, first_one))
     first_pieces = first_pieces + gather_three(after(first_pieces, first_low))
     mine, side = after(second_one, first_low)
@@ -1075,9 +1130,9 @@
             mask_in,
             member_in,
             (first_pieces, [fixed(PIECE, TAPS)] * 8),
-            (after([first_low, first_high], second_one, cots, embed_parts), [per_columns(TAPS // 2, PIX)] * 2),
+            (after([first_low, first_high], second_one, cots, embed_parts, steps_row), [per_columns(TAPS // 2, PIX)] * 2),
         ],
-        [image_wide, image_small, weight_out],
+        [image_wide, image_rows, weight_out],
         [value_scratch, product_scratch],
     )
     second_pieces = gather_two(second_one)
@@ -1090,14 +1145,16 @@
         images,
         [
             (after(second_normed, bundle_one), per_image(C, PIX)),
-            (whole, per_image(C, PIX)),
+            (stats_first, per_image(8, C)),
+            (features, own_image(HALF, PIX)),
+            (theirs, per_image(HALF, PIX)),
             (embed_parts, fixed(2, TAPS, 128)),
             mask_in,
             params_in,
             member_in,
             (second_pieces, [fixed(PIECE, 2 * SECOND)] * 8),
         ],
-        [input_out, input_out, image_wide, image_small],
+        [input_out, input_out, image_wide, image_rows],
         [
             pltpu.VMEM((TAPS, TAPS), LOW),
             pltpu.VMEM((2, 2, TAPS, 128), LOW),
@@ -1116,7 +1173,7 @@
         images,
         [
             (residual, per_image(C, PIX)),
-            (stats_second, per_image(C, 128)),
+            (stats_second, per_image(8, C)),
             (cotangent, own_image(HALF, PIX)),
             (their_cots, per_image(HALF, PIX)),
             mask_in,
@@ -1170,8 +1227,7 @@
             (after(second_grad, joint), per_image(C, PIX)),
             (second_pieces, [fixed(PIECE, 2 * SECOND)] * 8),
             (second_normed, per_image(C, PIX)),
-            (stats_first, per_image(C, 128)),
-            (stats_second, per_image(C, 128)),
+            (stats_second, per_image(8, C)),
             mask_in,
             params_in,
             member_in,
@@ -1203,8 +1259,9 @@
             + [
                 (back_grad, per_image(C, PIX, first=image)),
                 (first_weight, fixed(TAPS, TAPS)),
-                (whole, per_image(C, PIX, first=image)),
-                (stats_whole, per_image(C, 128, first=image)),
+                (features, own_image(HALF, PIX, first=image)),
+                (theirs, per_image(HALF, PIX, first=image)),
+                (stats_whole, per_image(8, C, first=image)),
                 (second_grad, per_image(C, PIX, first=image)),
                 (validity, per_image(1, PIX, first=image)),
                 params_in,
@@ -1216,7 +1273,7 @@
                 (shape(1, HALF, PIX, dtype=LOW), per_image(HALF, PIX)),
                 (small_shape, whole_array(small_shape)),
             ],
-            back_scratch,
+            back_scratch + [pltpu.VMEM((C, PIX), LOW)],
             {1: 0} if carried else None,
         )
         smalls.append(small)
@@ -1248,7 +1305,8 @@
         cost=1,
     )
 
-    message = merge([message] + [swap(message, m, 0) for m in (4, 2, 6)])
+    message = merge([message, swap(message, 4, 0)])
+    message = merge([message, swap(message, 2, 0)])
     one, two = after(message[:, :HALF], input_theirs[-1]), message[:, HALF:]
     own, away = jnp.where(left, one, two), jnp.where(left, two, one)
     message = merge([own, swap(away, 0, 1), swap(own, 8, 0), swap(away, 8, 1)])

time: 253 us -> 252 us (level)
  local copies, waits for them, and re-layouts: 22.1 us -> 17.5 us
    unnamed x136 -> x127, local copies, waits for them, and re-layouts: 11.9 us -> 9.21 us
    ppermute x53 -> x52, waiting for transfers between devices: 19.1 us -> 20.5 us  [swap(): return lax.ppermute(value, ('dp', 'chan'), pairs)]
    ppermute x53 -> x52, starting transfers between devices: 51.9 us -> 52.6 us  [swap(): return lax.ppermute(value, ('dp', 'chan'), pairs)]
  transfers between devices with their start and end apart: 53 -> 52, of which waited for: 12 -> 13; matrix products, arithmetic and copies ran while one was open for 6% -> 5% of each run, Pallas kernels for 33% -> 33%
where the time goes in v2:
time: 252 us; the launch traced here: 248 us
  Pallas kernels  148 us (59%)
  starting transfers between devices  52.6 us (21%)
  waiting for transfers between devices  20.5 us (8%)
  local copies, waits for them, and re-layouts  17.5 us (7%)
  other arithmetic  5.76 us (2%)
    pallas_call x17, Pallas kernels, run(): pl.pallas_call(body, grid_spec=pltpu.PrefetchScalarGridSpec(num_scalar_pr...  148 us
    ppermute x52, starting transfers between devices, swap(): return lax.ppermute(value, ('dp', 'chan'), pairs)  52.6 us
    ppermute x52, waiting for transfers between devices, swap(): return lax.ppermute(value, ('dp', 'chan'), pairs)  20.5 us
    unnamed x127, local copies, waits for them, and re-layouts  9.21 us
  transfers between devices with their start and end apart: 52, of which 13 were waited for; matrix products, arithmetic and copies ran while one was open for 5% of the time, Pallas kernels for 33%

profile of v2, /device:TPU:0, one launch (start us, length us, event | category | flops | bytes accessed | tf_op | source)
XLA Modules:
  0.0 247.6 jit_solution(6545238907542860096)
XLA Ops:
  1.9 4.1 %collective-permute-start.1 = (bf16[72,576]{1,0:T(8,128)(2,1)S(1)}, bf16[72,576]{1,0:T(8,128)(2,1)S(1)}, u32[]{:S(2)}, u32[]{:S(2)}) collective-permute-start(bf16[72,576]{1,0:T(8,128)(2,1)S(1)} %reshape.352), channel_id=1, source_target_pairs={{0,16},{1,17},{2,18},{3,19},{4,20},{5,21},{6,22},{7,23},{8,24},{9,... | collective-permute-start | bytes 248840 | tf_op jit(solution)/shard_map/ppermute | solution.py:928
  6.0 1.3 collective-permute-start.2
  9.1 2.1 constant_dynamic-slice_fusion.1
  11.2 1.7 collective-permute-start.6
  14.4 2.6 %collective-permute-start.11 = (bf16[72,1088]{1,0:T(8,128)(2,1)}, bf16[72,1088]{1,0:T(8,128)(2,1)}, u32[]{:S(2)}, u32[]{:S(2)}) collective-permute-start(bf16[72,1088]{1,0:T(8,128)(2,1)} %concatenate.81), channel_id=1, source_target_pairs={{0,16},{1,17},{2,18},{3,19},{4,20},{5,21},{6,22},{7,23},{8,24},{9,... | collective-permute-start | bytes 470024 | tf_op jit(solution)/shard_map/ppermute | solution.py:928
  18.5 1.6 collective-permute-start.3
  20.2 1.5 collective-permute-start.4
  28.5 4.1 %collective-permute-done.6.refs_1_.refs_3_.refs_4_ = bf16[2,192,1024]{2,1,0:T(8,128)(2,1)S(1)} collective-permute-done((bf16[2,192,1024]{2,1,0:T(8,128)(2,1)}, bf16[2,192,1024]{2,1,0:T(8,128)(2,1)S(1)}, u32[]{:S(2)}, u32[]{:S(2)}) %collective-permute-start.6) | collective-permute-done | bytes 786464 | tf_op jit(solution)/shard_map/ppermute | solution.py:928
  32.6 5.3 %shard_map.196 = (bf16[576,2048]{1,0:T(8,128)(2,1)S(1)}, bf16[576,2048]{1,0:T(8,128)(2,1)S(1)}, f32[2,8,384]{2,1,0:T(8,128)S(1)}) custom-call(s32[19]{0:T(128)S(1)} %pad_add_fusion.place, bf16[4,192,1024]{2,1,0:T(8,128)(2,1)S(1)} %copy-done.6, bf16[2,192,1024]{2,1,0:T(8,128)(2,1)S(1)} %collective-permute-done.6.refs_1_.refs_3_.refs_4_, ...), custom_call_target="tpu_custom_call" | custom-call | flops 8000000000 | bytes 1048576 | tf_op jit(solution)/shard_map/pallas_call | solution.py:829
  37.9 1.2 collective-permute-done.12
  41.0 1.5 collective-permute-start.14
  42.5 1.5 collective-permute-start.15
  44.0 10.9 %shard_map.197 = (f32[2,384,1024]{2,1,0:T(8,128)S(1)}, f32[2,8,384]{2,1,0:T(8,128)S(1)}, bf16[1152,1152]{1,0:T(8,128)(2,1)S(1)}) custom-call(s32[19]{0:T(128)S(1)} %pad_add_fusion.place, f32[2,1,1024]{2,1,0:T(1,128)S(1)} %reshape.350.refs_2_.refs_0_.refs_5_.refs_4_.refs_11_.refs_6_.refs_7_, ...), custom_call_target="tpu_custom_call" | custom-call | flops 8000000000 | bytes 1048576 | tf_op jit(solution)/shard_map/pallas_call | solution.py:829
  55.0 1.7 copy-done.34
  56.6 1.5 copy-done.36
  58.7 4.5 %collective-permute-done.14.refs_10_.refs_3_ = bf16[144,1664]{1,0:T(8,128)(2,1)S(1)} collective-permute-done((bf16[144,1664]{1,0:T(8,128)(2,1)S(1)}, bf16[144,1664]{1,0:T(8,128)(2,1)S(1)}, u32[]{:S(2)}, u32[]{:S(2)}) %collective-permute-start.14) | collective-permute-done | bytes 479264 | tf_op jit(solution)/shard_map/ppermute | solution.py:928
  63.2 1.5 collective-permute-done.15.refs_11_.refs_4_
  66.8 1.5 collective-permute-start.22
  71.1 18.2 %shard_map.198 = (bf16[192,2048]{1,0:T(8,128)(2,1)}, bf16[192,2048]{1,0:T(8,128)(2,1)}, f32[2,384,1024]{2,1,0:T(8,128)}, f32[2,8,384]{2,1,0:T(8,128)}) custom-call(s32[19]{0:T(128)} %copy-done.12, f32[2,384,1024]{2,1,0:T(8,128)} %copy-done.34, f32[2,8,384]{2,1,0:T(8,128)} %copy-done.42, bf16[4,192,1024]{2,1,0:T(8,128)(2,1)} %refs_3_.1, ...), custom_call_target="tpu_custom_call" | custom-call | flops 8000000000 | bytes 1048576 | tf_op jit(solution)/shard_map/pallas_call | solution.py:829
  92.4 65.6 %shard_map.199 = (bf16[4,192,1024]{2,1,0:T(8,128)(2,1)}, bf16[2,192,1024]{2,1,0:T(8,128)(2,1)}, bf16[2,384,1024]{2,1,0:T(8,128)(2,1)}, f32[256,1152]{1,0:T(8,128...) custom-call(s32[19]{0:T(128)} %copy-done.12, f32[2,384,1024]{2,1,0:T(8,128)} %get-tuple-element.106.refs_0_, ...), custom_call_target="tpu_custom_call" | custom-call | flops 60000002048 | bytes 1048576 | tf_op jit(solution)/shard_map/pallas_call | solution.py:829
  158.9 1.2 collective-permute-start.31
  160.1 1.4 copy-done.16
  161.5 1.1 copy-done.39
  162.6 4.0 %shard_map.200.refs_2_ = f32[576,1152]{1,0:T(8,128)S(1)} custom-call(s32[19]{0:T(128)S(1)} %copy-done.13, bf16[2,384,1024]{2,1,0:T(8,128)(2,1)S(1)} %copy-done.16, bf16[192,2048]{1,0:T(8,128)(2,1)S(1)} %copy-done.39), custom_call_target="tpu_custom_call" | custom-call | flops 8000000000 | bytes 1048576 | tf_op jit(solution)/shard_map/pallas_call | solution.py:829
  166.8 4.0 %shard_map.201 = (f32[208,1152]{1,0:T(8,128)S(1)}, bf16[208,1152]{1,0:T(8,128)(2,1)S(1)}, bf16[208,1152]{1,0:T(8,128)(2,1)S(1)}, bf16[208,1152]{1,0:T(8,128)(2,1)S(1)}) custom-call(s32[19]{0:T(128)S(1)} %copy-done.13, bf16[2,384,1024]{2,1,0:T(8,128)(2,1)S(1)} %collective-permute-done.28.refs_0_, bf16[192,2048]{1,0:T(8,128)(2,1)S(1)} %collective-permute-done.29.refs_1_, ...), custom_call_target="tpu_custom_call" | custom-call | flops 8000000000 | bytes 1048576 | tf_op jit(solution)/shard_map/pallas_call | solution.py:829
  171.7 1.5 collective-permute-start.34
  173.3 1.1 collective-permute-start.35
  174.5 11.4 %shard_map.202 = (bf16[2,384,1024]{2,1,0:T(8,128)(2,1)S(1)}, f32[2,8,384]{2,1,0:T(8,128)S(1)}) custom-call(s32[19]{0:T(128)S(1)} %copy-done.13, bf16[2,384,1024]{2,1,0:T(8,128)(2,1)S(1)} %copy-done.17, bf16[144,1664]{1,0:T(8,128)(2,1)S(1)} %copy-done.5, bf16[144,1664]{1,0:T(8,128)(2,1)S(1)} %copy-done.21, bf16[144,1664]{1,0:T(8,128)(2,1)S(1)} %copy-done.23, ...), custom_call_target="tpu_custom_call" | custom-call | flops 8000000000 | bytes 1048576 | tf_op jit(solution)/shard_map/pallas_call | solution.py:829
  186.1 7.0 %shard_map.203 = (bf16[576,1152]{1,0:T(8,128)(2,1)S(1)}, f32[576,1152]{1,0:T(8,128)S(1)}) custom-call(s32[19]{0:T(128)S(1)} %copy-done.13, bf16[2,384,1024]{2,1,0:T(8,128)(2,1)S(1)} %get-tuple-element.145.refs_0_.refs_1_, bf16[576,2048]{1,0:T(8,128)(2,1)S(1)} %copy-done.1, bf16[576,2048]{1,0:T(8,128)(2,1)S(1)} %copy-done.3), custom_call_target="tpu_custom_call" | custom-call | flops 1000000000 | bytes 1048576 | tf_op jit(solution)/shard_map/pallas_call | solution.py:829
  193.2 1.4 collective-permute-done.34.refs_2_
  195.5 1.1 collective-permute-start.36
  198.6 1.3 collective-permute-start.40
  199.9 1.2 collective-permute-start.41
  201.0 6.8 %shard_map.206 = (f32[4,192,1024]{2,1,0:T(8,128)}, bf16[1,192,1024]{2,1,0:T(8,128)(2,1)S(1)}, f32[8,384]{1,0:T(8,128)S(1)}) custom-call(s32[19]{0:T(128)S(1)} %copy-done.13, bf16[2,384,1024]{2,1,0:T(8,128)(2,1)S(1)} %get-tuple-element.145.refs_0_.refs_1_, bf16[1152,1152]{1,0:T(8,128)(2,1)S(1)} %copy-done.37, bf16[4,192,1024]{2,1,0:T(8,128)(2,1)S(1)} %copy-done.7, ...), custom_call_target="tpu_custom_call" | custom-call | flops 8000000000 | bytes 1048576 | tf_op jit(solution)/shard_map/pallas_call | solution.py:829
  208.4 3.2 %collective-permute-start.45 = (bf16[104,576]{1,0:T(8,128)(2,1)S(1)}, bf16[104,576]{1,0:T(8,128)(2,1)S(1)}, u32[]{:S(2)}, u32[]{:S(2)}) collective-permute-start(bf16[104,576]{1,0:T(8,128)(2,1)S(1)} %get-tuple-element.144), channel_id=1, source_target_pairs={{0,16},{1,17},{2,18},{3,19},{4,20},{5,21},{6,22},{7,23},{8,24},{9,... | collective-permute-start | bytes 359432 | tf_op jit(solution)/shard_map/ppermute | solution.py:928
  211.7 1.5 collective-permute-start.37
  213.2 7.0 %shard_map.208 = (f32[4,192,1024]{2,1,0:T(8,128)}, bf16[1,192,1024]{2,1,0:T(8,128)(2,1)S(1)}, f32[16,384]{1,0:T(8,128)S(1)}) custom-call(s32[19]{0:T(128)S(1)} %copy-done.13, f32[4,192,1024]{2,1,0:T(8,128)} %get-tuple-element.140.refs_0_, bf16[2,384,1024]{2,1,0:T(8,128)(2,1)S(1)} %get-tuple-element.145.refs_0_.refs_1_, ...), custom_call_target="tpu_custom_call", output_to_operand_aliasing={{0}: (1, {})} | custom-call | flops 8000000000 | bytes 1048576 | tf_op jit(solution)/shard_map/pallas_call | solution.py:829
  220.2 1.2 collective-permute-done.37.refs_1_
  222.9 1.6 collective-permute-start.42
  224.8 2.5 %collective-permute-start.44 = (bf16[72,576]{1,0:T(8,128)(2,1)S(1)}, bf16[72,576]{1,0:T(8,128)(2,1)S(1)}, u32[]{:S(2)}, u32[]{:S(2)}) collective-permute-start(bf16[72,576]{1,0:T(8,128)(2,1)S(1)} %get-tuple-element.154), channel_id=1, source_target_pairs={{0,17},{1,16},{2,19},{3,18},{4,21},{5,20},{6,23},{7,22},{8,25},{9,... | collective-permute-start | bytes 248840 | tf_op jit(solution)/shard_map/ppermute | solution.py:928
  227.4 1.2 collective-permute-start.47
  228.6 1.3 shard_map.212
  231.4 1.6 collective-permute-start.48
  233.0 1.8 shard_map.209
  235.8 1.8 collective-permute-start.49
  237.6 2.5 %collective-permute-start.51 = (f32[72,192]{1,0:T(8,128)S(1)}, f32[72,192]{1,0:T(8,128)S(1)}, u32[]{:S(2)}, u32[]{:S(2)}) collective-permute-start(f32[72,192]{1,0:T(8,128)S(1)} %get-tuple-element.219), channel_id=1, source_target_pairs={{0,17},{1,16},{2,19},{3,18},{4,21},{5,20},{6,23},{7,22},{8,25},{9,... | collective-permute-start | bytes 165896 | tf_op jit(solution)/shard_map/ppermute | solution.py:928
  240.3 1.3 shard_map.211
  241.7 3.7 %collective-permute-done.50 = f32[72,192]{1,0:T(8,128)S(1)} collective-permute-done((f32[72,192]{1,0:T(8,128)S(1)}, f32[72,192]{1,0:T(8,128)S(1)}, u32[]{:S(2)}, u32[]{:S(2)}) %collective-permute-start.50) | collective-permute-done | bytes 55328 | tf_op jit(solution)/shard_map/ppermute | solution.py:928
  (300 shorter events, 35.0 us)
Async XLA Ops:
  1.9 16.4 %collective-permute-start.1 = (bf16[72,576]{1,0:T(8,128)(2,1)S(1)}, bf16[72,576]{1,0:T(8,128)(2,1)S(1)}, u32[]{:S(2)}, u32[]{:S(2)}) collective-permute-start(bf16[72,576]{1,0:T(8,128)(2,1)S(1)} %reshape.352), channel_id=1, source_target_pairs={{0,16},{1,17},{2,18},{3,19},{4,20},{5,21},{6,22},{7,23},{8,24},{9,... | collective-permute-start | bytes 248840 | tf_op jit(solution)/shard_map/ppermute | solution.py:928
  6.0 12.3 %collective-permute-start.2 = (bf16[72,576]{1,0:T(8,128)(2,1)S(1)}, bf16[72,576]{1,0:T(8,128)(2,1)S(1)}, u32[]{:S(2)}, u32[]{:S(2)}) collective-permute-start(bf16[72,576]{1,0:T(8,128)(2,1)S(1)} %reshape.352), channel_id=1, source_target_pairs={{0,17},{1,16},{2,19},{3,18},{4,21},{5,20},{6,23},{7,22},{8,25},{9,... | collective-permute-start | bytes 248840 | tf_op jit(solution)/shard_map/ppermute | solution.py:928
  8.8 9.6 %collective-permute-start = (bf16[80,576]{1,0:T(8,128)(2,1)S(1)}, bf16[80,576]{1,0:T(8,128)(2,1)S(1)}, u32[]{:S(2)}, u32[]{:S(2)}) collective-permute-start(bf16[80,576]{1,0:T(8,128)(2,1)S(1)} %pad_maximum_fusion.9), channel_id=1, source_target_pairs={{0,1},{1,0},{2,3},{3,2},{4,5},{5,4},{6,7},{7,6},{8,9},{9,8},{10,11... | collective-permute-start | bytes 276488 | tf_op jit(solution)/shard_map/ppermute | solution.py:928
  11.2 21.4 %collective-permute-start.6 = (bf16[2,192,1024]{2,1,0:T(8,128)(2,1)}, bf16[2,192,1024]{2,1,0:T(8,128)(2,1)S(1)}, u32[]{:S(2)}, u32[]{:S(2)}) collective-permute-start(bf16[2,192,1024]{2,1,0:T(8,128)(2,1)} %constant_dynamic-slice_fusion.1), channel_id=1, source_target_pairs={{0,1},{1,0},{2,3},{3,2},{4,5},{5,4},{6,7},{7,6},{8,9},{9,8},{10,11... | collective-permute-start | bytes 2359304 | tf_op jit(solution)/shard_map/ppermute | solution.py:928
  14.4 12.5 %collective-permute-start.11 = (bf16[72,1088]{1,0:T(8,128)(2,1)}, bf16[72,1088]{1,0:T(8,128)(2,1)}, u32[]{:S(2)}, u32[]{:S(2)}) collective-permute-start(bf16[72,1088]{1,0:T(8,128)(2,1)} %concatenate.81), channel_id=1, source_target_pairs={{0,16},{1,17},{2,18},{3,19},{4,20},{5,21},{6,22},{7,23},{8,24},{9,... | collective-permute-start | bytes 470024 | tf_op jit(solution)/shard_map/ppermute | solution.py:928
  18.5 20.6 %collective-permute-start.3 = (bf16[144,1152]{1,0:T(8,128)(2,1)S(1)}, bf16[144,1152]{1,0:T(8,128)(2,1)S(1)}, u32[]{:S(2)}, u32[]{:S(2)}) collective-permute-start(bf16[144,1152]{1,0:T(8,128)(2,1)S(1)} %bitcast.82), channel_id=1, source_target_pairs={{0,8},{1,9},{2,10},{3,11},{4,12},{5,13},{6,14},{7,15},{8,0},{9,1},... | collective-permute-start | bytes 995336 | tf_op jit(solution)/shard_map/ppermute | solution.py:928
  20.2 19.0 %collective-permute-start.4 = (bf16[144,1152]{1,0:T(8,128)(2,1)S(1)}, bf16[144,1152]{1,0:T(8,128)(2,1)S(1)}, u32[]{:S(2)}, u32[]{:S(2)}) collective-permute-start(bf16[144,1152]{1,0:T(8,128)(2,1)S(1)} %bitcast.83), channel_id=1, source_target_pairs={{0,4},{1,5},{2,6},{3,7},{4,0},{5,1},{6,2},{7,3},{8,12},{9,13},{10,... | collective-permute-start | bytes 995336 | tf_op jit(solution)/shard_map/ppermute | solution.py:928
  21.7 17.4 %collective-permute-start.5 = (bf16[144,1152]{1,0:T(8,128)(2,1)S(1)}, bf16[144,1152]{1,0:T(8,128)(2,1)S(1)}, u32[]{:S(2)}, u32[]{:S(2)}) collective-permute-start(bf16[144,1152]{1,0:T(8,128)(2,1)S(1)} %bitcast.84), channel_id=1, source_target_pairs={{0,12},{1,13},{2,14},{3,15},{4,8},{5,9},{6,10},{7,11},{8,4},{9,5},... | collective-permute-start | bytes 995336 | tf_op jit(solution)/shard_map/ppermute | solution.py:928
  27.9 11.2 %collective-permute-start.12 = (bf16[144,1088]{1,0:T(8,128)(2,1)S(1)}, bf16[144,1088]{1,0:T(8,128)(2,1)S(1)}, u32[]{:S(2)}, u32[]{:S(2)}) collective-permute-start(bf16[144,1088]{1,0:T(8,128)(2,1)S(1)} %bitcast.87), channel_id=1, source_target_pairs={{0,1},{1,0},{2,3},{3,2},{4,5},{5,4},{6,7},{7,6},{8,9},{9,8},{10,11... | collective-permute-start | bytes 940040 | tf_op jit(solution)/shard_map/ppermute | solution.py:928
  39.1 1.9 collective-permute-start.10
  39.2 3.3 %collective-permute-start.7 = (bf16[144,1152]{1,0:T(8,128)(2,1)S(1)}, bf16[144,1152]{1,0:T(8,128)(2,1)S(1)}, u32[]{:S(2)}, u32[]{:S(2)}) collective-permute-start(bf16[144,1152]{1,0:T(8,128)(2,1)S(1)} %bitcast.85), channel_id=1, source_target_pairs={{0,2},{1,3},{2,0},{3,1},{4,6},{5,7},{6,4},{7,5},{8,10},{9,11},{10,... | collective-permute-start | bytes 995336 | tf_op jit(solution)/shard_map/ppermute | solution.py:928
  39.7 4.3 %collective-permute-start.8 = (bf16[144,1152]{1,0:T(8,128)(2,1)S(1)}, bf16[144,1152]{1,0:T(8,128)(2,1)S(1)}, u32[]{:S(2)}, u32[]{:S(2)}) collective-permute-start(bf16[144,1152]{1,0:T(8,128)(2,1)S(1)} %collective-permute-done.3.refs_3_), channel_id=1, source_target_pairs={{0,2},{1,3},{2,0},{3,1},{4,6},{5,7},{6,4},{7,5},{8,10},{9,11},{10,... | collective-permute-start | bytes 995336 | tf_op jit(solution)/shard_map/ppermute | solution.py:928
  39.8 4.2 %collective-permute-start.9 = (bf16[144,1152]{1,0:T(8,128)(2,1)S(1)}, bf16[144,1152]{1,0:T(8,128)(2,1)S(1)}, u32[]{:S(2)}, u32[]{:S(2)}) collective-permute-start(bf16[144,1152]{1,0:T(8,128)(2,1)S(1)} %collective-permute-done.4.refs_4_), channel_id=1, source_target_pairs={{0,2},{1,3},{2,0},{3,1},{4,6},{5,7},{6,4},{7,5},{8,10},{9,11},{10,... | collective-permute-start | bytes 995336 | tf_op jit(solution)/shard_map/ppermute | solution.py:928
  40.4 18.3 %collective-permute-start.13 = (bf16[144,1664]{1,0:T(8,128)(2,1)S(1)}, bf16[144,1664]{1,0:T(8,128)(2,1)S(1)}, u32[]{:S(2)}, u32[]{:S(2)}) collective-permute-start(bf16[144,1664]{1,0:T(8,128)(2,1)S(1)} %pad_maximum_fusion.refs_8_.refs_1_), channel_id=1, source_target_pairs={{0,8},{1,9},{2,10},{3,11},{4,12},{5,13},{6,14},{7,15},{8,0},{9,1},... | collective-permute-start | bytes 1437704 | tf_op jit(solution)/shard_map/ppermute | solution.py:928
  41.0 22.2 %collective-permute-start.14 = (bf16[144,1664]{1,0:T(8,128)(2,1)S(1)}, bf16[144,1664]{1,0:T(8,128)(2,1)S(1)}, u32[]{:S(2)}, u32[]{:S(2)}) collective-permute-start(bf16[144,1664]{1,0:T(8,128)(2,1)S(1)} %pad_maximum_fusion.refs_8_.refs_1_), channel_id=1, source_target_pairs={{0,4},{1,5},{2,6},{3,7},{4,0},{5,1},{6,2},{7,3},{8,12},{9,13},{10,... | collective-permute-start | bytes 1437704 | tf_op jit(solution)/shard_map/ppermute | solution.py:928
  42.5 22.1 %collective-permute-start.15 = (bf16[144,1664]{1,0:T(8,128)(2,1)S(1)}, bf16[144,1664]{1,0:T(8,128)(2,1)S(1)}, u32[]{:S(2)}, u32[]{:S(2)}) collective-permute-start(bf16[144,1664]{1,0:T(8,128)(2,1)S(1)} %pad_maximum_fusion.refs_8_.refs_1_), channel_id=1, source_target_pairs={{0,12},{1,13},{2,14},{3,15},{4,8},{5,9},{6,10},{7,11},{8,4},{9,5},... | collective-permute-start | bytes 1437704 | tf_op jit(solution)/shard_map/ppermute | solution.py:928
  64.7 2.1 collective-permute-start.16
  64.7 3.6 %collective-permute-start.17 = (bf16[144,1664]{1,0:T(8,128)(2,1)S(1)}, bf16[144,1664]{1,0:T(8,128)(2,1)S(1)}, u32[]{:S(2)}, u32[]{:S(2)}) collective-permute-start(bf16[144,1664]{1,0:T(8,128)(2,1)S(1)} %collective-permute-done.13.refs_9_.refs_2_), channel_id=1, source_target_pairs={{0,2},{1,3},{2,0},{3,1},{4,6},{5,7},{6,4},{7,5},{8,10},{9,11},{10,... | collective-permute-start | bytes 1437704 | tf_op jit(solution)/shard_map/ppermute | solution.py:928
  65.2 4.2 %collective-permute-start.18 = (bf16[144,1664]{1,0:T(8,128)(2,1)S(1)}, bf16[144,1664]{1,0:T(8,128)(2,1)S(1)}, u32[]{:S(2)}, u32[]{:S(2)}) collective-permute-start(bf16[144,1664]{1,0:T(8,128)(2,1)S(1)} %collective-permute-done.14.refs_10_.refs_3_), channel_id=1, source_target_pairs={{0,2},{1,3},{2,0},{3,1},{4,6},{5,7},{6,4},{7,5},{8,10},{9,11},{10,... | collective-permute-start | bytes 1437704 | tf_op jit(solution)/shard_map/ppermute | solution.py:928
  65.3 5.0 %collective-permute-start.19 = (bf16[144,1664]{1,0:T(8,128)(2,1)S(1)}, bf16[144,1664]{1,0:T(8,128)(2,1)S(1)}, u32[]{:S(2)}, u32[]{:S(2)}) collective-permute-start(bf16[144,1664]{1,0:T(8,128)(2,1)S(1)} %collective-permute-done.15.refs_11_.refs_4_), channel_id=1, source_target_pairs={{0,2},{1,3},{2,0},{3,1},{4,6},{5,7},{6,4},{7,5},{8,10},{9,11},{10,... | collective-permute-start | bytes 1437704 | tf_op jit(solution)/shard_map/ppermute | solution.py:928
  65.8 23.4 %collective-permute-start.21 = (bf16[144,512]{1,0:T(8,128)(2,1)S(1)}, bf16[144,512]{1,0:T(8,128)(2,1)S(1)}, u32[]{:S(2)}, u32[]{:S(2)}) collective-permute-start(bf16[144,512]{1,0:T(8,128)(2,1)S(1)} %pad_maximum_fusion.7.refs_7_), channel_id=1, source_target_pairs={{0,8},{1,9},{2,10},{3,11},{4,12},{5,13},{6,14},{7,15},{8,0},{9,1},... | collective-permute-start | bytes 442376 | tf_op jit(solution)/shard_map/ppermute | solution.py:928
  66.8 22.5 %collective-permute-start.22 = (bf16[144,512]{1,0:T(8,128)(2,1)S(1)}, bf16[144,512]{1,0:T(8,128)(2,1)S(1)}, u32[]{:S(2)}, u32[]{:S(2)}) collective-permute-start(bf16[144,512]{1,0:T(8,128)(2,1)S(1)} %pad_maximum_fusion.7.refs_7_), channel_id=1, source_target_pairs={{0,4},{1,5},{2,6},{3,7},{4,0},{5,1},{6,2},{7,3},{8,12},{9,13},{10,... | collective-permute-start | bytes 442376 | tf_op jit(solution)/shard_map/ppermute | solution.py:928
  68.3 21.0 %collective-permute-start.23 = (bf16[144,512]{1,0:T(8,128)(2,1)S(1)}, bf16[144,512]{1,0:T(8,128)(2,1)}, u32[]{:S(2)}, u32[]{:S(2)}) collective-permute-start(bf16[144,512]{1,0:T(8,128)(2,1)S(1)} %pad_maximum_fusion.7.refs_7_), channel_id=1, source_target_pairs={{0,12},{1,13},{2,14},{3,15},{4,8},{5,9},{6,10},{7,11},{8,4},{9,5},... | collective-permute-start | bytes 442376 | tf_op jit(solution)/shard_map/ppermute | solution.py:928
  69.4 21.0 %collective-permute-start.20 = (bf16[2,192,1024]{2,1,0:T(8,128)(2,1)}, bf16[2,192,1024]{2,1,0:T(8,128)(2,1)}, u32[]{:S(2)}, u32[]{:S(2)}) collective-permute-start(bf16[2,192,1024]{2,1,0:T(8,128)(2,1)} %constant_dynamic-slice_fusion), channel_id=1, source_target_pairs={{0,1},{1,0},{2,3},{3,2},{4,5},{5,4},{6,7},{7,6},{8,9},{9,8},{10,11... | collective-permute-start | bytes 2359304 | tf_op jit(solution)/shard_map/ppermute | solution.py:928
  158.0 8.6 %collective-permute-start.28 = (bf16[2,384,1024]{2,1,0:T(8,128)(2,1)}, bf16[2,384,1024]{2,1,0:T(8,128)(2,1)S(1)}, u32[]{:S(2)}, u32[]{:S(2)}) collective-permute-start(bf16[2,384,1024]{2,1,0:T(8,128)(2,1)} %get-tuple-element.125.refs_0_.refs_5_.refs_6_), channel_id=1, source_target_pairs={{0,2},{1,3},{2,0},{3,1},{4,6},{5,7},{6,4},{7,5},{8,10},{9,11},{10,... | collective-permute-start | bytes 4718600 | tf_op jit(solution)/shard_map/ppermute | solution.py:928
  158.4 8.2 %collective-permute-start.29 = (bf16[192,2048]{1,0:T(8,128)(2,1)}, bf16[192,2048]{1,0:T(8,128)(2,1)S(1)}, u32[]{:S(2)}, u32[]{:S(2)}) collective-permute-start(bf16[192,2048]{1,0:T(8,128)(2,1)} %get-tuple-element.115), channel_id=1, source_target_pairs={{0,2},{1,3},{2,0},{3,1},{4,6},{5,7},{6,4},{7,5},{8,10},{9,11},{10,... | collective-permute-start | bytes 2359304 | tf_op jit(solution)/shard_map/ppermute | solution.py:928
  158.6 8.0 %collective-permute-start.30 = (bf16[256,1152]{1,0:T(8,128)(2,1)}, bf16[256,1152]{1,0:T(8,128)(2,1)S(1)}, u32[]{:S(2)}, u32[]{:S(2)}) collective-permute-start(bf16[256,1152]{1,0:T(8,128)(2,1)} %get-tuple-element.118), channel_id=1, source_target_pairs={{0,2},{1,3},{2,0},{3,1},{4,6},{5,7},{6,4},{7,5},{8,10},{9,11},{10,... | collective-permute-start | bytes 1769480 | tf_op jit(solution)/shard_map/ppermute | solution.py:928
  158.9 27.0 %collective-permute-start.31 = (bf16[2,192,1024]{2,1,0:T(8,128)(2,1)}, bf16[2,192,1024]{2,1,0:T(8,128)(2,1)S(1)}, u32[]{:S(2)}, u32[]{:S(2)}) collective-permute-start(bf16[2,192,1024]{2,1,0:T(8,128)(2,1)} %get-tuple-element.124), channel_id=1, source_target_pairs={{0,1},{1,0},{2,3},{3,2},{4,5},{5,4},{6,7},{7,6},{8,9},{9,8},{10,11... | collective-permute-start | bytes 2359304 | tf_op jit(solution)/shard_map/ppermute | solution.py:928
  170.8 22.3 %collective-permute-start.33 = (bf16[208,1152]{1,0:T(8,128)(2,1)S(1)}, bf16[208,1152]{1,0:T(8,128)(2,1)S(1)}, u32[]{:S(2)}, u32[]{:S(2)}) collective-permute-start(bf16[208,1152]{1,0:T(8,128)(2,1)S(1)} %get-tuple-element.120), channel_id=1, source_target_pairs={{0,8},{1,9},{2,10},{3,11},{4,12},{5,13},{6,14},{7,15},{8,0},{9,1},... | collective-permute-start | bytes 1437704 | tf_op jit(solution)/shard_map/ppermute | solution.py:928
  171.7 22.8 %collective-permute-start.34 = (bf16[208,1152]{1,0:T(8,128)(2,1)S(1)}, bf16[208,1152]{1,0:T(8,128)(2,1)S(1)}, u32[]{:S(2)}, u32[]{:S(2)}) collective-permute-start(bf16[208,1152]{1,0:T(8,128)(2,1)S(1)} %get-tuple-element.121), channel_id=1, source_target_pairs={{0,4},{1,5},{2,6},{3,7},{4,0},{5,1},{6,2},{7,3},{8,12},{9,13},{10,... | collective-permute-start | bytes 1437704 | tf_op jit(solution)/shard_map/ppermute | solution.py:928
  173.3 21.3 %collective-permute-start.35 = (bf16[208,1152]{1,0:T(8,128)(2,1)S(1)}, bf16[208,1152]{1,0:T(8,128)(2,1)S(1)}, u32[]{:S(2)}, u32[]{:S(2)}) collective-permute-start(bf16[208,1152]{1,0:T(8,128)(2,1)S(1)} %get-tuple-element.122), channel_id=1, source_target_pairs={{0,12},{1,13},{2,14},{3,15},{4,8},{5,9},{6,10},{7,11},{8,4},{9,5},... | collective-permute-start | bytes 1437704 | tf_op jit(solution)/shard_map/ppermute | solution.py:928
  193.1 3.5 %collective-permute-start.32 = (bf16[576,1152]{1,0:T(8,128)(2,1)S(1)}, bf16[576,1152]{1,0:T(8,128)(2,1)S(1)}, u32[]{:S(2)}, u32[]{:S(2)}) collective-permute-start(bf16[576,1152]{1,0:T(8,128)(2,1)S(1)} %get-tuple-element.129), channel_id=1, source_target_pairs={{0,2},{1,3},{2,0},{3,1},{4,6},{5,7},{6,4},{7,5},{8,10},{9,11},{10,... | collective-permute-start | bytes 3981320 | tf_op jit(solution)/shard_map/ppermute | solution.py:928
  195.5 12.3 %collective-permute-start.36 = (bf16[208,576]{1,0:T(8,128)(2,1)S(1)}, bf16[208,576]{1,0:T(8,128)(2,1)S(1)}, u32[]{:S(2)}, u32[]{:S(2)}) collective-permute-start(bf16[208,576]{1,0:T(8,128)(2,1)S(1)} %get-tuple-element.136), channel_id=1, source_target_pairs={{0,1},{1,0},{2,3},{3,2},{4,5},{5,4},{6,7},{7,6},{8,9},{9,8},{10,11... | collective-permute-start | bytes 718856 | tf_op jit(solution)/shard_map/ppermute | solution.py:928
  197.5 24.5 %collective-permute-start.39 = (bf16[144,1152]{1,0:T(8,128)(2,1)S(1)}, bf16[144,1152]{1,0:T(8,128)(2,1)S(1)}, u32[]{:S(2)}, u32[]{:S(2)}) collective-permute-start(bf16[144,1152]{1,0:T(8,128)(2,1)S(1)} %get-tuple-element.131), channel_id=1, source_target_pairs={{0,8},{1,9},{2,10},{3,11},{4,12},{5,13},{6,14},{7,15},{8,0},{9,1},... | collective-permute-start | bytes 995336 | tf_op jit(solution)/shard_map/ppermute | solution.py:928
  198.6 23.4 %collective-permute-start.40 = (bf16[144,1152]{1,0:T(8,128)(2,1)S(1)}, bf16[144,1152]{1,0:T(8,128)(2,1)S(1)}, u32[]{:S(2)}, u32[]{:S(2)}) collective-permute-start(bf16[144,1152]{1,0:T(8,128)(2,1)S(1)} %get-tuple-element.132), channel_id=1, source_target_pairs={{0,4},{1,5},{2,6},{3,7},{4,0},{5,1},{6,2},{7,3},{8,12},{9,13},{10,... | collective-permute-start | bytes 995336 | tf_op jit(solution)/shard_map/ppermute | solution.py:928
  199.9 22.1 %collective-permute-start.41 = (bf16[144,1152]{1,0:T(8,128)(2,1)S(1)}, bf16[144,1152]{1,0:T(8,128)(2,1)S(1)}, u32[]{:S(2)}, u32[]{:S(2)}) collective-permute-start(bf16[144,1152]{1,0:T(8,128)(2,1)S(1)} %get-tuple-element.133), channel_id=1, source_target_pairs={{0,12},{1,13},{2,14},{3,15},{4,8},{5,9},{6,10},{7,11},{8,4},{9,5},... | collective-permute-start | bytes 995336 | tf_op jit(solution)/shard_map/ppermute | solution.py:928
  208.4 18.9 %collective-permute-start.45 = (bf16[104,576]{1,0:T(8,128)(2,1)S(1)}, bf16[104,576]{1,0:T(8,128)(2,1)S(1)}, u32[]{:S(2)}, u32[]{:S(2)}) collective-permute-start(bf16[104,576]{1,0:T(8,128)(2,1)S(1)} %get-tuple-element.144), channel_id=1, source_target_pairs={{0,16},{1,17},{2,18},{3,19},{4,20},{5,21},{6,22},{7,23},{8,24},{9,... | collective-permute-start | bytes 359432 | tf_op jit(solution)/shard_map/ppermute | solution.py:928
  211.7 9.8 %collective-permute-start.37 = (bf16[1,192,1024]{2,1,0:T(8,128)(2,1)S(1)}, bf16[1,192,1024]{2,1,0:T(8,128)(2,1)S(1)}, u32[]{:S(2)}, u32[]{:S(2)}) collective-permute-start(bf16[1,192,1024]{2,1,0:T(8,128)(2,1)S(1)} %get-tuple-element.149), channel_id=1, source_target_pairs={{0,1},{1,0},{2,3},{3,2},{4,5},{5,4},{6,7},{7,6},{8,9},{9,8},{10,11... | collective-permute-start | bytes 1179656 | tf_op jit(solution)/shard_map/ppermute | solution.py:928
  221.4 11.6 %collective-permute-start.38 = (bf16[1,192,1024]{2,1,0:T(8,128)(2,1)S(1)}, bf16[1,192,1024]{2,1,0:T(8,128)(2,1)S(1)}, u32[]{:S(2)}, u32[]{:S(2)}) collective-permute-start(bf16[1,192,1024]{2,1,0:T(8,128)(2,1)S(1)} %get-tuple-element.150), channel_id=1, source_target_pairs={{0,1},{1,0},{2,3},{3,2},{4,5},{5,4},{6,7},{7,6},{8,9},{9,8},{10,11... | collective-permute-start | bytes 1179656 | tf_op jit(solution)/shard_map/ppermute | solution.py:928
  222.0 2.8 %collective-permute-start.46 = (f32[16,384]{1,0:T(8,128)S(1)}, f32[16,384]{1,0:T(8,128)S(1)}, u32[]{:S(2)}, u32[]{:S(2)}) collective-permute-start(f32[16,384]{1,0:T(8,128)S(1)} %get-tuple-element.160), channel_id=1, source_target_pairs={{0,2},{1,3},{2,0},{3,1},{4,6},{5,7},{6,4},{7,5},{8,10},{9,11},{10,... | collective-permute-start | bytes 73736 | tf_op jit(solution)/shard_map/ppermute | solution.py:928
  222.9 17.2 %collective-permute-start.42 = (bf16[72,576]{1,0:T(8,128)(2,1)S(1)}, bf16[72,576]{1,0:T(8,128)(2,1)S(1)}, u32[]{:S(2)}, u32[]{:S(2)}) collective-permute-start(bf16[72,576]{1,0:T(8,128)(2,1)S(1)} %get-tuple-element.152), channel_id=1, source_target_pairs={{0,1},{1,0},{2,3},{3,2},{4,5},{5,4},{6,7},{7,6},{8,9},{9,8},{10,11... | collective-permute-start | bytes 248840 | tf_op jit(solution)/shard_map/ppermute | solution.py:928
  224.5 15.9 %collective-permute-start.43 = (bf16[72,576]{1,0:T(8,128)(2,1)S(1)}, bf16[72,576]{1,0:T(8,128)(2,1)S(1)}, u32[]{:S(2)}, u32[]{:S(2)}) collective-permute-start(bf16[72,576]{1,0:T(8,128)(2,1)S(1)} %get-tuple-element.153), channel_id=1, source_target_pairs={{0,16},{1,17},{2,18},{3,19},{4,20},{5,21},{6,22},{7,23},{8,24},{9,... | collective-permute-start | bytes 248840 | tf_op jit(solution)/shard_map/ppermute | solution.py:928
  224.8 15.5 %collective-permute-start.44 = (bf16[72,576]{1,0:T(8,128)(2,1)S(1)}, bf16[72,576]{1,0:T(8,128)(2,1)S(1)}, u32[]{:S(2)}, u32[]{:S(2)}) collective-permute-start(bf16[72,576]{1,0:T(8,128)(2,1)S(1)} %get-tuple-element.154), channel_id=1, source_target_pairs={{0,17},{1,16},{2,19},{3,18},{4,21},{5,20},{6,23},{7,22},{8,25},{9,... | collective-permute-start | bytes 248840 | tf_op jit(solution)/shard_map/ppermute | solution.py:928
  227.4 4.0 %collective-permute-start.47 = (f32[24,384]{1,0:T(8,128)S(1)}, f32[24,384]{1,0:T(8,128)S(1)}, u32[]{:S(2)}, u32[]{:S(2)}) collective-permute-start(f32[24,384]{1,0:T(8,128)S(1)} %pad_maximum_fusion.13), channel_id=1, source_target_pairs={{0,8},{1,9},{2,10},{3,11},{4,12},{5,13},{6,14},{7,15},{8,0},{9,1},... | collective-permute-start | bytes 110600 | tf_op jit(solution)/shard_map/ppermute | solution.py:928
  231.4 4.3 %collective-permute-start.48 = (f32[40,384]{1,0:T(8,128)S(1)}, f32[40,384]{1,0:T(8,128)S(1)}, u32[]{:S(2)}, u32[]{:S(2)}) collective-permute-start(f32[40,384]{1,0:T(8,128)S(1)} %pad_maximum_fusion.10), channel_id=1, source_target_pairs={{0,4},{1,5},{2,6},{3,7},{4,0},{5,1},{6,2},{7,3},{8,12},{9,13},{10,... | collective-permute-start | bytes 184328 | tf_op jit(solution)/shard_map/ppermute | solution.py:928
  235.8 5.8 %collective-permute-start.49 = (f32[72,192]{1,0:T(8,128)S(1)}, f32[72,192]{1,0:T(8,128)S(1)}, u32[]{:S(2)}, u32[]{:S(2)}) collective-permute-start(f32[72,192]{1,0:T(8,128)S(1)} %get-tuple-element.219), channel_id=1, source_target_pairs={{0,1},{1,0},{2,3},{3,2},{4,5},{5,4},{6,7},{7,6},{8,9},{9,8},{10,11... | collective-permute-start | bytes 165896 | tf_op jit(solution)/shard_map/ppermute | solution.py:928
  237.6 7.8 %collective-permute-start.51 = (f32[72,192]{1,0:T(8,128)S(1)}, f32[72,192]{1,0:T(8,128)S(1)}, u32[]{:S(2)}, u32[]{:S(2)}) collective-permute-start(f32[72,192]{1,0:T(8,128)S(1)} %get-tuple-element.219), channel_id=1, source_target_pairs={{0,17},{1,16},{2,19},{3,18},{4,21},{5,20},{6,23},{7,22},{8,25},{9,... | collective-permute-start | bytes 165896 | tf_op jit(solution)/shard_map/ppermute | solution.py:928
  240.1 5.3 %collective-permute-start.50 = (f32[72,192]{1,0:T(8,128)S(1)}, f32[72,192]{1,0:T(8,128)S(1)}, u32[]{:S(2)}, u32[]{:S(2)}) collective-permute-start(f32[72,192]{1,0:T(8,128)S(1)} %get-tuple-element.218), channel_id=1, source_target_pairs={{0,16},{1,17},{2,18},{3,19},{4,20},{5,21},{6,22},{7,23},{8,24},{9,... | collective-permute-start | bytes 165896 | tf_op jit(solution)/shard_map/ppermute | solution.py:928
  (67 other events, 546.5 us)

commit v3 on v2

--- a/solution.py
+++ b/solution.py
@@ -474,7 +474,7 @@
         )
         return carry
 
-    lax.fori_loop(0, C // HEAD, one_head, 0, unroll=3)
+    lax.fori_loop(0, C // HEAD, one_head, 0, unroll=6)
 
     value[...] = (residual[0] + dot(output[...], attended[...], NN)) * mask
     block_out[0] = value[pl.ds(own, HALF), :].astype(LOW)

time: 252 us -> 248 us (0.984)
  Pallas kernels: 148 us -> 144 us
    pallas_call x17, Pallas kernels: 148 us -> 144 us  [run(): pl.pallas_call(body, grid_spec=pltpu.PrefetchScalarGridSpec(num_scalar_pr...]
  transfers between devices with their start and end apart: 52 -> 52, of which waited for: 13 -> 13; matrix products, arithmetic and copies ran while one was open for 5% -> 5% of each run, Pallas kernels for 33% -> 34%
where the time goes in v3:
time: 248 us; the launch traced here: 244 us
  Pallas kernels  144 us (58%)
  starting transfers between devices  52.6 us (21%)
  waiting for transfers between devices  20.6 us (8%)
  local copies, waits for them, and re-layouts  17.5 us (7%)
  other arithmetic  5.76 us (2%)
    pallas_call x17, Pallas kernels, run(): pl.pallas_call(body, grid_spec=pltpu.PrefetchScalarGridSpec(num_scalar_pr...  144 us
    ppermute x52, starting transfers between devices, swap(): return lax.ppermute(value, ('dp', 'chan'), pairs)  52.6 us
    ppermute x52, waiting for transfers between devices, swap(): return lax.ppermute(value, ('dp', 'chan'), pairs)  20.6 us
    unnamed x127, local copies, waits for them, and re-layouts  9.21 us
  transfers between devices with their start and end apart: 52, of which 13 were waited for; matrix products, arithmetic and copies ran while one was open for 5% of the time, Pallas kernels for 34%

profile of v3, /device:TPU:0, one launch (start us, length us, event | category | flops | bytes accessed | tf_op | source)
XLA Modules:
  0.0 243.7 jit_solution(258297037054369239)
XLA Ops:
  1.9 4.1 %collective-permute-start.1 = (bf16[72,576]{1,0:T(8,128)(2,1)S(1)}, bf16[72,576]{1,0:T(8,128)(2,1)S(1)}, u32[]{:S(2)}, u32[]{:S(2)}) collective-permute-start(bf16[72,576]{1,0:T(8,128)(2,1)S(1)} %reshape.352), channel_id=1, source_target_pairs={{0,16},{1,17},{2,18},{3,19},{4,20},{5,21},{6,22},{7,23},{8,24},{9,... | collective-permute-start | bytes 248840 | tf_op jit(solution)/shard_map/ppermute | solution.py:928
  6.0 1.3 collective-permute-start.2
  9.1 2.1 constant_dynamic-slice_fusion.1
  11.2 1.7 collective-permute-start.6
  14.4 2.6 %collective-permute-start.11 = (bf16[72,1088]{1,0:T(8,128)(2,1)}, bf16[72,1088]{1,0:T(8,128)(2,1)}, u32[]{:S(2)}, u32[]{:S(2)}) collective-permute-start(bf16[72,1088]{1,0:T(8,128)(2,1)} %concatenate.81), channel_id=1, source_target_pairs={{0,16},{1,17},{2,18},{3,19},{4,20},{5,21},{6,22},{7,23},{8,24},{9,... | collective-permute-start | bytes 470024 | tf_op jit(solution)/shard_map/ppermute | solution.py:928
  18.5 1.6 collective-permute-start.3
  20.2 1.5 collective-permute-start.4
  28.5 4.1 %collective-permute-done.6.refs_1_.refs_3_.refs_4_ = bf16[2,192,1024]{2,1,0:T(8,128)(2,1)S(1)} collective-permute-done((bf16[2,192,1024]{2,1,0:T(8,128)(2,1)}, bf16[2,192,1024]{2,1,0:T(8,128)(2,1)S(1)}, u32[]{:S(2)}, u32[]{:S(2)}) %collective-permute-start.6) | collective-permute-done | bytes 786464 | tf_op jit(solution)/shard_map/ppermute | solution.py:928
  32.6 5.3 %shard_map.196 = (bf16[576,2048]{1,0:T(8,128)(2,1)S(1)}, bf16[576,2048]{1,0:T(8,128)(2,1)S(1)}, f32[2,8,384]{2,1,0:T(8,128)S(1)}) custom-call(s32[19]{0:T(128)S(1)} %pad_add_fusion.place, bf16[4,192,1024]{2,1,0:T(8,128)(2,1)S(1)} %copy-done.6, bf16[2,192,1024]{2,1,0:T(8,128)(2,1)S(1)} %collective-permute-done.6.refs_1_.refs_3_.refs_4_, ...), custom_call_target="tpu_custom_call" | custom-call | flops 8000000000 | bytes 1048576 | tf_op jit(solution)/shard_map/pallas_call | solution.py:829
  37.9 1.2 collective-permute-done.12
  41.0 1.5 collective-permute-start.14
  42.5 1.5 collective-permute-start.15
  44.0 10.9 %shard_map.197 = (f32[2,384,1024]{2,1,0:T(8,128)S(1)}, f32[2,8,384]{2,1,0:T(8,128)S(1)}, bf16[1152,1152]{1,0:T(8,128)(2,1)S(1)}) custom-call(s32[19]{0:T(128)S(1)} %pad_add_fusion.place, f32[2,1,1024]{2,1,0:T(1,128)S(1)} %reshape.350.refs_2_.refs_0_.refs_5_.refs_4_.refs_11_.refs_6_.refs_7_, ...), custom_call_target="tpu_custom_call" | custom-call | flops 8000000000 | bytes 1048576 | tf_op jit(solution)/shard_map/pallas_call | solution.py:829
  55.0 1.7 copy-done.34
  56.6 1.5 copy-done.36
  58.7 4.5 %collective-permute-done.14.refs_10_.refs_3_ = bf16[144,1664]{1,0:T(8,128)(2,1)S(1)} collective-permute-done((bf16[144,1664]{1,0:T(8,128)(2,1)S(1)}, bf16[144,1664]{1,0:T(8,128)(2,1)S(1)}, u32[]{:S(2)}, u32[]{:S(2)}) %collective-permute-start.14) | collective-permute-done | bytes 479264 | tf_op jit(solution)/shard_map/ppermute | solution.py:928
  63.2 1.5 collective-permute-done.15.refs_11_.refs_4_
  66.8 1.5 collective-permute-start.22
  71.1 18.4 %shard_map.198 = (bf16[192,2048]{1,0:T(8,128)(2,1)}, bf16[192,2048]{1,0:T(8,128)(2,1)}, f32[2,384,1024]{2,1,0:T(8,128)}, f32[2,8,384]{2,1,0:T(8,128)}) custom-call(s32[19]{0:T(128)} %copy-done.12, f32[2,384,1024]{2,1,0:T(8,128)} %copy-done.34, f32[2,8,384]{2,1,0:T(8,128)} %copy-done.42, bf16[4,192,1024]{2,1,0:T(8,128)(2,1)} %refs_3_.1, ...), custom_call_target="tpu_custom_call" | custom-call | flops 8000000000 | bytes 1048576 | tf_op jit(solution)/shard_map/pallas_call | solution.py:829
  92.6 61.6 %shard_map.199 = (bf16[4,192,1024]{2,1,0:T(8,128)(2,1)}, bf16[2,192,1024]{2,1,0:T(8,128)(2,1)}, bf16[2,384,1024]{2,1,0:T(8,128)(2,1)}, f32[256,1152]{1,0:T(8,128...) custom-call(s32[19]{0:T(128)} %copy-done.12, f32[2,384,1024]{2,1,0:T(8,128)} %get-tuple-element.106.refs_0_, ...), custom_call_target="tpu_custom_call" | custom-call | flops 60000002048 | bytes 1048576 | tf_op jit(solution)/shard_map/pallas_call | solution.py:829
  155.1 1.2 collective-permute-start.31
  156.3 1.4 copy-done.16
  157.7 1.1 copy-done.39
  158.8 4.0 %shard_map.200.refs_2_ = f32[576,1152]{1,0:T(8,128)S(1)} custom-call(s32[19]{0:T(128)S(1)} %copy-done.13, bf16[2,384,1024]{2,1,0:T(8,128)(2,1)S(1)} %copy-done.16, bf16[192,2048]{1,0:T(8,128)(2,1)S(1)} %copy-done.39), custom_call_target="tpu_custom_call" | custom-call | flops 8000000000 | bytes 1048576 | tf_op jit(solution)/shard_map/pallas_call | solution.py:829
  163.0 4.0 %shard_map.201 = (f32[208,1152]{1,0:T(8,128)S(1)}, bf16[208,1152]{1,0:T(8,128)(2,1)S(1)}, bf16[208,1152]{1,0:T(8,128)(2,1)S(1)}, bf16[208,1152]{1,0:T(8,128)(2,1)S(1)}) custom-call(s32[19]{0:T(128)S(1)} %copy-done.13, bf16[2,384,1024]{2,1,0:T(8,128)(2,1)S(1)} %collective-permute-done.28.refs_0_, bf16[192,2048]{1,0:T(8,128)(2,1)S(1)} %collective-permute-done.29.refs_1_, ...), custom_call_target="tpu_custom_call" | custom-call | flops 8000000000 | bytes 1048576 | tf_op jit(solution)/shard_map/pallas_call | solution.py:829
  167.9 1.5 collective-permute-start.34
  169.4 1.1 collective-permute-start.35
  170.7 11.4 %shard_map.202 = (bf16[2,384,1024]{2,1,0:T(8,128)(2,1)S(1)}, f32[2,8,384]{2,1,0:T(8,128)S(1)}) custom-call(s32[19]{0:T(128)S(1)} %copy-done.13, bf16[2,384,1024]{2,1,0:T(8,128)(2,1)S(1)} %copy-done.17, bf16[144,1664]{1,0:T(8,128)(2,1)S(1)} %copy-done.5, bf16[144,1664]{1,0:T(8,128)(2,1)S(1)} %copy-done.21, bf16[144,1664]{1,0:T(8,128)(2,1)S(1)} %copy-done.23, ...), custom_call_target="tpu_custom_call" | custom-call | flops 8000000000 | bytes 1048576 | tf_op jit(solution)/shard_map/pallas_call | solution.py:829
  182.2 7.0 %shard_map.203 = (bf16[576,1152]{1,0:T(8,128)(2,1)S(1)}, f32[576,1152]{1,0:T(8,128)S(1)}) custom-call(s32[19]{0:T(128)S(1)} %copy-done.13, bf16[2,384,1024]{2,1,0:T(8,128)(2,1)S(1)} %get-tuple-element.145.refs_0_.refs_1_, bf16[576,2048]{1,0:T(8,128)(2,1)S(1)} %copy-done.1, bf16[576,2048]{1,0:T(8,128)(2,1)S(1)} %copy-done.3), custom_call_target="tpu_custom_call" | custom-call | flops 1000000000 | bytes 1048576 | tf_op jit(solution)/shard_map/pallas_call | solution.py:829
  189.3 1.4 collective-permute-done.34.refs_2_
  193.6 1.1 collective-permute-start.39
  194.7 1.3 collective-permute-start.40
  196.0 1.2 collective-permute-start.41
  197.2 6.8 %shard_map.206 = (f32[4,192,1024]{2,1,0:T(8,128)}, bf16[1,192,1024]{2,1,0:T(8,128)(2,1)S(1)}, f32[8,384]{1,0:T(8,128)S(1)}) custom-call(s32[19]{0:T(128)S(1)} %copy-done.13, bf16[2,384,1024]{2,1,0:T(8,128)(2,1)S(1)} %get-tuple-element.145.refs_0_.refs_1_, bf16[1152,1152]{1,0:T(8,128)(2,1)S(1)} %copy-done.37, bf16[4,192,1024]{2,1,0:T(8,128)(2,1)S(1)} %copy-done.7, ...), custom_call_target="tpu_custom_call" | custom-call | flops 8000000000 | bytes 1048576 | tf_op jit(solution)/shard_map/pallas_call | solution.py:829
  204.6 3.2 %collective-permute-start.45 = (bf16[104,576]{1,0:T(8,128)(2,1)S(1)}, bf16[104,576]{1,0:T(8,128)(2,1)S(1)}, u32[]{:S(2)}, u32[]{:S(2)}) collective-permute-start(bf16[104,576]{1,0:T(8,128)(2,1)S(1)} %get-tuple-element.144), channel_id=1, source_target_pairs={{0,16},{1,17},{2,18},{3,19},{4,20},{5,21},{6,22},{7,23},{8,24},{9,... | collective-permute-start | bytes 359432 | tf_op jit(solution)/shard_map/ppermute | solution.py:928
  207.8 1.5 collective-permute-start.37
  209.3 7.0 %shard_map.208 = (f32[4,192,1024]{2,1,0:T(8,128)}, bf16[1,192,1024]{2,1,0:T(8,128)(2,1)S(1)}, f32[16,384]{1,0:T(8,128)S(1)}) custom-call(s32[19]{0:T(128)S(1)} %copy-done.13, f32[4,192,1024]{2,1,0:T(8,128)} %get-tuple-element.140.refs_0_, bf16[2,384,1024]{2,1,0:T(8,128)(2,1)S(1)} %get-tuple-element.145.refs_0_.refs_1_, ...), custom_call_target="tpu_custom_call", output_to_operand_aliasing={{0}: (1, {})} | custom-call | flops 8000000000 | bytes 1048576 | tf_op jit(solution)/shard_map/pallas_call | solution.py:829
  216.3 1.2 collective-permute-done.37.refs_1_
  219.0 1.6 collective-permute-start.42
  220.9 2.5 %collective-permute-start.44 = (bf16[72,576]{1,0:T(8,128)(2,1)S(1)}, bf16[72,576]{1,0:T(8,128)(2,1)S(1)}, u32[]{:S(2)}, u32[]{:S(2)}) collective-permute-start(bf16[72,576]{1,0:T(8,128)(2,1)S(1)} %get-tuple-element.154), channel_id=1, source_target_pairs={{0,17},{1,16},{2,19},{3,18},{4,21},{5,20},{6,23},{7,22},{8,25},{9,... | collective-permute-start | bytes 248840 | tf_op jit(solution)/shard_map/ppermute | solution.py:928
  223.5 1.2 collective-permute-start.47
  224.7 1.3 shard_map.212
  227.5 1.6 collective-permute-start.48
  229.1 1.8 shard_map.209
  232.0 1.8 collective-permute-start.49
  233.7 2.5 %collective-permute-start.51 = (f32[72,192]{1,0:T(8,128)S(1)}, f32[72,192]{1,0:T(8,128)S(1)}, u32[]{:S(2)}, u32[]{:S(2)}) collective-permute-start(f32[72,192]{1,0:T(8,128)S(1)} %get-tuple-element.219), channel_id=1, source_target_pairs={{0,17},{1,16},{2,19},{3,18},{4,21},{5,20},{6,23},{7,22},{8,25},{9,... | collective-permute-start | bytes 165896 | tf_op jit(solution)/shard_map/ppermute | solution.py:928
  236.4 1.3 shard_map.211
  237.8 3.7 %collective-permute-done.50 = f32[72,192]{1,0:T(8,128)S(1)} collective-permute-done((f32[72,192]{1,0:T(8,128)S(1)}, f32[72,192]{1,0:T(8,128)S(1)}, u32[]{:S(2)}, u32[]{:S(2)}) %collective-permute-start.50) | collective-permute-done | bytes 55328 | tf_op jit(solution)/shard_map/ppermute | solution.py:928
  (300 shorter events, 35.0 us)
Async XLA Ops:
  1.9 16.4 %collective-permute-start.1 = (bf16[72,576]{1,0:T(8,128)(2,1)S(1)}, bf16[72,576]{1,0:T(8,128)(2,1)S(1)}, u32[]{:S(2)}, u32[]{:S(2)}) collective-permute-start(bf16[72,576]{1,0:T(8,128)(2,1)S(1)} %reshape.352), channel_id=1, source_target_pairs={{0,16},{1,17},{2,18},{3,19},{4,20},{5,21},{6,22},{7,23},{8,24},{9,... | collective-permute-start | bytes 248840 | tf_op jit(solution)/shard_map/ppermute | solution.py:928
  6.0 12.3 %collective-permute-start.2 = (bf16[72,576]{1,0:T(8,128)(2,1)S(1)}, bf16[72,576]{1,0:T(8,128)(2,1)S(1)}, u32[]{:S(2)}, u32[]{:S(2)}) collective-permute-start(bf16[72,576]{1,0:T(8,128)(2,1)S(1)} %reshape.352), channel_id=1, source_target_pairs={{0,17},{1,16},{2,19},{3,18},{4,21},{5,20},{6,23},{7,22},{8,25},{9,... | collective-permute-start | bytes 248840 | tf_op jit(solution)/shard_map/ppermute | solution.py:928
  8.8 9.6 %collective-permute-start = (bf16[80,576]{1,0:T(8,128)(2,1)S(1)}, bf16[80,576]{1,0:T(8,128)(2,1)S(1)}, u32[]{:S(2)}, u32[]{:S(2)}) collective-permute-start(bf16[80,576]{1,0:T(8,128)(2,1)S(1)} %pad_maximum_fusion.9), channel_id=1, source_target_pairs={{0,1},{1,0},{2,3},{3,2},{4,5},{5,4},{6,7},{7,6},{8,9},{9,8},{10,11... | collective-permute-start | bytes 276488 | tf_op jit(solution)/shard_map/ppermute | solution.py:928
  11.2 21.4 %collective-permute-start.6 = (bf16[2,192,1024]{2,1,0:T(8,128)(2,1)}, bf16[2,192,1024]{2,1,0:T(8,128)(2,1)S(1)}, u32[]{:S(2)}, u32[]{:S(2)}) collective-permute-start(bf16[2,192,1024]{2,1,0:T(8,128)(2,1)} %constant_dynamic-slice_fusion.1), channel_id=1, source_target_pairs={{0,1},{1,0},{2,3},{3,2},{4,5},{5,4},{6,7},{7,6},{8,9},{9,8},{10,11... | collective-permute-start | bytes 2359304 | tf_op jit(solution)/shard_map/ppermute | solution.py:928
  14.4 12.5 %collective-permute-start.11 = (bf16[72,1088]{1,0:T(8,128)(2,1)}, bf16[72,1088]{1,0:T(8,128)(2,1)}, u32[]{:S(2)}, u32[]{:S(2)}) collective-permute-start(bf16[72,1088]{1,0:T(8,128)(2,1)} %concatenate.81), channel_id=1, source_target_pairs={{0,16},{1,17},{2,18},{3,19},{4,20},{5,21},{6,22},{7,23},{8,24},{9,... | collective-permute-start | bytes 470024 | tf_op jit(solution)/shard_map/ppermute | solution.py:928
  18.5 20.6 %collective-permute-start.3 = (bf16[144,1152]{1,0:T(8,128)(2,1)S(1)}, bf16[144,1152]{1,0:T(8,128)(2,1)S(1)}, u32[]{:S(2)}, u32[]{:S(2)}) collective-permute-start(bf16[144,1152]{1,0:T(8,128)(2,1)S(1)} %bitcast.82), channel_id=1, source_target_pairs={{0,8},{1,9},{2,10},{3,11},{4,12},{5,13},{6,14},{7,15},{8,0},{9,1},... | collective-permute-start | bytes 995336 | tf_op jit(solution)/shard_map/ppermute | solution.py:928
  20.2 19.0 %collective-permute-start.4 = (bf16[144,1152]{1,0:T(8,128)(2,1)S(1)}, bf16[144,1152]{1,0:T(8,128)(2,1)S(1)}, u32[]{:S(2)}, u32[]{:S(2)}) collective-permute-start(bf16[144,1152]{1,0:T(8,128)(2,1)S(1)} %bitcast.83), channel_id=1, source_target_pairs={{0,4},{1,5},{2,6},{3,7},{4,0},{5,1},{6,2},{7,3},{8,12},{9,13},{10,... | collective-permute-start | bytes 995336 | tf_op jit(solution)/shard_map/ppermute | solution.py:928
  21.7 17.4 %collective-permute-start.5 = (bf16[144,1152]{1,0:T(8,128)(2,1)S(1)}, bf16[144,1152]{1,0:T(8,128)(2,1)S(1)}, u32[]{:S(2)}, u32[]{:S(2)}) collective-permute-start(bf16[144,1152]{1,0:T(8,128)(2,1)S(1)} %bitcast.84), channel_id=1, source_target_pairs={{0,12},{1,13},{2,14},{3,15},{4,8},{5,9},{6,10},{7,11},{8,4},{9,5},... | collective-permute-start | bytes 995336 | tf_op jit(solution)/shard_map/ppermute | solution.py:928
  27.9 11.2 %collective-permute-start.12 = (bf16[144,1088]{1,0:T(8,128)(2,1)S(1)}, bf16[144,1088]{1,0:T(8,128)(2,1)S(1)}, u32[]{:S(2)}, u32[]{:S(2)}) collective-permute-start(bf16[144,1088]{1,0:T(8,128)(2,1)S(1)} %bitcast.87), channel_id=1, source_target_pairs={{0,1},{1,0},{2,3},{3,2},{4,5},{5,4},{6,7},{7,6},{8,9},{9,8},{10,11... | collective-permute-start | bytes 940040 | tf_op jit(solution)/shard_map/ppermute | solution.py:928
  39.1 1.9 collective-permute-start.10
  39.2 3.3 %collective-permute-start.7 = (bf16[144,1152]{1,0:T(8,128)(2,1)S(1)}, bf16[144,1152]{1,0:T(8,128)(2,1)S(1)}, u32[]{:S(2)}, u32[]{:S(2)}) collective-permute-start(bf16[144,1152]{1,0:T(8,128)(2,1)S(1)} %bitcast.85), channel_id=1, source_target_pairs={{0,2},{1,3},{2,0},{3,1},{4,6},{5,7},{6,4},{7,5},{8,10},{9,11},{10,... | collective-permute-start | bytes 995336 | tf_op jit(solution)/shard_map/ppermute | solution.py:928
  39.7 4.3 %collective-permute-start.8 = (bf16[144,1152]{1,0:T(8,128)(2,1)S(1)}, bf16[144,1152]{1,0:T(8,128)(2,1)S(1)}, u32[]{:S(2)}, u32[]{:S(2)}) collective-permute-start(bf16[144,1152]{1,0:T(8,128)(2,1)S(1)} %collective-permute-done.3.refs_3_), channel_id=1, source_target_pairs={{0,2},{1,3},{2,0},{3,1},{4,6},{5,7},{6,4},{7,5},{8,10},{9,11},{10,... | collective-permute-start | bytes 995336 | tf_op jit(solution)/shard_map/ppermute | solution.py:928
  39.8 4.2 %collective-permute-start.9 = (bf16[144,1152]{1,0:T(8,128)(2,1)S(1)}, bf16[144,1152]{1,0:T(8,128)(2,1)S(1)}, u32[]{:S(2)}, u32[]{:S(2)}) collective-permute-start(bf16[144,1152]{1,0:T(8,128)(2,1)S(1)} %collective-permute-done.4.refs_4_), channel_id=1, source_target_pairs={{0,2},{1,3},{2,0},{3,1},{4,6},{5,7},{6,4},{7,5},{8,10},{9,11},{10,... | collective-permute-start | bytes 995336 | tf_op jit(solution)/shard_map/ppermute | solution.py:928
  40.4 18.3 %collective-permute-start.13 = (bf16[144,1664]{1,0:T(8,128)(2,1)S(1)}, bf16[144,1664]{1,0:T(8,128)(2,1)S(1)}, u32[]{:S(2)}, u32[]{:S(2)}) collective-permute-start(bf16[144,1664]{1,0:T(8,128)(2,1)S(1)} %pad_maximum_fusion.refs_8_.refs_1_), channel_id=1, source_target_pairs={{0,8},{1,9},{2,10},{3,11},{4,12},{5,13},{6,14},{7,15},{8,0},{9,1},... | collective-permute-start | bytes 1437704 | tf_op jit(solution)/shard_map/ppermute | solution.py:928
  41.0 22.2 %collective-permute-start.14 = (bf16[144,1664]{1,0:T(8,128)(2,1)S(1)}, bf16[144,1664]{1,0:T(8,128)(2,1)S(1)}, u32[]{:S(2)}, u32[]{:S(2)}) collective-permute-start(bf16[144,1664]{1,0:T(8,128)(2,1)S(1)} %pad_maximum_fusion.refs_8_.refs_1_), channel_id=1, source_target_pairs={{0,4},{1,5},{2,6},{3,7},{4,0},{5,1},{6,2},{7,3},{8,12},{9,13},{10,... | collective-permute-start | bytes 1437704 | tf_op jit(solution)/shard_map/ppermute | solution.py:928
  42.5 22.1 %collective-permute-start.15 = (bf16[144,1664]{1,0:T(8,128)(2,1)S(1)}, bf16[144,1664]{1,0:T(8,128)(2,1)S(1)}, u32[]{:S(2)}, u32[]{:S(2)}) collective-permute-start(bf16[144,1664]{1,0:T(8,128)(2,1)S(1)} %pad_maximum_fusion.refs_8_.refs_1_), channel_id=1, source_target_pairs={{0,12},{1,13},{2,14},{3,15},{4,8},{5,9},{6,10},{7,11},{8,4},{9,5},... | collective-permute-start | bytes 1437704 | tf_op jit(solution)/shard_map/ppermute | solution.py:928
  64.7 2.1 collective-permute-start.16
  64.7 3.6 %collective-permute-start.17 = (bf16[144,1664]{1,0:T(8,128)(2,1)S(1)}, bf16[144,1664]{1,0:T(8,128)(2,1)S(1)}, u32[]{:S(2)}, u32[]{:S(2)}) collective-permute-start(bf16[144,1664]{1,0:T(8,128)(2,1)S(1)} %collective-permute-done.13.refs_9_.refs_2_), channel_id=1, source_target_pairs={{0,2},{1,3},{2,0},{3,1},{4,6},{5,7},{6,4},{7,5},{8,10},{9,11},{10,... | collective-permute-start | bytes 1437704 | tf_op jit(solution)/shard_map/ppermute | solution.py:928
  65.2 4.2 %collective-permute-start.18 = (bf16[144,1664]{1,0:T(8,128)(2,1)S(1)}, bf16[144,1664]{1,0:T(8,128)(2,1)S(1)}, u32[]{:S(2)}, u32[]{:S(2)}) collective-permute-start(bf16[144,1664]{1,0:T(8,128)(2,1)S(1)} %collective-permute-done.14.refs_10_.refs_3_), channel_id=1, source_target_pairs={{0,2},{1,3},{2,0},{3,1},{4,6},{5,7},{6,4},{7,5},{8,10},{9,11},{10,... | collective-permute-start | bytes 1437704 | tf_op jit(solution)/shard_map/ppermute | solution.py:928
  65.3 5.0 %collective-permute-start.19 = (bf16[144,1664]{1,0:T(8,128)(2,1)S(1)}, bf16[144,1664]{1,0:T(8,128)(2,1)S(1)}, u32[]{:S(2)}, u32[]{:S(2)}) collective-permute-start(bf16[144,1664]{1,0:T(8,128)(2,1)S(1)} %collective-permute-done.15.refs_11_.refs_4_), channel_id=1, source_target_pairs={{0,2},{1,3},{2,0},{3,1},{4,6},{5,7},{6,4},{7,5},{8,10},{9,11},{10,... | collective-permute-start | bytes 1437704 | tf_op jit(solution)/shard_map/ppermute | solution.py:928
  65.8 23.6 %collective-permute-start.21 = (bf16[144,512]{1,0:T(8,128)(2,1)S(1)}, bf16[144,512]{1,0:T(8,128)(2,1)S(1)}, u32[]{:S(2)}, u32[]{:S(2)}) collective-permute-start(bf16[144,512]{1,0:T(8,128)(2,1)S(1)} %pad_maximum_fusion.7.refs_7_), channel_id=1, source_target_pairs={{0,8},{1,9},{2,10},{3,11},{4,12},{5,13},{6,14},{7,15},{8,0},{9,1},... | collective-permute-start | bytes 442376 | tf_op jit(solution)/shard_map/ppermute | solution.py:928
  66.8 22.7 %collective-permute-start.22 = (bf16[144,512]{1,0:T(8,128)(2,1)S(1)}, bf16[144,512]{1,0:T(8,128)(2,1)S(1)}, u32[]{:S(2)}, u32[]{:S(2)}) collective-permute-start(bf16[144,512]{1,0:T(8,128)(2,1)S(1)} %pad_maximum_fusion.7.refs_7_), channel_id=1, source_target_pairs={{0,4},{1,5},{2,6},{3,7},{4,0},{5,1},{6,2},{7,3},{8,12},{9,13},{10,... | collective-permute-start | bytes 442376 | tf_op jit(solution)/shard_map/ppermute | solution.py:928
  68.3 21.2 %collective-permute-start.23 = (bf16[144,512]{1,0:T(8,128)(2,1)S(1)}, bf16[144,512]{1,0:T(8,128)(2,1)}, u32[]{:S(2)}, u32[]{:S(2)}) collective-permute-start(bf16[144,512]{1,0:T(8,128)(2,1)S(1)} %pad_maximum_fusion.7.refs_7_), channel_id=1, source_target_pairs={{0,12},{1,13},{2,14},{3,15},{4,8},{5,9},{6,10},{7,11},{8,4},{9,5},... | collective-permute-start | bytes 442376 | tf_op jit(solution)/shard_map/ppermute | solution.py:928
  69.4 21.2 %collective-permute-start.20 = (bf16[2,192,1024]{2,1,0:T(8,128)(2,1)}, bf16[2,192,1024]{2,1,0:T(8,128)(2,1)}, u32[]{:S(2)}, u32[]{:S(2)}) collective-permute-start(bf16[2,192,1024]{2,1,0:T(8,128)(2,1)} %constant_dynamic-slice_fusion), channel_id=1, source_target_pairs={{0,1},{1,0},{2,3},{3,2},{4,5},{5,4},{6,7},{7,6},{8,9},{9,8},{10,11... | collective-permute-start | bytes 2359304 | tf_op jit(solution)/shard_map/ppermute | solution.py:928
  154.2 8.6 %collective-permute-start.28 = (bf16[2,384,1024]{2,1,0:T(8,128)(2,1)}, bf16[2,384,1024]{2,1,0:T(8,128)(2,1)S(1)}, u32[]{:S(2)}, u32[]{:S(2)}) collective-permute-start(bf16[2,384,1024]{2,1,0:T(8,128)(2,1)} %get-tuple-element.125.refs_0_.refs_5_.refs_6_), channel_id=1, source_target_pairs={{0,2},{1,3},{2,0},{3,1},{4,6},{5,7},{6,4},{7,5},{8,10},{9,11},{10,... | collective-permute-start | bytes 4718600 | tf_op jit(solution)/shard_map/ppermute | solution.py:928
  154.6 8.2 %collective-permute-start.29 = (bf16[192,2048]{1,0:T(8,128)(2,1)}, bf16[192,2048]{1,0:T(8,128)(2,1)S(1)}, u32[]{:S(2)}, u32[]{:S(2)}) collective-permute-start(bf16[192,2048]{1,0:T(8,128)(2,1)} %get-tuple-element.115), channel_id=1, source_target_pairs={{0,2},{1,3},{2,0},{3,1},{4,6},{5,7},{6,4},{7,5},{8,10},{9,11},{10,... | collective-permute-start | bytes 2359304 | tf_op jit(solution)/shard_map/ppermute | solution.py:928
  154.8 8.0 %collective-permute-start.30 = (bf16[256,1152]{1,0:T(8,128)(2,1)}, bf16[256,1152]{1,0:T(8,128)(2,1)S(1)}, u32[]{:S(2)}, u32[]{:S(2)}) collective-permute-start(bf16[256,1152]{1,0:T(8,128)(2,1)} %get-tuple-element.118), channel_id=1, source_target_pairs={{0,2},{1,3},{2,0},{3,1},{4,6},{5,7},{6,4},{7,5},{8,10},{9,11},{10,... | collective-permute-start | bytes 1769480 | tf_op jit(solution)/shard_map/ppermute | solution.py:928
  155.1 27.0 %collective-permute-start.31 = (bf16[2,192,1024]{2,1,0:T(8,128)(2,1)}, bf16[2,192,1024]{2,1,0:T(8,128)(2,1)S(1)}, u32[]{:S(2)}, u32[]{:S(2)}) collective-permute-start(bf16[2,192,1024]{2,1,0:T(8,128)(2,1)} %get-tuple-element.124), channel_id=1, source_target_pairs={{0,1},{1,0},{2,3},{3,2},{4,5},{5,4},{6,7},{7,6},{8,9},{9,8},{10,11... | collective-permute-start | bytes 2359304 | tf_op jit(solution)/shard_map/ppermute | solution.py:928
  167.0 22.3 %collective-permute-start.33 = (bf16[208,1152]{1,0:T(8,128)(2,1)S(1)}, bf16[208,1152]{1,0:T(8,128)(2,1)S(1)}, u32[]{:S(2)}, u32[]{:S(2)}) collective-permute-start(bf16[208,1152]{1,0:T(8,128)(2,1)S(1)} %get-tuple-element.120), channel_id=1, source_target_pairs={{0,8},{1,9},{2,10},{3,11},{4,12},{5,13},{6,14},{7,15},{8,0},{9,1},... | collective-permute-start | bytes 1437704 | tf_op jit(solution)/shard_map/ppermute | solution.py:928
  167.9 22.8 %collective-permute-start.34 = (bf16[208,1152]{1,0:T(8,128)(2,1)S(1)}, bf16[208,1152]{1,0:T(8,128)(2,1)S(1)}, u32[]{:S(2)}, u32[]{:S(2)}) collective-permute-start(bf16[208,1152]{1,0:T(8,128)(2,1)S(1)} %get-tuple-element.121), channel_id=1, source_target_pairs={{0,4},{1,5},{2,6},{3,7},{4,0},{5,1},{6,2},{7,3},{8,12},{9,13},{10,... | collective-permute-start | bytes 1437704 | tf_op jit(solution)/shard_map/ppermute | solution.py:928
  169.4 21.3 %collective-permute-start.35 = (bf16[208,1152]{1,0:T(8,128)(2,1)S(1)}, bf16[208,1152]{1,0:T(8,128)(2,1)S(1)}, u32[]{:S(2)}, u32[]{:S(2)}) collective-permute-start(bf16[208,1152]{1,0:T(8,128)(2,1)S(1)} %get-tuple-element.122), channel_id=1, source_target_pairs={{0,12},{1,13},{2,14},{3,15},{4,8},{5,9},{6,10},{7,11},{8,4},{9,5},... | collective-permute-start | bytes 1437704 | tf_op jit(solution)/shard_map/ppermute | solution.py:928
  189.2 3.6 %collective-permute-start.32 = (bf16[576,1152]{1,0:T(8,128)(2,1)S(1)}, bf16[576,1152]{1,0:T(8,128)(2,1)S(1)}, u32[]{:S(2)}, u32[]{:S(2)}) collective-permute-start(bf16[576,1152]{1,0:T(8,128)(2,1)S(1)} %get-tuple-element.129), channel_id=1, source_target_pairs={{0,2},{1,3},{2,0},{3,1},{4,6},{5,7},{6,4},{7,5},{8,10},{9,11},{10,... | collective-permute-start | bytes 3981320 | tf_op jit(solution)/shard_map/ppermute | solution.py:928
  191.7 12.3 %collective-permute-start.36 = (bf16[208,576]{1,0:T(8,128)(2,1)S(1)}, bf16[208,576]{1,0:T(8,128)(2,1)S(1)}, u32[]{:S(2)}, u32[]{:S(2)}) collective-permute-start(bf16[208,576]{1,0:T(8,128)(2,1)S(1)} %get-tuple-element.136), channel_id=1, source_target_pairs={{0,1},{1,0},{2,3},{3,2},{4,5},{5,4},{6,7},{7,6},{8,9},{9,8},{10,11... | collective-permute-start | bytes 718856 | tf_op jit(solution)/shard_map/ppermute | solution.py:928
  193.6 24.4 %collective-permute-start.39 = (bf16[144,1152]{1,0:T(8,128)(2,1)S(1)}, bf16[144,1152]{1,0:T(8,128)(2,1)S(1)}, u32[]{:S(2)}, u32[]{:S(2)}) collective-permute-start(bf16[144,1152]{1,0:T(8,128)(2,1)S(1)} %get-tuple-element.131), channel_id=1, source_target_pairs={{0,8},{1,9},{2,10},{3,11},{4,12},{5,13},{6,14},{7,15},{8,0},{9,1},... | collective-permute-start | bytes 995336 | tf_op jit(solution)/shard_map/ppermute | solution.py:928
  194.7 23.3 %collective-permute-start.40 = (bf16[144,1152]{1,0:T(8,128)(2,1)S(1)}, bf16[144,1152]{1,0:T(8,128)(2,1)S(1)}, u32[]{:S(2)}, u32[]{:S(2)}) collective-permute-start(bf16[144,1152]{1,0:T(8,128)(2,1)S(1)} %get-tuple-element.132), channel_id=1, source_target_pairs={{0,4},{1,5},{2,6},{3,7},{4,0},{5,1},{6,2},{7,3},{8,12},{9,13},{10,... | collective-permute-start | bytes 995336 | tf_op jit(solution)/shard_map/ppermute | solution.py:928
  196.0 22.1 %collective-permute-start.41 = (bf16[144,1152]{1,0:T(8,128)(2,1)S(1)}, bf16[144,1152]{1,0:T(8,128)(2,1)S(1)}, u32[]{:S(2)}, u32[]{:S(2)}) collective-permute-start(bf16[144,1152]{1,0:T(8,128)(2,1)S(1)} %get-tuple-element.133), channel_id=1, source_target_pairs={{0,12},{1,13},{2,14},{3,15},{4,8},{5,9},{6,10},{7,11},{8,4},{9,5},... | collective-permute-start | bytes 995336 | tf_op jit(solution)/shard_map/ppermute | solution.py:928
  204.6 18.9 %collective-permute-start.45 = (bf16[104,576]{1,0:T(8,128)(2,1)S(1)}, bf16[104,576]{1,0:T(8,128)(2,1)S(1)}, u32[]{:S(2)}, u32[]{:S(2)}) collective-permute-start(bf16[104,576]{1,0:T(8,128)(2,1)S(1)} %get-tuple-element.144), channel_id=1, source_target_pairs={{0,16},{1,17},{2,18},{3,19},{4,20},{5,21},{6,22},{7,23},{8,24},{9,... | collective-permute-start | bytes 359432 | tf_op jit(solution)/shard_map/ppermute | solution.py:928
  207.8 9.7 %collective-permute-start.37 = (bf16[1,192,1024]{2,1,0:T(8,128)(2,1)S(1)}, bf16[1,192,1024]{2,1,0:T(8,128)(2,1)S(1)}, u32[]{:S(2)}, u32[]{:S(2)}) collective-permute-start(bf16[1,192,1024]{2,1,0:T(8,128)(2,1)S(1)} %get-tuple-element.149), channel_id=1, source_target_pairs={{0,1},{1,0},{2,3},{3,2},{4,5},{5,4},{6,7},{7,6},{8,9},{9,8},{10,11... | collective-permute-start | bytes 1179656 | tf_op jit(solution)/shard_map/ppermute | solution.py:928
  217.5 11.6 %collective-permute-start.38 = (bf16[1,192,1024]{2,1,0:T(8,128)(2,1)S(1)}, bf16[1,192,1024]{2,1,0:T(8,128)(2,1)S(1)}, u32[]{:S(2)}, u32[]{:S(2)}) collective-permute-start(bf16[1,192,1024]{2,1,0:T(8,128)(2,1)S(1)} %get-tuple-element.150), channel_id=1, source_target_pairs={{0,1},{1,0},{2,3},{3,2},{4,5},{5,4},{6,7},{7,6},{8,9},{9,8},{10,11... | collective-permute-start | bytes 1179656 | tf_op jit(solution)/shard_map/ppermute | solution.py:928
  218.1 2.9 %collective-permute-start.46 = (f32[16,384]{1,0:T(8,128)S(1)}, f32[16,384]{1,0:T(8,128)S(1)}, u32[]{:S(2)}, u32[]{:S(2)}) collective-permute-start(f32[16,384]{1,0:T(8,128)S(1)} %get-tuple-element.160), channel_id=1, source_target_pairs={{0,2},{1,3},{2,0},{3,1},{4,6},{5,7},{6,4},{7,5},{8,10},{9,11},{10,... | collective-permute-start | bytes 73736 | tf_op jit(solution)/shard_map/ppermute | solution.py:928
  219.0 17.2 %collective-permute-start.42 = (bf16[72,576]{1,0:T(8,128)(2,1)S(1)}, bf16[72,576]{1,0:T(8,128)(2,1)S(1)}, u32[]{:S(2)}, u32[]{:S(2)}) collective-permute-start(bf16[72,576]{1,0:T(8,128)(2,1)S(1)} %get-tuple-element.152), channel_id=1, source_target_pairs={{0,1},{1,0},{2,3},{3,2},{4,5},{5,4},{6,7},{7,6},{8,9},{9,8},{10,11... | collective-permute-start | bytes 248840 | tf_op jit(solution)/shard_map/ppermute | solution.py:928
  220.6 15.8 %collective-permute-start.43 = (bf16[72,576]{1,0:T(8,128)(2,1)S(1)}, bf16[72,576]{1,0:T(8,128)(2,1)S(1)}, u32[]{:S(2)}, u32[]{:S(2)}) collective-permute-start(bf16[72,576]{1,0:T(8,128)(2,1)S(1)} %get-tuple-element.153), channel_id=1, source_target_pairs={{0,16},{1,17},{2,18},{3,19},{4,20},{5,21},{6,22},{7,23},{8,24},{9,... | collective-permute-start | bytes 248840 | tf_op jit(solution)/shard_map/ppermute | solution.py:928
  220.9 15.5 %collective-permute-start.44 = (bf16[72,576]{1,0:T(8,128)(2,1)S(1)}, bf16[72,576]{1,0:T(8,128)(2,1)S(1)}, u32[]{:S(2)}, u32[]{:S(2)}) collective-permute-start(bf16[72,576]{1,0:T(8,128)(2,1)S(1)} %get-tuple-element.154), channel_id=1, source_target_pairs={{0,17},{1,16},{2,19},{3,18},{4,21},{5,20},{6,23},{7,22},{8,25},{9,... | collective-permute-start | bytes 248840 | tf_op jit(solution)/shard_map/ppermute | solution.py:928
  223.5 4.0 %collective-permute-start.47 = (f32[24,384]{1,0:T(8,128)S(1)}, f32[24,384]{1,0:T(8,128)S(1)}, u32[]{:S(2)}, u32[]{:S(2)}) collective-permute-start(f32[24,384]{1,0:T(8,128)S(1)} %pad_maximum_fusion.13), channel_id=1, source_target_pairs={{0,8},{1,9},{2,10},{3,11},{4,12},{5,13},{6,14},{7,15},{8,0},{9,1},... | collective-permute-start | bytes 110600 | tf_op jit(solution)/shard_map/ppermute | solution.py:928
  227.5 4.3 %collective-permute-start.48 = (f32[40,384]{1,0:T(8,128)S(1)}, f32[40,384]{1,0:T(8,128)S(1)}, u32[]{:S(2)}, u32[]{:S(2)}) collective-permute-start(f32[40,384]{1,0:T(8,128)S(1)} %pad_maximum_fusion.10), channel_id=1, source_target_pairs={{0,4},{1,5},{2,6},{3,7},{4,0},{5,1},{6,2},{7,3},{8,12},{9,13},{10,... | collective-permute-start | bytes 184328 | tf_op jit(solution)/shard_map/ppermute | solution.py:928
  232.0 5.8 %collective-permute-start.49 = (f32[72,192]{1,0:T(8,128)S(1)}, f32[72,192]{1,0:T(8,128)S(1)}, u32[]{:S(2)}, u32[]{:S(2)}) collective-permute-start(f32[72,192]{1,0:T(8,128)S(1)} %get-tuple-element.219), channel_id=1, source_target_pairs={{0,1},{1,0},{2,3},{3,2},{4,5},{5,4},{6,7},{7,6},{8,9},{9,8},{10,11... | collective-permute-start | bytes 165896 | tf_op jit(solution)/shard_map/ppermute | solution.py:928
  233.7 7.7 %collective-permute-start.51 = (f32[72,192]{1,0:T(8,128)S(1)}, f32[72,192]{1,0:T(8,128)S(1)}, u32[]{:S(2)}, u32[]{:S(2)}) collective-permute-start(f32[72,192]{1,0:T(8,128)S(1)} %get-tuple-element.219), channel_id=1, source_target_pairs={{0,17},{1,16},{2,19},{3,18},{4,21},{5,20},{6,23},{7,22},{8,25},{9,... | collective-permute-start | bytes 165896 | tf_op jit(solution)/shard_map/ppermute | solution.py:928
  236.2 5.3 %collective-permute-start.50 = (f32[72,192]{1,0:T(8,128)S(1)}, f32[72,192]{1,0:T(8,128)S(1)}, u32[]{:S(2)}, u32[]{:S(2)}) collective-permute-start(f32[72,192]{1,0:T(8,128)S(1)} %get-tuple-element.218), channel_id=1, source_target_pairs={{0,16},{1,17},{2,18},{3,19},{4,20},{5,21},{6,22},{7,23},{8,24},{9,... | collective-permute-start | bytes 165896 | tf_op jit(solution)/shard_map/ppermute | solution.py:928
  (67 other events, 542.5 us)

commit v4 on v3

--- a/solution.py
+++ b/solution.py
@@ -300,6 +300,7 @@
     stats_out,
     weight,
     weight_e,
+    sums,
     value,
     stack,
     product,
@@ -309,13 +310,18 @@
     count = count_of(mask)
     image = pl.program_id(0)
 
-    def own_columns(sums):
-        return jnp.where(image == 0, sums[:, :6], sums[:, 6:12])
+    @pl.when(image == 0)
+    def _():
+        for chan in range(2):
+            for part in range(2):
+                sums[chan, part] = dot(weight_e[chan, part], embed_in[part], TN)
+
+    def own_columns(both):
+        return jnp.where(image == 0, both[:, :6], both[:, 6:12])
 
     scales, shifts = [], []
     for chan in range(2):
-        low = own_columns(dot(weight_e[chan, 0], embed_in[0], TN))
-        high = own_columns(dot(weight_e[chan, 1], embed_in[1], TN))
+        low, high = own_columns(sums[chan, 0]), own_columns(sums[chan, 1])
         column = jnp.concatenate(
             [
                 low[:, 0:1] + low[:, 1:2] + low[:, 2:3],
@@ -1158,6 +1164,7 @@
         [
             pltpu.VMEM((TAPS, TAPS), LOW),
             pltpu.VMEM((2, 2, TAPS, 128), LOW),
+            pltpu.VMEM((2, 2, 128, 128), WIDE),
             value_scratch,
             pltpu.VMEM((TAPS, PIX), LOW),
             product_scratch,

time: 248 us -> 248 us (level)
  no operation moved by 1% of the time
where the time goes in v4:
time: 248 us; the launch traced here: 244 us
  Pallas kernels  144 us (58%)
  starting transfers between devices  52.6 us (21%)
  waiting for transfers between devices  20.6 us (8%)
  local copies, waits for them, and re-layouts  17.5 us (7%)
  other arithmetic  5.76 us (2%)
    pallas_call x17, Pallas kernels, run(): pl.pallas_call(body, grid_spec=pltpu.PrefetchScalarGridSpec(num_scalar_pr...  144 us
    ppermute x52, starting transfers between devices, swap(): return lax.ppermute(value, ('dp', 'chan'), pairs)  52.6 us
    ppermute x52, waiting for transfers between devices, swap(): return lax.ppermute(value, ('dp', 'chan'), pairs)  20.6 us
    unnamed x127, local copies, waits for them, and re-layouts  9.21 us
  transfers between devices with their start and end apart: 52, of which 13 were waited for; matrix products, arithmetic and copies ran while one was open for 5% of the time, Pallas kernels for 34%

profile of v4, /device:TPU:0, one launch (start us, length us, event | category | flops | bytes accessed | tf_op | source)
XLA Modules:
  0.0 243.9 jit_solution(2028303393040783202)
XLA Ops:
  1.9 4.1 %collective-permute-start.1 = (bf16[72,576]{1,0:T(8,128)(2,1)S(1)}, bf16[72,576]{1,0:T(8,128)(2,1)S(1)}, u32[]{:S(2)}, u32[]{:S(2)}) collective-permute-start(bf16[72,576]{1,0:T(8,128)(2,1)S(1)} %reshape.352), channel_id=1, source_target_pairs={{0,16},{1,17},{2,18},{3,19},{4,20},{5,21},{6,22},{7,23},{8,24},{9,... | collective-permute-start | bytes 248840 | tf_op jit(solution)/shard_map/ppermute | solution.py:934
  6.0 1.3 collective-permute-start.2
  9.1 2.1 constant_dynamic-slice_fusion.1
  11.2 1.7 collective-permute-start.6
  14.4 2.6 %collective-permute-start.11 = (bf16[72,1088]{1,0:T(8,128)(2,1)}, bf16[72,1088]{1,0:T(8,128)(2,1)}, u32[]{:S(2)}, u32[]{:S(2)}) collective-permute-start(bf16[72,1088]{1,0:T(8,128)(2,1)} %concatenate.81), channel_id=1, source_target_pairs={{0,16},{1,17},{2,18},{3,19},{4,20},{5,21},{6,22},{7,23},{8,24},{9,... | collective-permute-start | bytes 470024 | tf_op jit(solution)/shard_map/ppermute | solution.py:934
  18.5 1.6 collective-permute-start.3
  20.2 1.5 collective-permute-start.4
  28.5 4.1 %collective-permute-done.6.refs_1_.refs_3_.refs_4_ = bf16[2,192,1024]{2,1,0:T(8,128)(2,1)S(1)} collective-permute-done((bf16[2,192,1024]{2,1,0:T(8,128)(2,1)}, bf16[2,192,1024]{2,1,0:T(8,128)(2,1)S(1)}, u32[]{:S(2)}, u32[]{:S(2)}) %collective-permute-start.6) | collective-permute-done | bytes 786464 | tf_op jit(solution)/shard_map/ppermute | solution.py:934
  32.6 5.3 %shard_map.196 = (bf16[576,2048]{1,0:T(8,128)(2,1)S(1)}, bf16[576,2048]{1,0:T(8,128)(2,1)S(1)}, f32[2,8,384]{2,1,0:T(8,128)S(1)}) custom-call(s32[19]{0:T(128)S(1)} %pad_add_fusion.place, bf16[4,192,1024]{2,1,0:T(8,128)(2,1)S(1)} %copy-done.6, bf16[2,192,1024]{2,1,0:T(8,128)(2,1)S(1)} %collective-permute-done.6.refs_1_.refs_3_.refs_4_, ...), custom_call_target="tpu_custom_call" | custom-call | flops 8000000000 | bytes 1048576 | tf_op jit(solution)/shard_map/pallas_call | solution.py:835
  37.9 1.2 collective-permute-done.12
  41.0 1.5 collective-permute-start.14
  42.5 1.5 collective-permute-start.15
  44.0 10.9 %shard_map.197 = (f32[2,384,1024]{2,1,0:T(8,128)S(1)}, f32[2,8,384]{2,1,0:T(8,128)S(1)}, bf16[1152,1152]{1,0:T(8,128)(2,1)S(1)}) custom-call(s32[19]{0:T(128)S(1)} %pad_add_fusion.place, f32[2,1,1024]{2,1,0:T(1,128)S(1)} %reshape.350.refs_2_.refs_0_.refs_5_.refs_4_.refs_11_.refs_6_.refs_7_, ...), custom_call_target="tpu_custom_call" | custom-call | flops 8000000000 | bytes 1048576 | tf_op jit(solution)/shard_map/pallas_call | solution.py:835
  55.0 1.7 copy-done.34
  56.6 1.5 copy-done.36
  58.7 4.5 %collective-permute-done.14.refs_10_.refs_3_ = bf16[144,1664]{1,0:T(8,128)(2,1)S(1)} collective-permute-done((bf16[144,1664]{1,0:T(8,128)(2,1)S(1)}, bf16[144,1664]{1,0:T(8,128)(2,1)S(1)}, u32[]{:S(2)}, u32[]{:S(2)}) %collective-permute-start.14) | collective-permute-done | bytes 479264 | tf_op jit(solution)/shard_map/ppermute | solution.py:934
  63.2 1.5 collective-permute-done.15.refs_11_.refs_4_
  66.8 1.5 collective-permute-start.22
  68.3 1.1 collective-permute-start.23
  71.1 18.6 %shard_map.198 = (bf16[192,2048]{1,0:T(8,128)(2,1)}, bf16[192,2048]{1,0:T(8,128)(2,1)}, f32[2,384,1024]{2,1,0:T(8,128)}, f32[2,8,384]{2,1,0:T(8,128)}) custom-call(s32[19]{0:T(128)} %copy-done.12, f32[2,384,1024]{2,1,0:T(8,128)} %copy-done.34, f32[2,8,384]{2,1,0:T(8,128)} %copy-done.42, bf16[4,192,1024]{2,1,0:T(8,128)(2,1)} %refs_3_.1, ...), custom_call_target="tpu_custom_call" | custom-call | flops 8000000000 | bytes 1048576 | tf_op jit(solution)/shard_map/pallas_call | solution.py:835
  92.8 61.6 %shard_map.199 = (bf16[4,192,1024]{2,1,0:T(8,128)(2,1)}, bf16[2,192,1024]{2,1,0:T(8,128)(2,1)}, bf16[2,384,1024]{2,1,0:T(8,128)(2,1)}, f32[256,1152]{1,0:T(8,128...) custom-call(s32[19]{0:T(128)} %copy-done.12, f32[2,384,1024]{2,1,0:T(8,128)} %get-tuple-element.106.refs_0_, ...), custom_call_target="tpu_custom_call" | custom-call | flops 60000002048 | bytes 1048576 | tf_op jit(solution)/shard_map/pallas_call | solution.py:835
  155.3 1.2 collective-permute-start.31
  156.5 1.4 copy-done.16
  157.9 1.1 copy-done.39
  159.0 4.0 %shard_map.200.refs_2_ = f32[576,1152]{1,0:T(8,128)S(1)} custom-call(s32[19]{0:T(128)S(1)} %copy-done.13, bf16[2,384,1024]{2,1,0:T(8,128)(2,1)S(1)} %copy-done.16, bf16[192,2048]{1,0:T(8,128)(2,1)S(1)} %copy-done.39), custom_call_target="tpu_custom_call" | custom-call | flops 8000000000 | bytes 1048576 | tf_op jit(solution)/shard_map/pallas_call | solution.py:835
  163.2 4.0 %shard_map.201 = (f32[208,1152]{1,0:T(8,128)S(1)}, bf16[208,1152]{1,0:T(8,128)(2,1)S(1)}, bf16[208,1152]{1,0:T(8,128)(2,1)S(1)}, bf16[208,1152]{1,0:T(8,128)(2,1)S(1)}) custom-call(s32[19]{0:T(128)S(1)} %copy-done.13, bf16[2,384,1024]{2,1,0:T(8,128)(2,1)S(1)} %collective-permute-done.28.refs_0_, bf16[192,2048]{1,0:T(8,128)(2,1)S(1)} %collective-permute-done.29.refs_1_, ...), custom_call_target="tpu_custom_call" | custom-call | flops 8000000000 | bytes 1048576 | tf_op jit(solution)/shard_map/pallas_call | solution.py:835
  168.1 1.5 collective-permute-start.34
  170.9 11.4 %shard_map.202 = (bf16[2,384,1024]{2,1,0:T(8,128)(2,1)S(1)}, f32[2,8,384]{2,1,0:T(8,128)S(1)}) custom-call(s32[19]{0:T(128)S(1)} %copy-done.13, bf16[2,384,1024]{2,1,0:T(8,128)(2,1)S(1)} %copy-done.17, bf16[144,1664]{1,0:T(8,128)(2,1)S(1)} %copy-done.5, bf16[144,1664]{1,0:T(8,128)(2,1)S(1)} %copy-done.21, bf16[144,1664]{1,0:T(8,128)(2,1)S(1)} %copy-done.23, ...), custom_call_target="tpu_custom_call" | custom-call | flops 8000000000 | bytes 1048576 | tf_op jit(solution)/shard_map/pallas_call | solution.py:835
  182.4 7.0 %shard_map.203 = (bf16[576,1152]{1,0:T(8,128)(2,1)S(1)}, f32[576,1152]{1,0:T(8,128)S(1)}) custom-call(s32[19]{0:T(128)S(1)} %copy-done.13, bf16[2,384,1024]{2,1,0:T(8,128)(2,1)S(1)} %get-tuple-element.145.refs_0_.refs_1_, bf16[576,2048]{1,0:T(8,128)(2,1)S(1)} %copy-done.1, bf16[576,2048]{1,0:T(8,128)(2,1)S(1)} %copy-done.3), custom_call_target="tpu_custom_call" | custom-call | flops 1000000000 | bytes 1048576 | tf_op jit(solution)/shard_map/pallas_call | solution.py:835
  189.5 1.4 collective-permute-done.34.refs_2_
  193.9 1.1 collective-permute-start.39
  195.0 1.3 collective-permute-start.40
  196.3 1.2 collective-permute-start.41
  197.4 6.8 %shard_map.206 = (f32[4,192,1024]{2,1,0:T(8,128)}, bf16[1,192,1024]{2,1,0:T(8,128)(2,1)S(1)}, f32[8,384]{1,0:T(8,128)S(1)}) custom-call(s32[19]{0:T(128)S(1)} %copy-done.13, bf16[2,384,1024]{2,1,0:T(8,128)(2,1)S(1)} %get-tuple-element.145.refs_0_.refs_1_, bf16[1152,1152]{1,0:T(8,128)(2,1)S(1)} %copy-done.37, bf16[4,192,1024]{2,1,0:T(8,128)(2,1)S(1)} %copy-done.7, ...), custom_call_target="tpu_custom_call" | custom-call | flops 8000000000 | bytes 1048576 | tf_op jit(solution)/shard_map/pallas_call | solution.py:835
  204.8 3.2 %collective-permute-start.45 = (bf16[104,576]{1,0:T(8,128)(2,1)S(1)}, bf16[104,576]{1,0:T(8,128)(2,1)S(1)}, u32[]{:S(2)}, u32[]{:S(2)}) collective-permute-start(bf16[104,576]{1,0:T(8,128)(2,1)S(1)} %get-tuple-element.144), channel_id=1, source_target_pairs={{0,16},{1,17},{2,18},{3,19},{4,20},{5,21},{6,22},{7,23},{8,24},{9,... | collective-permute-start | bytes 359432 | tf_op jit(solution)/shard_map/ppermute | solution.py:934
  208.1 1.5 collective-permute-start.37
  209.6 7.0 %shard_map.208 = (f32[4,192,1024]{2,1,0:T(8,128)}, bf16[1,192,1024]{2,1,0:T(8,128)(2,1)S(1)}, f32[16,384]{1,0:T(8,128)S(1)}) custom-call(s32[19]{0:T(128)S(1)} %copy-done.13, f32[4,192,1024]{2,1,0:T(8,128)} %get-tuple-element.140.refs_0_, bf16[2,384,1024]{2,1,0:T(8,128)(2,1)S(1)} %get-tuple-element.145.refs_0_.refs_1_, ...), custom_call_target="tpu_custom_call", output_to_operand_aliasing={{0}: (1, {})} | custom-call | flops 8000000000 | bytes 1048576 | tf_op jit(solution)/shard_map/pallas_call | solution.py:835
  216.6 1.2 collective-permute-done.37.refs_1_
  219.3 1.6 collective-permute-start.42
  221.2 2.5 %collective-permute-start.44 = (bf16[72,576]{1,0:T(8,128)(2,1)S(1)}, bf16[72,576]{1,0:T(8,128)(2,1)S(1)}, u32[]{:S(2)}, u32[]{:S(2)}) collective-permute-start(bf16[72,576]{1,0:T(8,128)(2,1)S(1)} %get-tuple-element.154), channel_id=1, source_target_pairs={{0,17},{1,16},{2,19},{3,18},{4,21},{5,20},{6,23},{7,22},{8,25},{9,... | collective-permute-start | bytes 248840 | tf_op jit(solution)/shard_map/ppermute | solution.py:934
  223.7 1.2 collective-permute-start.47
  225.0 1.3 shard_map.212
  227.8 1.6 collective-permute-start.48
  229.4 1.8 shard_map.209
  232.2 1.8 collective-permute-start.49
  234.0 2.5 %collective-permute-start.51 = (f32[72,192]{1,0:T(8,128)S(1)}, f32[72,192]{1,0:T(8,128)S(1)}, u32[]{:S(2)}, u32[]{:S(2)}) collective-permute-start(f32[72,192]{1,0:T(8,128)S(1)} %get-tuple-element.219), channel_id=1, source_target_pairs={{0,17},{1,16},{2,19},{3,18},{4,21},{5,20},{6,23},{7,22},{8,25},{9,... | collective-permute-start | bytes 165896 | tf_op jit(solution)/shard_map/ppermute | solution.py:934
  236.7 1.3 shard_map.211
  238.0 3.7 %collective-permute-done.50 = f32[72,192]{1,0:T(8,128)S(1)} collective-permute-done((f32[72,192]{1,0:T(8,128)S(1)}, f32[72,192]{1,0:T(8,128)S(1)}, u32[]{:S(2)}, u32[]{:S(2)}) %collective-permute-start.50) | collective-permute-done | bytes 55328 | tf_op jit(solution)/shard_map/ppermute | solution.py:934
  (300 shorter events, 35.0 us)
Async XLA Ops:
  1.9 16.4 %collective-permute-start.1 = (bf16[72,576]{1,0:T(8,128)(2,1)S(1)}, bf16[72,576]{1,0:T(8,128)(2,1)S(1)}, u32[]{:S(2)}, u32[]{:S(2)}) collective-permute-start(bf16[72,576]{1,0:T(8,128)(2,1)S(1)} %reshape.352), channel_id=1, source_target_pairs={{0,16},{1,17},{2,18},{3,19},{4,20},{5,21},{6,22},{7,23},{8,24},{9,... | collective-permute-start | bytes 248840 | tf_op jit(solution)/shard_map/ppermute | solution.py:934
  6.0 12.3 %collective-permute-start.2 = (bf16[72,576]{1,0:T(8,128)(2,1)S(1)}, bf16[72,576]{1,0:T(8,128)(2,1)S(1)}, u32[]{:S(2)}, u32[]{:S(2)}) collective-permute-start(bf16[72,576]{1,0:T(8,128)(2,1)S(1)} %reshape.352), channel_id=1, source_target_pairs={{0,17},{1,16},{2,19},{3,18},{4,21},{5,20},{6,23},{7,22},{8,25},{9,... | collective-permute-start | bytes 248840 | tf_op jit(solution)/shard_map/ppermute | solution.py:934
  8.8 9.6 %collective-permute-start = (bf16[80,576]{1,0:T(8,128)(2,1)S(1)}, bf16[80,576]{1,0:T(8,128)(2,1)S(1)}, u32[]{:S(2)}, u32[]{:S(2)}) collective-permute-start(bf16[80,576]{1,0:T(8,128)(2,1)S(1)} %pad_maximum_fusion.9), channel_id=1, source_target_pairs={{0,1},{1,0},{2,3},{3,2},{4,5},{5,4},{6,7},{7,6},{8,9},{9,8},{10,11... | collective-permute-start | bytes 276488 | tf_op jit(solution)/shard_map/ppermute | solution.py:934
  11.2 21.4 %collective-permute-start.6 = (bf16[2,192,1024]{2,1,0:T(8,128)(2,1)}, bf16[2,192,1024]{2,1,0:T(8,128)(2,1)S(1)}, u32[]{:S(2)}, u32[]{:S(2)}) collective-permute-start(bf16[2,192,1024]{2,1,0:T(8,128)(2,1)} %constant_dynamic-slice_fusion.1), channel_id=1, source_target_pairs={{0,1},{1,0},{2,3},{3,2},{4,5},{5,4},{6,7},{7,6},{8,9},{9,8},{10,11... | collective-permute-start | bytes 2359304 | tf_op jit(solution)/shard_map/ppermute | solution.py:934
  14.4 12.5 %collective-permute-start.11 = (bf16[72,1088]{1,0:T(8,128)(2,1)}, bf16[72,1088]{1,0:T(8,128)(2,1)}, u32[]{:S(2)}, u32[]{:S(2)}) collective-permute-start(bf16[72,1088]{1,0:T(8,128)(2,1)} %concatenate.81), channel_id=1, source_target_pairs={{0,16},{1,17},{2,18},{3,19},{4,20},{5,21},{6,22},{7,23},{8,24},{9,... | collective-permute-start | bytes 470024 | tf_op jit(solution)/shard_map/ppermute | solution.py:934
  18.5 20.6 %collective-permute-start.3 = (bf16[144,1152]{1,0:T(8,128)(2,1)S(1)}, bf16[144,1152]{1,0:T(8,128)(2,1)S(1)}, u32[]{:S(2)}, u32[]{:S(2)}) collective-permute-start(bf16[144,1152]{1,0:T(8,128)(2,1)S(1)} %bitcast.82), channel_id=1, source_target_pairs={{0,8},{1,9},{2,10},{3,11},{4,12},{5,13},{6,14},{7,15},{8,0},{9,1},... | collective-permute-start | bytes 995336 | tf_op jit(solution)/shard_map/ppermute | solution.py:934
  20.2 19.0 %collective-permute-start.4 = (bf16[144,1152]{1,0:T(8,128)(2,1)S(1)}, bf16[144,1152]{1,0:T(8,128)(2,1)S(1)}, u32[]{:S(2)}, u32[]{:S(2)}) collective-permute-start(bf16[144,1152]{1,0:T(8,128)(2,1)S(1)} %bitcast.83), channel_id=1, source_target_pairs={{0,4},{1,5},{2,6},{3,7},{4,0},{5,1},{6,2},{7,3},{8,12},{9,13},{10,... | collective-permute-start | bytes 995336 | tf_op jit(solution)/shard_map/ppermute | solution.py:934
  21.7 17.4 %collective-permute-start.5 = (bf16[144,1152]{1,0:T(8,128)(2,1)S(1)}, bf16[144,1152]{1,0:T(8,128)(2,1)S(1)}, u32[]{:S(2)}, u32[]{:S(2)}) collective-permute-start(bf16[144,1152]{1,0:T(8,128)(2,1)S(1)} %bitcast.84), channel_id=1, source_target_pairs={{0,12},{1,13},{2,14},{3,15},{4,8},{5,9},{6,10},{7,11},{8,4},{9,5},... | collective-permute-start | bytes 995336 | tf_op jit(solution)/shard_map/ppermute | solution.py:934
  27.9 11.2 %collective-permute-start.12 = (bf16[144,1088]{1,0:T(8,128)(2,1)S(1)}, bf16[144,1088]{1,0:T(8,128)(2,1)S(1)}, u32[]{:S(2)}, u32[]{:S(2)}) collective-permute-start(bf16[144,1088]{1,0:T(8,128)(2,1)S(1)} %bitcast.87), channel_id=1, source_target_pairs={{0,1},{1,0},{2,3},{3,2},{4,5},{5,4},{6,7},{7,6},{8,9},{9,8},{10,11... | collective-permute-start | bytes 940040 | tf_op jit(solution)/shard_map/ppermute | solution.py:934
  39.1 1.9 collective-permute-start.10
  39.2 3.3 %collective-permute-start.7 = (bf16[144,1152]{1,0:T(8,128)(2,1)S(1)}, bf16[144,1152]{1,0:T(8,128)(2,1)S(1)}, u32[]{:S(2)}, u32[]{:S(2)}) collective-permute-start(bf16[144,1152]{1,0:T(8,128)(2,1)S(1)} %bitcast.85), channel_id=1, source_target_pairs={{0,2},{1,3},{2,0},{3,1},{4,6},{5,7},{6,4},{7,5},{8,10},{9,11},{10,... | collective-permute-start | bytes 995336 | tf_op jit(solution)/shard_map/ppermute | solution.py:934
  39.7 4.3 %collective-permute-start.8 = (bf16[144,1152]{1,0:T(8,128)(2,1)S(1)}, bf16[144,1152]{1,0:T(8,128)(2,1)S(1)}, u32[]{:S(2)}, u32[]{:S(2)}) collective-permute-start(bf16[144,1152]{1,0:T(8,128)(2,1)S(1)} %collective-permute-done.3.refs_3_), channel_id=1, source_target_pairs={{0,2},{1,3},{2,0},{3,1},{4,6},{5,7},{6,4},{7,5},{8,10},{9,11},{10,... | collective-permute-start | bytes 995336 | tf_op jit(solution)/shard_map/ppermute | solution.py:934
  39.8 4.2 %collective-permute-start.9 = (bf16[144,1152]{1,0:T(8,128)(2,1)S(1)}, bf16[144,1152]{1,0:T(8,128)(2,1)S(1)}, u32[]{:S(2)}, u32[]{:S(2)}) collective-permute-start(bf16[144,1152]{1,0:T(8,128)(2,1)S(1)} %collective-permute-done.4.refs_4_), channel_id=1, source_target_pairs={{0,2},{1,3},{2,0},{3,1},{4,6},{5,7},{6,4},{7,5},{8,10},{9,11},{10,... | collective-permute-start | bytes 995336 | tf_op jit(solution)/shard_map/ppermute | solution.py:934
  40.4 18.3 %collective-permute-start.13 = (bf16[144,1664]{1,0:T(8,128)(2,1)S(1)}, bf16[144,1664]{1,0:T(8,128)(2,1)S(1)}, u32[]{:S(2)}, u32[]{:S(2)}) collective-permute-start(bf16[144,1664]{1,0:T(8,128)(2,1)S(1)} %pad_maximum_fusion.refs_8_.refs_1_), channel_id=1, source_target_pairs={{0,8},{1,9},{2,10},{3,11},{4,12},{5,13},{6,14},{7,15},{8,0},{9,1},... | collective-permute-start | bytes 1437704 | tf_op jit(solution)/shard_map/ppermute | solution.py:934
  41.0 22.2 %collective-permute-start.14 = (bf16[144,1664]{1,0:T(8,128)(2,1)S(1)}, bf16[144,1664]{1,0:T(8,128)(2,1)S(1)}, u32[]{:S(2)}, u32[]{:S(2)}) collective-permute-start(bf16[144,1664]{1,0:T(8,128)(2,1)S(1)} %pad_maximum_fusion.refs_8_.refs_1_), channel_id=1, source_target_pairs={{0,4},{1,5},{2,6},{3,7},{4,0},{5,1},{6,2},{7,3},{8,12},{9,13},{10,... | collective-permute-start | bytes 1437704 | tf_op jit(solution)/shard_map/ppermute | solution.py:934
  42.5 22.1 %collective-permute-start.15 = (bf16[144,1664]{1,0:T(8,128)(2,1)S(1)}, bf16[144,1664]{1,0:T(8,128)(2,1)S(1)}, u32[]{:S(2)}, u32[]{:S(2)}) collective-permute-start(bf16[144,1664]{1,0:T(8,128)(2,1)S(1)} %pad_maximum_fusion.refs_8_.refs_1_), channel_id=1, source_target_pairs={{0,12},{1,13},{2,14},{3,15},{4,8},{5,9},{6,10},{7,11},{8,4},{9,5},... | collective-permute-start | bytes 1437704 | tf_op jit(solution)/shard_map/ppermute | solution.py:934
  64.7 2.1 collective-permute-start.16
  64.7 3.6 %collective-permute-start.17 = (bf16[144,1664]{1,0:T(8,128)(2,1)S(1)}, bf16[144,1664]{1,0:T(8,128)(2,1)S(1)}, u32[]{:S(2)}, u32[]{:S(2)}) collective-permute-start(bf16[144,1664]{1,0:T(8,128)(2,1)S(1)} %collective-permute-done.13.refs_9_.refs_2_), channel_id=1, source_target_pairs={{0,2},{1,3},{2,0},{3,1},{4,6},{5,7},{6,4},{7,5},{8,10},{9,11},{10,... | collective-permute-start | bytes 1437704 | tf_op jit(solution)/shard_map/ppermute | solution.py:934
  65.2 4.2 %collective-permute-start.18 = (bf16[144,1664]{1,0:T(8,128)(2,1)S(1)}, bf16[144,1664]{1,0:T(8,128)(2,1)S(1)}, u32[]{:S(2)}, u32[]{:S(2)}) collective-permute-start(bf16[144,1664]{1,0:T(8,128)(2,1)S(1)} %collective-permute-done.14.refs_10_.refs_3_), channel_id=1, source_target_pairs={{0,2},{1,3},{2,0},{3,1},{4,6},{5,7},{6,4},{7,5},{8,10},{9,11},{10,... | collective-permute-start | bytes 1437704 | tf_op jit(solution)/shard_map/ppermute | solution.py:934
  65.3 5.0 %collective-permute-start.19 = (bf16[144,1664]{1,0:T(8,128)(2,1)S(1)}, bf16[144,1664]{1,0:T(8,128)(2,1)S(1)}, u32[]{:S(2)}, u32[]{:S(2)}) collective-permute-start(bf16[144,1664]{1,0:T(8,128)(2,1)S(1)} %collective-permute-done.15.refs_11_.refs_4_), channel_id=1, source_target_pairs={{0,2},{1,3},{2,0},{3,1},{4,6},{5,7},{6,4},{7,5},{8,10},{9,11},{10,... | collective-permute-start | bytes 1437704 | tf_op jit(solution)/shard_map/ppermute | solution.py:934
  65.8 23.9 %collective-permute-start.21 = (bf16[144,512]{1,0:T(8,128)(2,1)S(1)}, bf16[144,512]{1,0:T(8,128)(2,1)S(1)}, u32[]{:S(2)}, u32[]{:S(2)}) collective-permute-start(bf16[144,512]{1,0:T(8,128)(2,1)S(1)} %pad_maximum_fusion.7.refs_7_), channel_id=1, source_target_pairs={{0,8},{1,9},{2,10},{3,11},{4,12},{5,13},{6,14},{7,15},{8,0},{9,1},... | collective-permute-start | bytes 442376 | tf_op jit(solution)/shard_map/ppermute | solution.py:934
  66.8 22.9 %collective-permute-start.22 = (bf16[144,512]{1,0:T(8,128)(2,1)S(1)}, bf16[144,512]{1,0:T(8,128)(2,1)S(1)}, u32[]{:S(2)}, u32[]{:S(2)}) collective-permute-start(bf16[144,512]{1,0:T(8,128)(2,1)S(1)} %pad_maximum_fusion.7.refs_7_), channel_id=1, source_target_pairs={{0,4},{1,5},{2,6},{3,7},{4,0},{5,1},{6,2},{7,3},{8,12},{9,13},{10,... | collective-permute-start | bytes 442376 | tf_op jit(solution)/shard_map/ppermute | solution.py:934
  68.3 21.4 %collective-permute-start.23 = (bf16[144,512]{1,0:T(8,128)(2,1)S(1)}, bf16[144,512]{1,0:T(8,128)(2,1)}, u32[]{:S(2)}, u32[]{:S(2)}) collective-permute-start(bf16[144,512]{1,0:T(8,128)(2,1)S(1)} %pad_maximum_fusion.7.refs_7_), channel_id=1, source_target_pairs={{0,12},{1,13},{2,14},{3,15},{4,8},{5,9},{6,10},{7,11},{8,4},{9,5},... | collective-permute-start | bytes 442376 | tf_op jit(solution)/shard_map/ppermute | solution.py:934
  69.4 21.4 %collective-permute-start.20 = (bf16[2,192,1024]{2,1,0:T(8,128)(2,1)}, bf16[2,192,1024]{2,1,0:T(8,128)(2,1)}, u32[]{:S(2)}, u32[]{:S(2)}) collective-permute-start(bf16[2,192,1024]{2,1,0:T(8,128)(2,1)} %constant_dynamic-slice_fusion), channel_id=1, source_target_pairs={{0,1},{1,0},{2,3},{3,2},{4,5},{5,4},{6,7},{7,6},{8,9},{9,8},{10,11... | collective-permute-start | bytes 2359304 | tf_op jit(solution)/shard_map/ppermute | solution.py:934
  154.4 8.6 %collective-permute-start.28 = (bf16[2,384,1024]{2,1,0:T(8,128)(2,1)}, bf16[2,384,1024]{2,1,0:T(8,128)(2,1)S(1)}, u32[]{:S(2)}, u32[]{:S(2)}) collective-permute-start(bf16[2,384,1024]{2,1,0:T(8,128)(2,1)} %get-tuple-element.125.refs_0_.refs_5_.refs_6_), channel_id=1, source_target_pairs={{0,2},{1,3},{2,0},{3,1},{4,6},{5,7},{6,4},{7,5},{8,10},{9,11},{10,... | collective-permute-start | bytes 4718600 | tf_op jit(solution)/shard_map/ppermute | solution.py:934
  154.8 8.2 %collective-permute-start.29 = (bf16[192,2048]{1,0:T(8,128)(2,1)}, bf16[192,2048]{1,0:T(8,128)(2,1)S(1)}, u32[]{:S(2)}, u32[]{:S(2)}) collective-permute-start(bf16[192,2048]{1,0:T(8,128)(2,1)} %get-tuple-element.115), channel_id=1, source_target_pairs={{0,2},{1,3},{2,0},{3,1},{4,6},{5,7},{6,4},{7,5},{8,10},{9,11},{10,... | collective-permute-start | bytes 2359304 | tf_op jit(solution)/shard_map/ppermute | solution.py:934
  155.0 8.0 %collective-permute-start.30 = (bf16[256,1152]{1,0:T(8,128)(2,1)}, bf16[256,1152]{1,0:T(8,128)(2,1)S(1)}, u32[]{:S(2)}, u32[]{:S(2)}) collective-permute-start(bf16[256,1152]{1,0:T(8,128)(2,1)} %get-tuple-element.118), channel_id=1, source_target_pairs={{0,2},{1,3},{2,0},{3,1},{4,6},{5,7},{6,4},{7,5},{8,10},{9,11},{10,... | collective-permute-start | bytes 1769480 | tf_op jit(solution)/shard_map/ppermute | solution.py:934
  155.3 27.0 %collective-permute-start.31 = (bf16[2,192,1024]{2,1,0:T(8,128)(2,1)}, bf16[2,192,1024]{2,1,0:T(8,128)(2,1)S(1)}, u32[]{:S(2)}, u32[]{:S(2)}) collective-permute-start(bf16[2,192,1024]{2,1,0:T(8,128)(2,1)} %get-tuple-element.124), channel_id=1, source_target_pairs={{0,1},{1,0},{2,3},{3,2},{4,5},{5,4},{6,7},{7,6},{8,9},{9,8},{10,11... | collective-permute-start | bytes 2359304 | tf_op jit(solution)/shard_map/ppermute | solution.py:934
  167.2 22.3 %collective-permute-start.33 = (bf16[208,1152]{1,0:T(8,128)(2,1)S(1)}, bf16[208,1152]{1,0:T(8,128)(2,1)S(1)}, u32[]{:S(2)}, u32[]{:S(2)}) collective-permute-start(bf16[208,1152]{1,0:T(8,128)(2,1)S(1)} %get-tuple-element.120), channel_id=1, source_target_pairs={{0,8},{1,9},{2,10},{3,11},{4,12},{5,13},{6,14},{7,15},{8,0},{9,1},... | collective-permute-start | bytes 1437704 | tf_op jit(solution)/shard_map/ppermute | solution.py:934
  168.1 22.8 %collective-permute-start.34 = (bf16[208,1152]{1,0:T(8,128)(2,1)S(1)}, bf16[208,1152]{1,0:T(8,128)(2,1)S(1)}, u32[]{:S(2)}, u32[]{:S(2)}) collective-permute-start(bf16[208,1152]{1,0:T(8,128)(2,1)S(1)} %get-tuple-element.121), channel_id=1, source_target_pairs={{0,4},{1,5},{2,6},{3,7},{4,0},{5,1},{6,2},{7,3},{8,12},{9,13},{10,... | collective-permute-start | bytes 1437704 | tf_op jit(solution)/shard_map/ppermute | solution.py:934
  169.7 21.3 %collective-permute-start.35 = (bf16[208,1152]{1,0:T(8,128)(2,1)S(1)}, bf16[208,1152]{1,0:T(8,128)(2,1)S(1)}, u32[]{:S(2)}, u32[]{:S(2)}) collective-permute-start(bf16[208,1152]{1,0:T(8,128)(2,1)S(1)} %get-tuple-element.122), channel_id=1, source_target_pairs={{0,12},{1,13},{2,14},{3,15},{4,8},{5,9},{6,10},{7,11},{8,4},{9,5},... | collective-permute-start | bytes 1437704 | tf_op jit(solution)/shard_map/ppermute | solution.py:934
  189.4 3.6 %collective-permute-start.32 = (bf16[576,1152]{1,0:T(8,128)(2,1)S(1)}, bf16[576,1152]{1,0:T(8,128)(2,1)S(1)}, u32[]{:S(2)}, u32[]{:S(2)}) collective-permute-start(bf16[576,1152]{1,0:T(8,128)(2,1)S(1)} %get-tuple-element.129), channel_id=1, source_target_pairs={{0,2},{1,3},{2,0},{3,1},{4,6},{5,7},{6,4},{7,5},{8,10},{9,11},{10,... | collective-permute-start | bytes 3981320 | tf_op jit(solution)/shard_map/ppermute | solution.py:934
  191.9 12.3 %collective-permute-start.36 = (bf16[208,576]{1,0:T(8,128)(2,1)S(1)}, bf16[208,576]{1,0:T(8,128)(2,1)S(1)}, u32[]{:S(2)}, u32[]{:S(2)}) collective-permute-start(bf16[208,576]{1,0:T(8,128)(2,1)S(1)} %get-tuple-element.136), channel_id=1, source_target_pairs={{0,1},{1,0},{2,3},{3,2},{4,5},{5,4},{6,7},{7,6},{8,9},{9,8},{10,11... | collective-permute-start | bytes 718856 | tf_op jit(solution)/shard_map/ppermute | solution.py:934
  193.9 24.4 %collective-permute-start.39 = (bf16[144,1152]{1,0:T(8,128)(2,1)S(1)}, bf16[144,1152]{1,0:T(8,128)(2,1)S(1)}, u32[]{:S(2)}, u32[]{:S(2)}) collective-permute-start(bf16[144,1152]{1,0:T(8,128)(2,1)S(1)} %get-tuple-element.131), channel_id=1, source_target_pairs={{0,8},{1,9},{2,10},{3,11},{4,12},{5,13},{6,14},{7,15},{8,0},{9,1},... | collective-permute-start | bytes 995336 | tf_op jit(solution)/shard_map/ppermute | solution.py:934
  195.0 23.3 %collective-permute-start.40 = (bf16[144,1152]{1,0:T(8,128)(2,1)S(1)}, bf16[144,1152]{1,0:T(8,128)(2,1)S(1)}, u32[]{:S(2)}, u32[]{:S(2)}) collective-permute-start(bf16[144,1152]{1,0:T(8,128)(2,1)S(1)} %get-tuple-element.132), channel_id=1, source_target_pairs={{0,4},{1,5},{2,6},{3,7},{4,0},{5,1},{6,2},{7,3},{8,12},{9,13},{10,... | collective-permute-start | bytes 995336 | tf_op jit(solution)/shard_map/ppermute | solution.py:934
  196.3 22.1 %collective-permute-start.41 = (bf16[144,1152]{1,0:T(8,128)(2,1)S(1)}, bf16[144,1152]{1,0:T(8,128)(2,1)S(1)}, u32[]{:S(2)}, u32[]{:S(2)}) collective-permute-start(bf16[144,1152]{1,0:T(8,128)(2,1)S(1)} %get-tuple-element.133), channel_id=1, source_target_pairs={{0,12},{1,13},{2,14},{3,15},{4,8},{5,9},{6,10},{7,11},{8,4},{9,5},... | collective-permute-start | bytes 995336 | tf_op jit(solution)/shard_map/ppermute | solution.py:934
  204.8 18.9 %collective-permute-start.45 = (bf16[104,576]{1,0:T(8,128)(2,1)S(1)}, bf16[104,576]{1,0:T(8,128)(2,1)S(1)}, u32[]{:S(2)}, u32[]{:S(2)}) collective-permute-start(bf16[104,576]{1,0:T(8,128)(2,1)S(1)} %get-tuple-element.144), channel_id=1, source_target_pairs={{0,16},{1,17},{2,18},{3,19},{4,20},{5,21},{6,22},{7,23},{8,24},{9,... | collective-permute-start | bytes 359432 | tf_op jit(solution)/shard_map/ppermute | solution.py:934
  208.1 9.7 %collective-permute-start.37 = (bf16[1,192,1024]{2,1,0:T(8,128)(2,1)S(1)}, bf16[1,192,1024]{2,1,0:T(8,128)(2,1)S(1)}, u32[]{:S(2)}, u32[]{:S(2)}) collective-permute-start(bf16[1,192,1024]{2,1,0:T(8,128)(2,1)S(1)} %get-tuple-element.149), channel_id=1, source_target_pairs={{0,1},{1,0},{2,3},{3,2},{4,5},{5,4},{6,7},{7,6},{8,9},{9,8},{10,11... | collective-permute-start | bytes 1179656 | tf_op jit(solution)/shard_map/ppermute | solution.py:934
  217.8 11.6 %collective-permute-start.38 = (bf16[1,192,1024]{2,1,0:T(8,128)(2,1)S(1)}, bf16[1,192,1024]{2,1,0:T(8,128)(2,1)S(1)}, u32[]{:S(2)}, u32[]{:S(2)}) collective-permute-start(bf16[1,192,1024]{2,1,0:T(8,128)(2,1)S(1)} %get-tuple-element.150), channel_id=1, source_target_pairs={{0,1},{1,0},{2,3},{3,2},{4,5},{5,4},{6,7},{7,6},{8,9},{9,8},{10,11... | collective-permute-start | bytes 1179656 | tf_op jit(solution)/shard_map/ppermute | solution.py:934
  218.3 2.9 %collective-permute-start.46 = (f32[16,384]{1,0:T(8,128)S(1)}, f32[16,384]{1,0:T(8,128)S(1)}, u32[]{:S(2)}, u32[]{:S(2)}) collective-permute-start(f32[16,384]{1,0:T(8,128)S(1)} %get-tuple-element.160), channel_id=1, source_target_pairs={{0,2},{1,3},{2,0},{3,1},{4,6},{5,7},{6,4},{7,5},{8,10},{9,11},{10,... | collective-permute-start | bytes 73736 | tf_op jit(solution)/shard_map/ppermute | solution.py:934
  219.3 17.2 %collective-permute-start.42 = (bf16[72,576]{1,0:T(8,128)(2,1)S(1)}, bf16[72,576]{1,0:T(8,128)(2,1)S(1)}, u32[]{:S(2)}, u32[]{:S(2)}) collective-permute-start(bf16[72,576]{1,0:T(8,128)(2,1)S(1)} %get-tuple-element.152), channel_id=1, source_target_pairs={{0,1},{1,0},{2,3},{3,2},{4,5},{5,4},{6,7},{7,6},{8,9},{9,8},{10,11... | collective-permute-start | bytes 248840 | tf_op jit(solution)/shard_map/ppermute | solution.py:934
  220.8 15.8 %collective-permute-start.43 = (bf16[72,576]{1,0:T(8,128)(2,1)S(1)}, bf16[72,576]{1,0:T(8,128)(2,1)S(1)}, u32[]{:S(2)}, u32[]{:S(2)}) collective-permute-start(bf16[72,576]{1,0:T(8,128)(2,1)S(1)} %get-tuple-element.153), channel_id=1, source_target_pairs={{0,16},{1,17},{2,18},{3,19},{4,20},{5,21},{6,22},{7,23},{8,24},{9,... | collective-permute-start | bytes 248840 | tf_op jit(solution)/shard_map/ppermute | solution.py:934
  221.2 15.5 %collective-permute-start.44 = (bf16[72,576]{1,0:T(8,128)(2,1)S(1)}, bf16[72,576]{1,0:T(8,128)(2,1)S(1)}, u32[]{:S(2)}, u32[]{:S(2)}) collective-permute-start(bf16[72,576]{1,0:T(8,128)(2,1)S(1)} %get-tuple-element.154), channel_id=1, source_target_pairs={{0,17},{1,16},{2,19},{3,18},{4,21},{5,20},{6,23},{7,22},{8,25},{9,... | collective-permute-start | bytes 248840 | tf_op jit(solution)/shard_map/ppermute | solution.py:934
  223.7 4.0 %collective-permute-start.47 = (f32[24,384]{1,0:T(8,128)S(1)}, f32[24,384]{1,0:T(8,128)S(1)}, u32[]{:S(2)}, u32[]{:S(2)}) collective-permute-start(f32[24,384]{1,0:T(8,128)S(1)} %pad_maximum_fusion.13), channel_id=1, source_target_pairs={{0,8},{1,9},{2,10},{3,11},{4,12},{5,13},{6,14},{7,15},{8,0},{9,1},... | collective-permute-start | bytes 110600 | tf_op jit(solution)/shard_map/ppermute | solution.py:934
  227.8 4.3 %collective-permute-start.48 = (f32[40,384]{1,0:T(8,128)S(1)}, f32[40,384]{1,0:T(8,128)S(1)}, u32[]{:S(2)}, u32[]{:S(2)}) collective-permute-start(f32[40,384]{1,0:T(8,128)S(1)} %pad_maximum_fusion.10), channel_id=1, source_target_pairs={{0,4},{1,5},{2,6},{3,7},{4,0},{5,1},{6,2},{7,3},{8,12},{9,13},{10,... | collective-permute-start | bytes 184328 | tf_op jit(solution)/shard_map/ppermute | solution.py:934
  232.2 5.8 %collective-permute-start.49 = (f32[72,192]{1,0:T(8,128)S(1)}, f32[72,192]{1,0:T(8,128)S(1)}, u32[]{:S(2)}, u32[]{:S(2)}) collective-permute-start(f32[72,192]{1,0:T(8,128)S(1)} %get-tuple-element.219), channel_id=1, source_target_pairs={{0,1},{1,0},{2,3},{3,2},{4,5},{5,4},{6,7},{7,6},{8,9},{9,8},{10,11... | collective-permute-start | bytes 165896 | tf_op jit(solution)/shard_map/ppermute | solution.py:934
  234.0 7.7 %collective-permute-start.51 = (f32[72,192]{1,0:T(8,128)S(1)}, f32[72,192]{1,0:T(8,128)S(1)}, u32[]{:S(2)}, u32[]{:S(2)}) collective-permute-start(f32[72,192]{1,0:T(8,128)S(1)} %get-tuple-element.219), channel_id=1, source_target_pairs={{0,17},{1,16},{2,19},{3,18},{4,21},{5,20},{6,23},{7,22},{8,25},{9,... | collective-permute-start | bytes 165896 | tf_op jit(solution)/shard_map/ppermute | solution.py:934
  236.4 5.3 %collective-permute-start.50 = (f32[72,192]{1,0:T(8,128)S(1)}, f32[72,192]{1,0:T(8,128)S(1)}, u32[]{:S(2)}, u32[]{:S(2)}) collective-permute-start(f32[72,192]{1,0:T(8,128)S(1)} %get-tuple-element.218), channel_id=1, source_target_pairs={{0,16},{1,17},{2,18},{3,19},{4,20},{5,21},{6,22},{7,23},{8,24},{9,... | collective-permute-start | bytes 165896 | tf_op jit(solution)/shard_map/ppermute | solution.py:934
  (67 other events, 542.7 us)
